TPU v7x, 512 devices: a whole 4x4x16 slice. The times are simulated.
512 devices in a mesh: gx: 8 (over z_lo, core), gy: 16 (over y, x), gz: 4 (over z_hi).
Axes of the slice: x: 4, y: 4, z: 16 (z_hi: 4, z_lo: 4; z = z_hi * 4 + z_lo), core: 2. Of those that a mesh axis runs over, the one named last changes fastest.
Arguments:
- right_side: float32 [64, 512, 512], P('gx', 'gy', 'gz'), may hold values from -8 to 8
- predicted: float32 [64, 512, 512], P('gx', 'gy', 'gz'), may hold values from -4 to 4
- zone: int32 [64, 512, 512], P('gx', 'gy', 'gz'), may hold values from 0 to 15
- zone_table: float32 [16], replicated, may hold values from 0.002 to 0.5
Outputs:
- solution_field: float32 [64, 512, 512], P('gx', 'gy', 'gz')
All inputs are finite; a program needn't handle non-finite values.
Results may differ from a plain program's by a relative error of at most 0.0001.
Values sent between devices are 32-bit elements; how exact they have to be, the bound alone decides.
No kernel may reach another device: no remote copies, remote signals or barrier semaphores. Data moves between devices by JAX's collectives and lax.ppermute only.
A program may use at most 128 MiB of HBM per device.

v0:
```python
import jax
import jax.numpy as jnp
from jax import lax
from jax.sharding import PartitionSpec as P

FINE_LEVELS = 2
SMOOTH_DEG = 4
COARSE_DEG = 8


newmark_shift = 0.0005
smooth_low = 0.5
smooth_high = 2.0
coarse_low = 0.1
coarse_high = 2.0


def padded_2(block, sides, width):
    for axis, dim in sides:
        count = lax.axis_size(axis)
        forward = [(i, i + 1) for i in range(count - 1)]
        backward = [(target, source) for source, target in forward]
        low = lax.ppermute(
            lax.slice_in_dim(block, block.shape[dim] - width, None, axis=dim), axis, forward
        )
        high = lax.ppermute(lax.slice_in_dim(block, 0, width, axis=dim), axis, backward)
        block = jnp.concatenate([low, block, high], axis=dim)
    return block


def lookup(zone, zone_table):
    absorb = jnp.zeros(zone.shape, jnp.float32)
    for code in range(zone_table.shape[0]):
        absorb = absorb + jnp.where(zone == code, zone_table[code], jnp.float32(0.0))
    return absorb


def coarsen(values):
    sx, sy, sz = values.shape
    return values.reshape(sx // 2, 2, sy // 2, 2, sz // 2, 2).sum(axis=(1, 3, 5)) * 0.5


def refine(values):
    return jnp.repeat(jnp.repeat(jnp.repeat(values, 2, axis=0), 2, axis=1), 2, axis=2)


def fine_padder(field):
    return padded_2(field, (("gx", 0), ("gy", 1), ("gz", 2)), 1)


def spread_padder(field):
    return padded_2(field, (("gx", 0), ("gy", 1), ("gz", 2)), 1)


def operate(field, diagonal, padder):
    padded = padder(field)
    beside = padded[2:, 1:-1, 1:-1] + padded[:-2, 1:-1, 1:-1]
    beside = beside + padded[1:-1, 2:, 1:-1] + padded[1:-1, :-2, 1:-1]
    beside = beside + padded[1:-1, 1:-1, 2:] + padded[1:-1, 1:-1, :-2]
    return diagonal * field - beside


def chebyshev(field, source, diagonal, padder, degree, low, high, start_zero):
    centre_value = (high + low) / 2.0
    half_width = (high - low) / 2.0
    ratio_value = centre_value / half_width
    factor = 1.0 / ratio_value
    if start_zero:
        scaled = source / diagonal
    else:
        scaled = (source - operate(field, diagonal, padder)) / diagonal
    update = scaled / centre_value
    field = field + update
    for sweep in range(1, degree):
        scaled = (source - operate(field, diagonal, padder)) / diagonal
        factor_next = 1.0 / (2.0 * ratio_value - factor)
        update = factor_next * factor * update + 2.0 * factor_next / half_width * scaled
        field = field + update
        factor = factor_next
    return field


def per_device(right_side, predicted, zone, zone_table):
    masses = [newmark_shift + lookup(zone, zone_table)]
    for depth in range(FINE_LEVELS):
        masses.append(coarsen(masses[-1]))
    smoothed = []
    sources = []
    source = right_side
    field = predicted
    for depth in range(FINE_LEVELS):
        diagonal = 6.0 + masses[depth]
        field = chebyshev(
            field, source, diagonal, fine_padder, SMOOTH_DEG, smooth_low, smooth_high, depth > 0
        )
        residual = source - operate(field, diagonal, fine_padder)
        smoothed.append(field)
        sources.append(source)
        source = coarsen(residual)
        field = jnp.zeros_like(source)
    coarse_mass = masses[FINE_LEVELS]
    correction = chebyshev(
        jnp.zeros_like(source),
        source,
        6.0 + coarse_mass,
        spread_padder,
        COARSE_DEG,
        coarse_low,
        coarse_high,
        True,
    )
    for depth in reversed(range(FINE_LEVELS)):
        field = smoothed[depth] + refine(correction)
        correction = chebyshev(
            field,
            sources[depth],
            6.0 + masses[depth],
            fine_padder,
            SMOOTH_DEG,
            smooth_low,
            smooth_high,
            False,
        )
    return correction


def solution(mesh):
    placed = (P("gx", "gy", "gz"), P("gx", "gy", "gz"), P("gx", "gy", "gz"), P())
    return jax.shard_map(
        per_device, mesh=mesh, in_specs=placed, out_specs=P("gx", "gy", "gz"), check_vma=False
    )
```

profile of v0, /device:TPU:439, one launch (start us, length us, event | category | flops | bytes accessed | tf_op | source)
XLA Modules:
  0.0 1026.1 jit_solution(2044894296161334188)
XLA Ops:
  45.0 12.9 %multiply_add_fusion.5 = (f32[8,32,128]{1,0,2:T(8,128)S(1)}, f32[8,32,128]{1,0,2:T(8,128)}) fusion(f32[8,32,128]{1,0,2:T(8,128)S(1)} %copy.299, f32[8,32,128]{1,0,2:T(8,128)S(1)} %copy.298, f32[8,32,128]{1,0,2:T(8,128)} %copy.376, f32[8,32,128]{1,0,2:T(8,128)} %copy.375, f32[8,32,128]{1,0,2:T(8,128)} %copy.374, f32[8,32,128]{1,0,2:T(8,128)} %copy.373, ...), kind=kLoop, calls=%fused_computation.87 | loop fusion | flops 1933312 | bytes 1441856 | tf_op jit(solution)/shard_map/add | solution.py:73
  88.5 11.9 %collective-permute-done.10 = f32[10,34,1]{2,1,0:T(8,128)S(1)} collective-permute-done((f32[10,34,1]{2,1,0:T(8,128)S(1)}, f32[10,34,1]{2,1,0:T(8,128)S(1)}, u32[]{:S(2)}, u32[]{:S(2)}) %collective-permute-start.10) | collective-permute-done | bytes 1392 | tf_op jit(solution)/shard_map/ppermute | solution.py:26
  106.4 13.0 %fusion.238 = (f32[8,32,128]{1,0,2:T(8,128)S(1)}, f32[8,32,128]{1,0,2:T(8,128)}) fusion(f32[8,32,128]{1,0,2:T(8,128)S(1)} %get-tuple-element.37, f32[8,32,128]{1,0,2:T(8,128)S(1)} %copy.298, f32[8,32,128]{1,0,2:T(8,128)} %copy.380, f32[8,32,128]{1,0,2:T(8,128)} %copy.379, f32[8,32,128]{1,0,2:T(8,128)S(1)} %copy.378, f32[8,32,128]{1,0,2:T(8,128)S(1)} %copy.377, ...), kind=kLoop, calls=%fused_computation.763 | loop fusion | flops 2064384 | bytes 1343552 | tf_op jit(solution)/shard_map/add | solution.py:78
  149.0 10.2 collective-permute-done.16
  159.2 10.9 %collective-permute-done.17 = f32[10,34,1]{2,1,0:T(8,128)S(1)} collective-permute-done((f32[10,34,1]{2,1,0:T(8,128)S(1)}, f32[10,34,1]{2,1,0:T(8,128)S(1)}, u32[]{:S(2)}, u32[]{:S(2)}) %collective-permute-start.17) | collective-permute-done | bytes 1392 | tf_op jit(solution)/shard_map/ppermute | solution.py:23
  172.5 13.0 %fusion.237 = (f32[8,32,128]{1,0,2:T(8,128)S(1)}, f32[8,32,128]{1,0,2:T(8,128)}) fusion(f32[8,32,128]{1,0,2:T(8,128)S(1)} %get-tuple-element.35, f32[8,32,128]{1,0,2:T(8,128)S(1)} %copy.298, f32[8,32,128]{1,0,2:T(8,128)} %copy.384, f32[8,32,128]{1,0,2:T(8,128)} %copy.383, f32[8,32,128]{1,0,2:T(8,128)S(1)} %copy.382, f32[8,32,128]{1,0,2:T(8,128)S(1)} %copy.381, ...), kind=kLoop, calls=%fused_computation.762 | loop fusion | flops 2064384 | bytes 1343552 | tf_op jit(solution)/shard_map/add | solution.py:78
  217.5 11.7 %collective-permute-done.23 = f32[10,34,1]{2,1,0:T(8,128)} collective-permute-done((f32[10,34,1]{2,1,0:T(8,128)S(1)}, f32[10,34,1]{2,1,0:T(8,128)}, u32[]{:S(2)}, u32[]{:S(2)}) %collective-permute-start.23) | collective-permute-done | bytes 1392 | tf_op jit(solution)/shard_map/ppermute | solution.py:23
  232.6 12.2 %add_add_fusion.1 = f32[8,32,128]{1,0,2:T(8,128)S(1)} fusion(f32[8,32,128]{1,0,2:T(8,128)S(1)} %get-tuple-element.33, f32[8,32,128]{1,0,2:T(8,128)S(1)} %copy.298, f32[8,32,128]{1,0,2:T(8,128)} %copy.388, f32[8,32,128]{1,0,2:T(8,128)} %copy.387, f32[8,32,128]{1,0,2:T(8,128)S(1)} %copy.386, f32[8,32,128]{1,0,2:T(8,128)S(1)} %copy.385, ...), kind=kLoop, calls=%fused_computation.84 | loop fusion | flops 2064384 | bytes 1212480 | tf_op jit(solution)/shard_map/add | solution.py:78
  257.8 10.4 %broadcast_add_fusion = f32[8,32,128]{1,0,2:T(8,128)S(1)} fusion(f32[]{:T(128)} %bitcast.15, s32[8,32,128]{1,0,2:T(8,128)S(1)} %copy.275, f32[]{:T(128)} %bitcast.14, f32[]{:T(128)} %bitcast.13, f32[]{:T(128)} %bitcast.12, f32[]{:T(128)} %bitcast.11, f32[]{:T(128)} %bitcast.10, f32[]{:T(128)} %bitcast.9, f32[]{:T(128)} %bitcast.8, f32[]{:T(128)} %bitcast.7, ...), kind=kLoop, calls=%fused_computation.90 | loop fusion | flops 1572864 | bytes 262208 | tf_op jit(solution)/shard_map/add | solution.py:84
  268.3 9.7 reshape.32
  286.1 9.4 collective-permute-done.28
  304.6 12.6 %fusion.38 = f32[8,32,128]{1,0,2:T(8,128)} fusion(f32[8,32,128]{1,0,2:T(8,128)S(1)} %copy.298, f32[8,32,128]{1,0,2:T(8,128)} %copy.392, f32[8,32,128]{1,0,2:T(8,128)S(1)} %copy.391, f32[8,32,128]{1,0,2:T(8,128)S(1)} %copy.390, f32[8,32,128]{1,0,2:T(8,128)S(1)} %copy.389, f32[8,32,128]{1,0,2:T(8,128)S(1)} %add_add_fusion.1, ...), kind=kLoop, calls=%fused_computation.47 | loop fusion | flops 1900544 | bytes 1081408 | tf_op jit(solution)/shard_map/sub | solution.py:96
  318.4 9.7 reshape.31
  335.0 10.3 %collective-permute-start.31 = (f32[1,16,64]{2,1,0:T(8,128)S(1)}, f32[1,16,64]{2,1,0:T(8,128)S(1)}, u32[]{:S(2)}, u32[]{:S(2)}) collective-permute-start(f32[1,16,64]{2,1,0:T(8,128)S(1)} %get-tuple-element.186), channel_id=1, source_target_pairs={{0,64},{64,128},{128,192},{192,256},{256,320},{320,384},{384,448},... | collective-permute-start | bytes 12296 | tf_op jit(solution)/shard_map/ppermute | solution.py:23
  680.2 10.1 collective-permute-done.101
  810.2 9.5 collective-permute-done.124
  827.2 12.8 %multiply_add_fusion.2 = (f32[8,32,128]{1,0,2:T(8,128)S(1)}, f32[8,32,128]{1,0,2:T(8,128)}) fusion(f32[8,32,128]{1,0,2:T(8,128)S(1)} %bitcast_add_fusion, f32[8,32,128]{1,0,2:T(8,128)S(1)} %copy.298, f32[8,32,128]{1,0,2:T(8,128)} %copy.396, f32[8,32,128]{1,0,2:T(8,128)} %copy.395, f32[8,32,128]{1,0,2:T(8,128)S(1)} %copy.394, f32[8,32,128]{1,0,2:T(8,128)S(1)} %copy.393, ...), kind=kLoop, calls=%fused_computation.83 | loop fusion | flops 1998848 | bytes 1212480 | tf_op jit(solution)/shard_map/add | solution.py:73
  867.6 11.7 %collective-permute-done.130 = f32[10,34,1]{2,1,0:T(8,128)S(1)} collective-permute-done((f32[10,34,1]{2,1,0:T(8,128)S(1)}, f32[10,34,1]{2,1,0:T(8,128)S(1)}, u32[]{:S(2)}, u32[]{:S(2)}) %collective-permute-start.130) | collective-permute-done | bytes 1392 | tf_op jit(solution)/shard_map/ppermute | solution.py:26
  884.4 13.0 %fusion.214 = (f32[8,32,128]{1,0,2:T(8,128)S(1)}, f32[8,32,128]{1,0,2:T(8,128)}) fusion(f32[8,32,128]{1,0,2:T(8,128)S(1)} %get-tuple-element.9, f32[8,32,128]{1,0,2:T(8,128)S(1)} %copy.298, f32[8,32,128]{1,0,2:T(8,128)} %copy.400, f32[8,32,128]{1,0,2:T(8,128)} %copy.399, f32[8,32,128]{1,0,2:T(8,128)S(1)} %copy.398, f32[8,32,128]{1,0,2:T(8,128)S(1)} %copy.397, ...), kind=kLoop, calls=%fused_computation.751 | loop fusion | flops 2064384 | bytes 1343552 | tf_op jit(solution)/shard_map/add | solution.py:78
  926.9 9.7 collective-permute-done.136
  936.6 12.1 %collective-permute-done.137 = f32[10,34,1]{2,1,0:T(8,128)} collective-permute-done((f32[10,34,1]{2,1,0:T(8,128)S(1)}, f32[10,34,1]{2,1,0:T(8,128)}, u32[]{:S(2)}, u32[]{:S(2)}) %collective-permute-start.137) | collective-permute-done | bytes 1392 | tf_op jit(solution)/shard_map/ppermute | solution.py:23
  952.0 13.0 %fusion.213 = (f32[8,32,128]{1,0,2:T(8,128)S(1)}, f32[8,32,128]{1,0,2:T(8,128)}) fusion(f32[8,32,128]{1,0,2:T(8,128)S(1)} %get-tuple-element.7, f32[8,32,128]{1,0,2:T(8,128)S(1)} %copy.298, f32[8,32,128]{1,0,2:T(8,128)} %copy.404, f32[8,32,128]{1,0,2:T(8,128)} %copy.403, f32[8,32,128]{1,0,2:T(8,128)S(1)} %copy.402, f32[8,32,128]{1,0,2:T(8,128)S(1)} %copy.401, ...), kind=kLoop, calls=%fused_computation.750 | loop fusion | flops 2064384 | bytes 1343552 | tf_op jit(solution)/shard_map/add | solution.py:78
  996.7 11.8 %collective-permute-done.143 = f32[10,34,1]{2,1,0:T(8,128)} collective-permute-done((f32[10,34,1]{2,1,0:T(8,128)S(1)}, f32[10,34,1]{2,1,0:T(8,128)}, u32[]{:S(2)}, u32[]{:S(2)}) %collective-permute-start.143) | collective-permute-done | bytes 1392 | tf_op jit(solution)/shard_map/ppermute | solution.py:23
  1011.1 12.9 %add_add_fusion = f32[8,32,128]{1,0,2:T(8,128)} fusion(f32[8,32,128]{1,0,2:T(8,128)S(1)} %get-tuple-element.5, f32[8,32,128]{1,0,2:T(8,128)S(1)} %copy.298, f32[8,32,128]{1,0,2:T(8,128)} %copy.408, f32[8,32,128]{1,0,2:T(8,128)S(1)} %copy.407, f32[8,32,128]{1,0,2:T(8,128)S(1)} %copy.406, f32[8,32,128]{1,0,2:T(8,128)S(1)} %copy.405, f32[1,32,128]{1,0,2:T(1,128)} %copy-done, ...), kind=kLoop, calls=%fused_computation.80 | loop fusion | flops 2064384 | bytes 1212480 | tf_op jit(solution)/shard_map/add | solution.py:78
  (501 shorter events, 749.0 us)
Async XLA Ops:
  18.4 16.6 %collective-permute-start.4 = (f32[10,34,1]{2,1,0:T(8,128)S(1)}, f32[10,34,1]{2,1,0:T(8,128)}, u32[]{:S(2)}, u32[]{:S(2)}) collective-permute-start(f32[10,34,1]{2,1,0:T(8,128)S(1)} %get-tuple-element.71), channel_id=1, source_target_pairs={{1,0},{2,1},{3,2},{5,4},{6,5},{7,6},{9,8},{10,9},{11,10},{13,12},{... | collective-permute-start | bytes 4088 | tf_op jit(solution)/shard_map/ppermute | solution.py:26
  24.3 15.5 %collective-permute-start.5 = (f32[10,34,1]{2,1,0:T(8,128)S(1)}, f32[10,34,1]{2,1,0:T(8,128)}, u32[]{:S(2)}, u32[]{:S(2)}) collective-permute-start(f32[10,34,1]{2,1,0:T(8,128)S(1)} %get-tuple-element.72), channel_id=1, source_target_pairs={{0,1},{1,2},{2,3},{4,5},{5,6},{6,7},{8,9},{9,10},{10,11},{12,13},{... | collective-permute-start | bytes 4088 | tf_op jit(solution)/shard_map/ppermute | solution.py:23
  84.0 16.3 %collective-permute-start.10 = (f32[10,34,1]{2,1,0:T(8,128)S(1)}, f32[10,34,1]{2,1,0:T(8,128)S(1)}, u32[]{:S(2)}, u32[]{:S(2)}) collective-permute-start(f32[10,34,1]{2,1,0:T(8,128)S(1)} %get-tuple-element.69), channel_id=1, source_target_pairs={{1,0},{2,1},{3,2},{5,4},{6,5},{7,6},{9,8},{10,9},{11,10},{13,12},{... | collective-permute-start | bytes 4088 | tf_op jit(solution)/shard_map/ppermute | solution.py:26
  86.9 16.1 %collective-permute-start.11 = (f32[10,34,1]{2,1,0:T(8,128)S(1)}, f32[10,34,1]{2,1,0:T(8,128)}, u32[]{:S(2)}, u32[]{:S(2)}) collective-permute-start(f32[10,34,1]{2,1,0:T(8,128)S(1)} %get-tuple-element.70), channel_id=1, source_target_pairs={{0,1},{1,2},{2,3},{4,5},{5,6},{6,7},{8,9},{9,10},{10,11},{12,13},{... | collective-permute-start | bytes 4088 | tf_op jit(solution)/shard_map/ppermute | solution.py:23
  119.4 11.2 %collective-permute-start.13 = (f32[1,32,128]{1,0,2:T(1,128)S(1)}, f32[1,32,128]{1,0,2:T(1,128)S(1)}, u32[]{:S(2)}, u32[]{:S(2)}) collective-permute-start(f32[1,32,128]{1,0,2:T(1,128)S(1)} %get-tuple-element.51), channel_id=1, source_target_pairs={{0,64},{64,128},{128,192},{192,256},{256,320},{320,384},{384,448},... | collective-permute-start | bytes 49160 | tf_op jit(solution)/shard_map/ppermute | solution.py:23
  142.8 16.4 %collective-permute-start.16 = (f32[10,34,1]{2,1,0:T(8,128)S(1)}, f32[10,34,1]{2,1,0:T(8,128)S(1)}, u32[]{:S(2)}, u32[]{:S(2)}) collective-permute-start(f32[10,34,1]{2,1,0:T(8,128)S(1)} %get-tuple-element.67), channel_id=1, source_target_pairs={{1,0},{2,1},{3,2},{5,4},{6,5},{7,6},{9,8},{10,9},{11,10},{13,12},{... | collective-permute-start | bytes 4088 | tf_op jit(solution)/shard_map/ppermute | solution.py:26
  147.5 22.6 %collective-permute-start.17 = (f32[10,34,1]{2,1,0:T(8,128)S(1)}, f32[10,34,1]{2,1,0:T(8,128)S(1)}, u32[]{:S(2)}, u32[]{:S(2)}) collective-permute-start(f32[10,34,1]{2,1,0:T(8,128)S(1)} %get-tuple-element.68), channel_id=1, source_target_pairs={{0,1},{1,2},{2,3},{4,5},{5,6},{6,7},{8,9},{9,10},{10,11},{12,13},{... | collective-permute-start | bytes 4088 | tf_op jit(solution)/shard_map/ppermute | solution.py:23
  203.3 14.2 %collective-permute-start.22 = (f32[10,34,1]{2,1,0:T(8,128)S(1)}, f32[10,34,1]{2,1,0:T(8,128)S(1)}, u32[]{:S(2)}, u32[]{:S(2)}) collective-permute-start(f32[10,34,1]{2,1,0:T(8,128)S(1)} %get-tuple-element.65), channel_id=1, source_target_pairs={{1,0},{2,1},{3,2},{5,4},{6,5},{7,6},{9,8},{10,9},{11,10},{13,12},{... | collective-permute-start | bytes 4088 | tf_op jit(solution)/shard_map/ppermute | solution.py:26
  206.6 22.6 %collective-permute-start.23 = (f32[10,34,1]{2,1,0:T(8,128)S(1)}, f32[10,34,1]{2,1,0:T(8,128)}, u32[]{:S(2)}, u32[]{:S(2)}) collective-permute-start(f32[10,34,1]{2,1,0:T(8,128)S(1)} %get-tuple-element.66), channel_id=1, source_target_pairs={{0,1},{1,2},{2,3},{4,5},{5,6},{6,7},{8,9},{9,10},{10,11},{12,13},{... | collective-permute-start | bytes 4088 | tf_op jit(solution)/shard_map/ppermute | solution.py:23
  252.4 29.6 %collective-permute-start.27 = (f32[10,1,128]{2,1,0:T(1,128)S(1)}, f32[10,1,128]{2,1,0:T(1,128)S(1)}, u32[]{:S(2)}, u32[]{:S(2)}) collective-permute-start(f32[10,1,128]{2,1,0:T(1,128)S(1)} %get-tuple-element.109), channel_id=1, source_target_pairs={{0,4},{4,8},{8,12},{12,16},{16,20},{20,24},{24,28},{28,32},{32,36}... | collective-permute-start | bytes 15368 | tf_op jit(solution)/shard_map/ppermute | solution.py:23
  254.4 27.7 %collective-permute-start.26 = (f32[10,1,128]{2,1,0:T(1,128)S(1)}, f32[10,1,128]{2,1,0:T(1,128)S(1)}, u32[]{:S(2)}, u32[]{:S(2)}) collective-permute-start(f32[10,1,128]{2,1,0:T(1,128)S(1)} %get-tuple-element.110), channel_id=1, source_target_pairs={{4,0},{8,4},{12,8},{16,12},{20,16},{24,20},{28,24},{32,28},{36,32}... | collective-permute-start | bytes 15368 | tf_op jit(solution)/shard_map/ppermute | solution.py:26
  282.2 13.3 %collective-permute-start.28 = (f32[10,34,1]{2,1,0:T(8,128)S(1)}, f32[10,34,1]{2,1,0:T(8,128)S(1)}, u32[]{:S(2)}, u32[]{:S(2)}) collective-permute-start(f32[10,34,1]{2,1,0:T(8,128)S(1)} %get-tuple-element.63), channel_id=1, source_target_pairs={{1,0},{2,1},{3,2},{5,4},{6,5},{7,6},{9,8},{10,9},{11,10},{13,12},{... | collective-permute-start | bytes 4088 | tf_op jit(solution)/shard_map/ppermute | solution.py:26
  284.6 15.9 %collective-permute-start.29 = (f32[10,34,1]{2,1,0:T(8,128)S(1)}, f32[10,34,1]{2,1,0:T(8,128)}, u32[]{:S(2)}, u32[]{:S(2)}) collective-permute-start(f32[10,34,1]{2,1,0:T(8,128)S(1)} %get-tuple-element.64), channel_id=1, source_target_pairs={{0,1},{1,2},{2,3},{4,5},{5,6},{6,7},{8,9},{9,10},{10,11},{12,13},{... | collective-permute-start | bytes 4088 | tf_op jit(solution)/shard_map/ppermute | solution.py:23
  332.1 13.2 %collective-permute-start.30 = (f32[1,16,64]{2,1,0:T(8,128)S(1)}, f32[1,16,64]{2,1,0:T(8,128)S(1)}, u32[]{:S(2)}, u32[]{:S(2)}) collective-permute-start(f32[1,16,64]{2,1,0:T(8,128)S(1)} %get-tuple-element.187), channel_id=1, source_target_pairs={{64,0},{128,64},{192,128},{256,192},{320,256},{384,320},{448,384},... | collective-permute-start | bytes 12296 | tf_op jit(solution)/shard_map/ppermute | solution.py:26
  335.0 11.1 %collective-permute-start.31 = (f32[1,16,64]{2,1,0:T(8,128)S(1)}, f32[1,16,64]{2,1,0:T(8,128)S(1)}, u32[]{:S(2)}, u32[]{:S(2)}) collective-permute-start(f32[1,16,64]{2,1,0:T(8,128)S(1)} %get-tuple-element.186), channel_id=1, source_target_pairs={{0,64},{64,128},{128,192},{192,256},{256,320},{320,384},{384,448},... | collective-permute-start | bytes 12296 | tf_op jit(solution)/shard_map/ppermute | solution.py:23
  678.8 11.5 %collective-permute-start.101 = (f32[6,18,1]{2,1,0:T(8,128)S(1)}, f32[6,18,1]{2,1,0:T(8,128)S(1)}, u32[]{:S(2)}, u32[]{:S(2)}) collective-permute-start(f32[6,18,1]{2,1,0:T(8,128)S(1)} %get-tuple-element.131), channel_id=1, source_target_pairs={{0,1},{1,2},{2,3},{4,5},{5,6},{6,7},{8,9},{9,10},{10,11},{12,13},{... | collective-permute-start | bytes 1304 | tf_op jit(solution)/shard_map/ppermute | solution.py:23
  807.3 12.4 %collective-permute-start.124 = (f32[10,34,1]{2,1,0:T(8,128)S(1)}, f32[10,34,1]{2,1,0:T(8,128)S(1)}, u32[]{:S(2)}, u32[]{:S(2)}) collective-permute-start(f32[10,34,1]{2,1,0:T(8,128)S(1)} %get-tuple-element.61), channel_id=1, source_target_pairs={{1,0},{2,1},{3,2},{5,4},{6,5},{7,6},{9,8},{10,9},{11,10},{13,12},{... | collective-permute-start | bytes 4088 | tf_op jit(solution)/shard_map/ppermute | solution.py:26
  808.6 15.2 %collective-permute-start.125 = (f32[10,34,1]{2,1,0:T(8,128)S(1)}, f32[10,34,1]{2,1,0:T(8,128)}, u32[]{:S(2)}, u32[]{:S(2)}) collective-permute-start(f32[10,34,1]{2,1,0:T(8,128)S(1)} %get-tuple-element.62), channel_id=1, source_target_pairs={{0,1},{1,2},{2,3},{4,5},{5,6},{6,7},{8,9},{9,10},{10,11},{12,13},{... | collective-permute-start | bytes 4088 | tf_op jit(solution)/shard_map/ppermute | solution.py:23
  862.9 16.4 %collective-permute-start.130 = (f32[10,34,1]{2,1,0:T(8,128)S(1)}, f32[10,34,1]{2,1,0:T(8,128)S(1)}, u32[]{:S(2)}, u32[]{:S(2)}) collective-permute-start(f32[10,34,1]{2,1,0:T(8,128)S(1)} %get-tuple-element.59), channel_id=1, source_target_pairs={{1,0},{2,1},{3,2},{5,4},{6,5},{7,6},{9,8},{10,9},{11,10},{13,12},{... | collective-permute-start | bytes 4088 | tf_op jit(solution)/shard_map/ppermute | solution.py:26
  865.8 16.1 %collective-permute-start.131 = (f32[10,34,1]{2,1,0:T(8,128)S(1)}, f32[10,34,1]{2,1,0:T(8,128)S(1)}, u32[]{:S(2)}, u32[]{:S(2)}) collective-permute-start(f32[10,34,1]{2,1,0:T(8,128)S(1)} %get-tuple-element.60), channel_id=1, source_target_pairs={{0,1},{1,2},{2,3},{4,5},{5,6},{6,7},{8,9},{9,10},{10,11},{12,13},{... | collective-permute-start | bytes 4088 | tf_op jit(solution)/shard_map/ppermute | solution.py:23
  920.5 16.1 %collective-permute-start.136 = (f32[10,34,1]{2,1,0:T(8,128)S(1)}, f32[10,34,1]{2,1,0:T(8,128)S(1)}, u32[]{:S(2)}, u32[]{:S(2)}) collective-permute-start(f32[10,34,1]{2,1,0:T(8,128)S(1)} %get-tuple-element.57), channel_id=1, source_target_pairs={{1,0},{2,1},{3,2},{5,4},{6,5},{7,6},{9,8},{10,9},{11,10},{13,12},{... | collective-permute-start | bytes 4088 | tf_op jit(solution)/shard_map/ppermute | solution.py:26
  925.3 23.3 %collective-permute-start.137 = (f32[10,34,1]{2,1,0:T(8,128)S(1)}, f32[10,34,1]{2,1,0:T(8,128)}, u32[]{:S(2)}, u32[]{:S(2)}) collective-permute-start(f32[10,34,1]{2,1,0:T(8,128)S(1)} %get-tuple-element.58), channel_id=1, source_target_pairs={{0,1},{1,2},{2,3},{4,5},{5,6},{6,7},{8,9},{9,10},{10,11},{12,13},{... | collective-permute-start | bytes 4088 | tf_op jit(solution)/shard_map/ppermute | solution.py:23
  982.8 13.9 %collective-permute-start.142 = (f32[10,34,1]{2,1,0:T(8,128)S(1)}, f32[10,34,1]{2,1,0:T(8,128)S(1)}, u32[]{:S(2)}, u32[]{:S(2)}) collective-permute-start(f32[10,34,1]{2,1,0:T(8,128)S(1)} %get-tuple-element.55), channel_id=1, source_target_pairs={{1,0},{2,1},{3,2},{5,4},{6,5},{7,6},{9,8},{10,9},{11,10},{13,12},{... | collective-permute-start | bytes 4088 | tf_op jit(solution)/shard_map/ppermute | solution.py:26
  985.8 22.7 %collective-permute-start.143 = (f32[10,34,1]{2,1,0:T(8,128)S(1)}, f32[10,34,1]{2,1,0:T(8,128)}, u32[]{:S(2)}, u32[]{:S(2)}) collective-permute-start(f32[10,34,1]{2,1,0:T(8,128)S(1)} %get-tuple-element.56), channel_id=1, source_target_pairs={{0,1},{1,2},{2,3},{4,5},{5,6},{6,7},{8,9},{9,10},{10,11},{12,13},{... | collective-permute-start | bytes 4088 | tf_op jit(solution)/shard_map/ppermute | solution.py:23
  (123 other events, 807.1 us)
where the time goes:
time: 1040 us; the launch traced here: 1030 us
  starting transfers between devices  467 us (45%)
  waiting for transfers between devices  349 us (34%)
  other arithmetic  147 us (14%)
  local copies, waits for them, and re-layouts  60.5 us (6%)
    ppermute x72, starting transfers between devices, padded_2(): lax.ppermute(lax.slice_in_dim(block, block.shape[dim] - width, None, axis...  243 us
    ppermute x72, starting transfers between devices, padded_2(): lax.ppermute(lax.slice_in_dim(block, 0, width, axis=dim), axis, backward)  225 us
    ppermute x72, waiting for transfers between devices, padded_2(): lax.ppermute(lax.slice_in_dim(block, block.shape[dim] - width, None, axis...  205 us
    ppermute x72, waiting for transfers between devices, padded_2(): lax.ppermute(lax.slice_in_dim(block, 0, width, axis=dim), axis, backward)  144 us
    add x22, other arithmetic, chebyshev(): field = field + update  104 us
    unnamed x48, local copies, waits for them, and re-layouts  27.1 us
  transfers between devices with their start and end apart: 144, of which 87 were waited for; matrix products, arithmetic and copies ran while one was open for 3% of the time, Pallas kernels for 0%

commit v1 on v0

v1 whole, which is shorter than its diff:
```python
import jax
import jax.numpy as jnp
from jax import lax
from jax.experimental import pallas as pl
from jax.experimental.pallas import tpu as pltpu
from jax.sharding import PartitionSpec as P

SMOOTH_DEG = 4
COARSE_DEG = 8
SHIFT = 0.0005
SMOOTH = (0.5, 2.0)
COARSE = (0.1, 2.0)
F32 = jnp.float32
HIGHEST = lax.Precision.HIGHEST


def factors(degree, low, high):
    centre, half = (high + low) / 2.0, (high - low) / 2.0
    ratio = centre / half
    factor = 1.0 / ratio
    pairs = [(0.0, 1.0 / centre)]
    for _ in range(1, degree):
        following = 1.0 / (2.0 * ratio - factor)
        pairs.append((following * factor, 2.0 * following / half))
        factor = following
    return pairs


def lanes_like(shape):
    return lax.broadcasted_iota(jnp.int32, shape, len(shape) - 1)


def rows_like(shape):
    return lax.broadcasted_iota(jnp.int32, shape, len(shape) - 2)


def turn(v, by, axis):
    by = by % v.shape[axis]
    return v if by == 0 else pltpu.roll(v, by, axis)


def across(own, lane):
    up = [turn(v, 1, 1) for v in own]
    down = [turn(v, -1, 1) for v in own]
    if len(own) == 2:
        up = [jnp.where(lane == 0, up[1 - h], up[h]) for h in range(2)]
        down = [jnp.where(lane == 127, down[1 - h], down[h]) for h in range(2)]
    return [p + q for p, q in zip(up, down)]


def put(x, i, h, row, value, height, cyclic):
    x[i, h, pl.ds(8 + row, 8)] = value
    if cyclic and row == 0:
        x[i, h, pl.ds(8 + height, 1)] = value[0:1]
    if cyclic and row == height - 8:
        x[i, h, pl.ds(7, 1)] = value[7:8]


def stencil(x, first, group, halves, rows, use):
    lane = lanes_like((8, 128))
    for row in rows:
        def load(i):
            return [x[i, h, pl.ds(8 + row, 8)] for h in range(halves)]

        below, own = load(first - 1), load(first)
        for j in range(group):
            i = first + j
            above = load(i + 1)
            side = across(own, lane)
            total = [
                (below[h] + above[h]) + (x[i, h, pl.ds(7 + row, 8)] + x[i, h, pl.ds(9 + row, 8)]) + side[h]
                for h in range(halves)
            ]
            use(j, row, own, total)
            below, own = own, above


def sweep(xin, xout, upd, src, inv, start, stop, a, c, group, cyclic, offset=0):
    halves, height = src.shape[1], src.shape[2]

    def body(first):
        def use(j, row, own, total):
            i, tile = first + j, pl.ds(row, 8)
            for h in range(halves):
                g = (src[i + offset, h, tile] + total[h]) * inv[i + offset, h, tile] - own[h]
                u = c * g if a == 0.0 else a * upd[i, h, tile] + c * g
                upd[i, h, tile] = u
                put(xout, i, h, row, own[h] + u, height, cyclic)

        stencil(xin, first, group, halves, range(0, height, 8), use)

    steps = (stop - start) // group
    if steps == 1:
        body(start)
    else:
        def step(n, carry):
            body(start + n * group)
            return carry

        lax.fori_loop(0, steps, step, 0)


def dot(a, b):
    return lax.dot_general(a, b, (((1,), (0,)), ((), ())), precision=HIGHEST, preferred_element_type=F32)


def inverse(mass):
    return jnp.where(mass > 0.0, 1.0 / (6.0 + mass), 0.0)


def first_kernel(table, pred, right, zone, main, to_next, to_before, codes, sems):
    moves = ((zone, codes), (pred, main.at[0]), (right, main.at[1]))
    copies = [pltpu.make_async_copy(*move, sems.at[n]) for n, move in enumerate(moves)]
    for copy in copies:
        copy.start()
    copies[0].wait()
    lane = lanes_like((32, 128))
    for x in range(8):
        code = codes[x]
        absorb = jnp.zeros((32, 128), F32)
        for k in range(16):
            absorb = absorb + jnp.where(code == k, table[k], 0.0)
        main[2, x] = SHIFT + absorb
    copies[1].wait()
    copies[2].wait()
    for edge, out in ((120, to_next), (0, to_before)):
        for half, fields in ((0, (0, 1)), (1, (2,))):
            packed = jnp.zeros((32, 128), F32)
            for n, f in enumerate(fields):
                for x in range(8):
                    at = 64 * n + 8 * x
                    moved = turn(main[f, x], at - edge, 1)
                    packed = jnp.where((lane >= at) & (lane < at + 8), moved, packed)
            out[half] = packed


def second_kernel(main, zbefore, znext, to_next, to_before):
    for start, out in ((24, to_next), (0, to_before)):
        rows = pl.ds(start, 8)
        for f in range(3):
            for x in range(8):
                out[f * 8 + x] = main[f, x, rows]
        for half in range(2):
            out[24 + half] = zbefore[half, rows]
            out[26 + half] = znext[half, rows]


def main_tile(f, k, t):
    return 4 * k + t + (f > 0) * (32 + 28 * (f - 1))


def y_tile(f, k):
    return 88 + 10 * f + (2 * k if k < 3 else 3 + k)


TILES = 142


def third_kernel(main, zbefore, znext, ybefore, ynext, to_next, to_before):
    row = rows_like((8, 128))
    for out in (to_next, to_before):
        for k in range(8):
            x = 7 - k if out is to_next else k
            for f in range(3 if k < 7 else 1):
                for t in range(4):
                    out[main_tile(f, k, t)] = main[f, x, pl.ds(8 * t, 8)]
                n, at = f * 8 + x, y_tile(f, k)
                if k < 3:
                    out[at] = ynext[n]
                    out[at + 1] = ybefore[n]
                elif k < 7:
                    out[at] = jnp.where(row < 4, ynext[n], ybefore[n])
        for half in range(2):
            for t in range(4):
                out[118 + half * 4 + t] = zbefore[half, pl.ds(8 * t, 8)]
                out[126 + half * 4 + t] = znext[half, pl.ds(8 * t, 8)]
        out[134:138] = ynext[24:28]
        out[138:142] = ybefore[24:28]


def coarsen_matrix(source):
    rows = lax.broadcasted_iota(jnp.int32, (128, 128), 0)
    cols = lax.broadcasted_iota(jnp.int32, (128, 128), 1)
    return jnp.where(source(rows) == cols, 0.5, 0.0).astype(F32)


def descend_kernel(main, zbefore, znext, ybefore, ynext, before, after, fa, src, inv, one_out, to_next, to_before,
                   fb, upd, mass, pair):
    lane = lanes_like((8, 128))
    row = rows_like((8, 128))
    zero = jnp.zeros((8, 128), F32)

    def own_tile(f, x, t):
        half = f // 2
        if 1 <= t < 5:
            tile = pl.ds(8 * t - 8, 8)
            return main[f, x, tile], zbefore[half, tile], znext[half, tile]
        side = ynext if t == 5 else ybefore
        return side[f * 8 + x], side[24 + half], side[26 + half]

    def far_tile(message, f, k, t):
        half = f // 2
        if 1 <= t < 5:
            return message[main_tile(f, k, t - 1)], message[118 + half * 4 + t - 1], message[126 + half * 4 + t - 1]
        at, corner = y_tile(f, k), 134 if t == 5 else 138
        if k < 3:
            centre = message[at + (t == 0)]
        elif k < 7:
            centre = jnp.where((row < 4) == (t == 5), message[at], 0.0)
        else:
            centre = zero
        return centre, message[corner + half], message[corner + 2 + half]

    for plane in range(24):
        x = plane % 8
        for h in range(2):
            for field in (fa, fb):
                field[plane, h, pl.ds(0, 8)] = zero
                field[plane, h, pl.ds(56, 8)] = zero
        for f in range(3 if 0 < plane < 23 else 1):
            at = (f % 2) * 64 + 8 * x
            for t in range(6):
                if plane < 8:
                    centre, zb, zn = far_tile(before, f, 7 - x, t)
                elif plane < 16:
                    centre, zb, zn = own_tile(f, x, t)
                else:
                    centre, zb, zn = far_tile(after, f, x, t)
                side = jnp.where(lane < 8, turn(zn, -at, 1), 0.0)
                side = jnp.where(lane >= 120, turn(zb, 120 - at, 1), side)
                if f == 2:
                    if 8 <= plane < 16 and 1 <= t < 5:
                        mass[x, pl.ds(8 * t - 8, 8)] = centre
                    centre, side = inverse(centre), inverse(side)
                dest, down = ((fa, 8), (src, 0), (inv, 0))[f]
                dest[plane, 0, pl.ds(8 * t + down, 8)] = centre
                dest[plane, 1, pl.ds(8 * t + down, 8)] = side
    xin, xout = fa, fb
    for k, (a, c) in enumerate(factors(SMOOTH_DEG, *SMOOTH)):
        sweep(xin, xout, upd, src, inv, k + 1, 23 - k, a, c, 2, False)
        xin, xout = xout, xin
    def residual(j, row, own_tile, total):
        if 8 <= row < 40:
            tile = pl.ds(row - 8, 8)
            res = (src[8 + j, 0, pl.ds(row, 8)] + total[0]) - (6.0 + mass[j, tile]) * own_tile[0]
            if j % 2 == 0:
                held[row] = res
            else:
                pair[j // 2, tile] = held[row] + res
                pair[4 + j // 2, tile] = mass[j - 1, tile] + mass[j, tile]

    held = {}
    stencil(xin, 8, 8, 2, range(8, 40, 8), residual)
    even = pair[:, pl.ds(0, 16, stride=2), :] + pair[:, pl.ds(1, 16, stride=2), :]
    one = dot(even.reshape(128, 128), coarsen_matrix(lambda r: r // 2)).reshape(2, 4, 16, 128)
    one_out[...] = one
    lane = lanes_like((16, 128))
    for edge, out in ((32, to_next), (0, to_before)):
        for f in range(2):
            packed = jnp.zeros((16, 128), F32)
            for i in range(4):
                packed = jnp.where(lane // 32 == i, turn(one[f, i], 32 * i - edge, 1), packed)
            out[f] = packed


def widen_kernel(one, zbefore, znext, out):
    lane = lanes_like((16, 128))
    for f in range(2):
        for i in range(4):
            v = one[f, i]
            v = jnp.where(lane // 32 == 2, turn(znext[f], 64 - 32 * i, 1), v)
            out[0, f, i] = jnp.where(lane // 32 == 3, turn(zbefore[f], 96 - 32 * i, 1), v)


def rows_kernel(near, to_next, to_before):
    for start, extra, out in ((8, 7, to_next), (0, 8, to_before)):
        for n in range(32):
            block = near.at[n // 4 % 4, n // 16, n % 4]
            out[n] = block[pl.ds(start, 8)]
            out[32 + n // 8, pl.ds(n % 8, 1)] = block[pl.ds(extra, 1)]


def join_kernel(near, ybefore, ynext, out):
    row = rows_like((8, 128))
    for n in range(32):
        place = n // 4 % 4, n // 16, n % 4
        tile, at = 32 + n // 8, pl.ds(n % 8, 1)
        out[(*place, pl.ds(0, 16))] = near[place]
        out[(*place, pl.ds(16, 8))] = ynext[n]
        mix = jnp.where(row == 0, ynext[tile, at], 0.0)
        out[(*place, pl.ds(24, 8))] = jnp.where(row == 7, ybefore[tile, at], mix)
        out[(*place, pl.ds(32, 8))] = ybefore[n]


def middle_kernel(place, near, far, fb, src, inv, two_out, to_next, to_before,
                  fa, upd, mass, pair, pairs):
    zero = jnp.zeros((40, 128), F32)
    for end in (0, 1, 2, 3, 4, 5, 6, 39, 40, 41, 42, 43, 44, 45, 46):
        for field in (fa, fb):
            field[end, 0, pl.ds(8, 40)] = zero
        src[end, 0] = zero
        inv[end, 0] = zero
    (_, scale), *later = factors(SMOOTH_DEG, *SMOOTH)
    for j in range(8):
        group = place[0] ^ ((j & 1) * 4 + (j >> 1 & 1) * 2 + (j >> 2))
        for i in range(4):
            plane = 7 + 4 * group + i
            values = [(near if j < 4 else far)[j % 4, f, i] for f in range(2)]
            mass[plane] = values[1]
            values[1] = inverse(values[1])
            src[plane, 0] = values[0]
            inv[plane, 0] = values[1]
            u = scale * (values[0] * values[1])
            upd[plane, 0] = u
            for t in range(5):
                put(fa, plane, 0, 8 * t, u[8 * t:8 * t + 8], 40, True)
    xin, xout = fa, fb
    for a, c in later:
        sweep(xin, xout, upd, src, inv, 7, 39, a, c, 4, True)
        xin, xout = xout, xin

    def step(n, carry):
        def residual(j, row, own, total):
            p, tile = 7 + 4 * n + j, pl.ds(row, 8)
            res = (src[p, 0, tile] + total[0]) - (6.0 + mass[p, tile]) * own[0]
            if j % 2 == 0:
                held[row] = res
            else:
                pair[2 * n + j // 2, tile] = held[row] + res
                pair[16 + 2 * n + j // 2, tile] = mass[p - 1, tile] + mass[p, tile]

        held = {}
        stencil(xin, 7 + 4 * n, 4, 1, range(0, 40, 8), residual)
        return carry

    lax.fori_loop(0, 8, step, 0)
    even = pair[:, pl.ds(0, 20, stride=2), :] + pair[:, pl.ds(1, 20, stride=2), :]
    pairs[:, pl.ds(0, 20)] = even
    pairs[:, pl.ds(20, 4)] = jnp.zeros((32, 4, 128), F32)
    down = [coarsen_matrix(lambda r, h=h: 64 * h + 16 + jnp.where(r < 96, r // 2, r // 2 - 64)) for h in range(2)]
    for f in range(2):
        low = pairs[pl.ds(16 * f, 8)].reshape(192, 128)
        high = pairs[pl.ds(16 * f + 8, 8)].reshape(192, 128)
        made = (dot(low, down[0]) + dot(high, down[1])).reshape(8, 24, 128)
        for i in range(8):
            n = 8 * f + i
            two_out[n] = made[i, 0:8]
            at = pl.ds(2 * (n % 4), 2)
            to_next[n] = made[i, 0:8]
            to_before[n] = made[i, 0:8]
            to_next[16 + n // 4, at] = made[i, 18:20]
            to_before[16 + n // 4, at] = made[i, 8:10]


def one_hot(shape, axis, source):
    at = lax.broadcasted_iota(jnp.int32, shape, axis)
    return jnp.where(at == source, 1.0, 0.0).astype(F32)


def ascend_kernel(place, two, before, after, x1, src1, inv1, x0, src0, inv0, out,
                  ca, cb, cupd, csrc, cinv, flat, oa, ob, oupd, za, zb, zupd):
    row = rows_like((8, 128))
    lane = lanes_like((32, 128))
    (_, scale), *later = factors(COARSE_DEG, *COARSE)
    for i in range(8):
        values = []
        for f in range(2):
            n = 8 * f + i
            mix = jnp.where(row < 2, turn(after[16 + n // 4], -2 * (n % 4), 0), 0.0)
            mix = jnp.where(row >= 6, turn(before[16 + n // 4], 6 - 2 * (n % 4), 0), mix)
            values.append(jnp.concatenate([two[n], after[n], mix, before[n]], axis=0))
        values[1] = inverse(values[1])
        csrc[1 + i, 0] = values[0]
        cinv[1 + i, 0] = values[1]
        u = scale * (values[0] * values[1])
        cupd[1 + i, 0] = u
        for t in range(4):
            put(ca, 1 + i, 0, 8 * t, u[8 * t:8 * t + 8], 32, True)
    xin, xout = ca, cb
    core = pl.ds(8, 32)
    for a, c in later:
        xin[0, 0, core] = jnp.where(lane >= 64, pltpu.roll(xin[8, 0, core], 64, 1), 0.0)
        xin[9, 0, core] = jnp.where(lane < 64, pltpu.roll(xin[1, 0, core], 64, 1), 0.0)
        sweep(xin, xout, cupd, csrc, cinv, 1, 9, a, c, 8, True)
        xin, xout = xout, xin
    zero = jnp.zeros((32, 128), F32)
    for end in (0, 1, 2, 19, 20, 21):
        flat[end] = zero
    for q in range(16):
        v = xin[1 + q % 8, 0, core]
        flat[3 + q] = v if q < 8 else pltpu.roll(v, 64, 1)
    l = lax.broadcasted_iota(jnp.int32, (1, 128), 1)
    wide = one_hot((128, 128), 0, jnp.where(l < 96, 16 + l // 2, l // 2 - 48))
    r = lax.broadcasted_iota(jnp.int32, (40, 1), 0)
    tall = one_hot((40, 32), 1, jnp.where(r < 28, r // 2, 12 + r // 2))
    part = dot(flat[pl.ds(2 * place[0], 8)].reshape(256, 128), wide)
    fine = dot(tall, jnp.concatenate([part[32 * w:32 * w + 32] for w in range(8)], axis=1))
    first = 4 * place[0] + 1
    for w in range(16):
        v = w // 2
        for t in range(5):
            value = x1[first + w, 0, pl.ds(8 + 8 * t, 8)] + fine[8 * t:8 * t + 8, 128 * v:128 * v + 128]
            put(oa, w, 0, 8 * t, value, 40, True)
    xin, xout = oa, ob
    for k, (a, c) in enumerate(factors(SMOOTH_DEG, *SMOOTH)):
        sweep(xin, xout, oupd, src1, inv1, k + 1, 15 - k, a, c, 14 - 2 * k, True, offset=first)
        xin, xout = xout, xin
    side = jnp.where((l < 8) | (l >= 120), 64 + l // 2, -1)
    wide = [one_hot((128, 128), 0, l // 2), one_hot((128, 128), 0, side)]
    r = lax.broadcasted_iota(jnp.int32, (48, 1), 0)
    tall = one_hot((48, 40), 1, jnp.where(r < 8, 36 + r // 2, r // 2 - 4))
    below = xin[4:12, 0, 8:48].reshape(320, 128)
    zero = jnp.zeros((8, 128), F32)
    for h in range(2):
        part = dot(below, wide[h])
        fine = dot(tall, jnp.concatenate([part[40 * w:40 * w + 40] for w in range(8)], axis=1))
        for w in range(16):
            v = w // 2
            za[w, h, pl.ds(8, 48)] = x0[4 + w, h, pl.ds(8, 48)] + fine[:, 128 * v:128 * v + 128]
            for field in (za, zb):
                field[w, h, pl.ds(0, 8)] = zero
                field[w, h, pl.ds(56, 8)] = zero
    xin, xout = za, zb
    for k, (a, c) in enumerate(factors(SMOOTH_DEG, *SMOOTH)):
        sweep(xin, xout, zupd, src0, inv0, k + 1, 15 - k, a, c, 2, False, offset=4)
        xin, xout = xout, xin
    out[...] = xin[4:12, 0, 16:48]


def call(kernel, outs, scratch, *args, spaces=(), limit=24):
    vmem = pl.BlockSpec(memory_space=pltpu.VMEM)
    spaces = [pl.BlockSpec(memory_space=space) for space in spaces]
    scratch = [pltpu.VMEM(s, F32) if isinstance(s, tuple) else s for s in scratch]
    return pl.pallas_call(
        kernel,
        out_shape=[jax.ShapeDtypeStruct(s, F32) for s in outs],
        in_specs=spaces + [vmem] * (len(args) - len(spaces)),
        out_specs=[vmem] * len(outs),
        scratch_shapes=scratch,
        compiler_params=pltpu.CompilerParams(vmem_limit_bytes=limit * 1024 * 1024),
    )(*args)


def shift(value, axis, by):
    count = lax.axis_size(axis)
    pairs = [(i, i + by) for i in range(count) if 0 <= i + by < count]
    return lax.ppermute(value, axis, pairs)


def swap(value, axis, bit):
    return lax.ppermute(value, axis, [(i, i ^ bit) for i in range(lax.axis_size(axis))])


def per_device(right_side, predicted, zone, zone_table):
    place = lax.axis_index("gx").astype(jnp.int32).reshape(1)
    block = (8, 32, 128)
    main, nxt, bef = call(first_kernel, [(3, *block), (2, 32, 128), (2, 32, 128)],
                          [pltpu.VMEM(block, jnp.int32), pltpu.SemaphoreType.DMA((3,))],
                          zone_table, predicted, right_side, zone,
                          spaces=[pltpu.SMEM, pltpu.HBM, pltpu.HBM, pltpu.HBM], limit=56)
    zbefore, znext = shift(nxt, "gz", 1), shift(bef, "gz", -1)
    nxt, bef = call(second_kernel, [(28, 8, 128)] * 2, [], main, zbefore, znext)
    ybefore, ynext = shift(nxt, "gy", 1), shift(bef, "gy", -1)
    nxt, bef = call(third_kernel, [(TILES, 8, 128)] * 2, [], main, zbefore, znext, ybefore, ynext)
    before, after = shift(nxt, "gx", 1), shift(bef, "gx", -1)
    tall, flat = (24, 2, 64, 128), (24, 2, 48, 128)
    x0, src0, inv0, one, nxt, bef = call(
        descend_kernel,
        [tall, flat, flat, (2, 4, 16, 128), (2, 16, 128), (2, 16, 128)],
        [tall, flat, block, block],
        main, zbefore, znext, ybefore, ynext, before, after)
    zbefore, znext = shift(nxt, "gz", 1), shift(bef, "gz", -1)
    near, = call(widen_kernel, [(1, 2, 4, 16, 128)], [], one, zbefore, znext)
    near = jnp.concatenate([near, swap(near, "gx", 4)])
    near = jnp.concatenate([near, swap(near, "gx", 2)])
    nxt, bef = call(rows_kernel, [(36, 8, 128)] * 2, [], near)
    ybefore, ynext = shift(nxt, "gy", 1), shift(bef, "gy", -1)
    near, = call(join_kernel, [(4, 2, 4, 40, 128)], [], near, ybefore, ynext)
    far = swap(near, "gx", 1)
    tall, flat = (47, 1, 56, 128), (47, 1, 40, 128)
    x1, src1, inv1, two, nxt, bef = call(
        middle_kernel,
        [tall, flat, flat, (16, 8, 128), (20, 8, 128), (20, 8, 128)],
        [tall, flat, (47, 40, 128), (32, 40, 128), (32, 24, 128)],
        place, near, far, spaces=[pltpu.SMEM])
    before, after = shift(nxt, "gy", 1), shift(bef, "gy", -1)
    out, = call(
        ascend_kernel,
        [(8, 32, 128)],
        [(10, 1, 48, 128)] * 2 + [(10, 1, 32, 128)] * 3 + [(22, 32, 128)]
        + [(16, 1, 56, 128)] * 2 + [(16, 1, 40, 128)] + [(16, 2, 64, 128)] * 2 + [(16, 2, 48, 128)],
        place, two, before, after, x1, src1, inv1, x0, src0, inv0, spaces=[pltpu.SMEM])
    return out


def solution(mesh):
    placed = (P("gx", "gy", "gz"), P("gx", "gy", "gz"), P("gx", "gy", "gz"), P())
    return jax.shard_map(
        per_device, mesh=mesh, in_specs=placed, out_specs=P("gx", "gy", "gz"), check_vma=False
    )
```

time: 1040 us -> 127 us (0.12)
  the two profiles are of different devices: /device:TPU:439 before, /device:TPU:14 now
where the time goes in v1:
time: 127 us
  starting transfers between devices  55 us (43%)
  waiting for transfers between devices  49 us (39%)
  Pallas kernels  21.7 us (17%)
    ppermute x12, starting transfers between devices, shift(): return lax.ppermute(value, axis, pairs)  39.9 us
    ppermute x12, waiting for transfers between devices, shift(): return lax.ppermute(value, axis, pairs)  38.6 us
    pallas_call x9, Pallas kernels, call(): pl.pallas_call(kernel, out_shape=[jax.ShapeDtypeStruct(s, F32) for s in o...  21.7 us
    ppermute x3, starting transfers between devices, swap(): lax.ppermute(value, axis, [(i, i ^ bit) for i in range(lax.axis_size(axis...  15 us
    ppermute x3, waiting for transfers between devices, swap(): lax.ppermute(value, axis, [(i, i ^ bit) for i in range(lax.axis_size(axis...  10.4 us
  transfers between devices with their start and end apart: 15, of which 15 were waited for; matrix products, arithmetic and copies ran while one was open for 0% of the time, Pallas kernels for 0%

profile of v1, /device:TPU:14, one launch (start us, length us, event | category | flops | bytes accessed | tf_op | source)
XLA Modules:
  0.0 126.9 jit_solution(4483593221794025475)
XLA Ops:
  0.0 2.7 %shard_map.46 = (f32[3,8,32,128]{3,2,1,0:T(8,128)}, f32[2,32,128]{2,1,0:T(8,128)}, f32[2,32,128]{2,1,0:T(8,128)}) custom-call(f32[16]{0:T(128)} %table.1, f32[8,32,128]{2,1,0:T(8,128)} %pred_.1, f32[8,32,128]{2,1,0:T(8,128)} %right.1, s32[8,32,128]{2,1,0:T(8,128)} %zone.1), custom_call_target="tpu_custom_call" | custom-call | tf_op jit(solution)/shard_map/pallas_call | solution.py:434
  2.7 9.1 %collective-permute-start = (f32[2,32,128]{2,1,0:T(8,128)}, f32[2,32,128]{2,1,0:T(8,128)S(1)}, u32[]{:S(2)}, u32[]{:S(2)}) collective-permute-start(f32[2,32,128]{2,1,0:T(8,128)} %get-tuple-element.27), channel_id=1, source_target_pairs={{0,1},{1,2},{2,3},{4,5},{5,6},{6,7},{8,9},{9,10},{10,11},{12,13},{... | collective-permute-start | bytes 98312 | tf_op jit(solution)/shard_map/ppermute | solution.py:447
  13.7 10.0 %collective-permute-done.1.znext = f32[2,32,128]{2,1,0:T(8,128)S(1)} collective-permute-done((f32[2,32,128]{2,1,0:T(8,128)}, f32[2,32,128]{2,1,0:T(8,128)S(1)}, u32[]{:S(2)}, u32[]{:S(2)}) %collective-permute-start.1) | collective-permute-done | bytes 32800 | tf_op jit(solution)/shard_map/ppermute | solution.py:447
  24.7 3.4 %collective-permute-start.2 = (f32[28,8,128]{2,1,0:T(8,128)S(1)}, f32[28,8,128]{2,1,0:T(8,128)S(1)}, u32[]{:S(2)}, u32[]{:S(2)}) collective-permute-start(f32[28,8,128]{2,1,0:T(8,128)S(1)} %get-tuple-element.29), channel_id=1, source_target_pairs={{0,4},{4,8},{8,12},{12,16},{16,20},{20,24},{24,28},{28,32},{32,36}... | collective-permute-start | bytes 344072 | tf_op jit(solution)/shard_map/ppermute | solution.py:447
  28.1 2.4 %collective-permute-start.3 = (f32[28,8,128]{2,1,0:T(8,128)S(1)}, f32[28,8,128]{2,1,0:T(8,128)S(1)}, u32[]{:S(2)}, u32[]{:S(2)}) collective-permute-start(f32[28,8,128]{2,1,0:T(8,128)S(1)} %get-tuple-element.30), channel_id=1, source_target_pairs={{4,0},{8,4},{12,8},{16,12},{20,16},{24,20},{28,24},{32,28},{36,32}... | collective-permute-start | bytes 344072 | tf_op jit(solution)/shard_map/ppermute | solution.py:447
  31.4 5.5 %collective-permute-done.3.ynext = f32[28,8,128]{2,1,0:T(8,128)S(1)} collective-permute-done((f32[28,8,128]{2,1,0:T(8,128)S(1)}, f32[28,8,128]{2,1,0:T(8,128)S(1)}, u32[]{:S(2)}, u32[]{:S(2)}) %collective-permute-start.3) | collective-permute-done | bytes 114720 | tf_op jit(solution)/shard_map/ppermute | solution.py:447
  39.9 2.9 %collective-permute-done.5.after = f32[142,8,128]{2,1,0:T(8,128)S(1)} collective-permute-done((f32[142,8,128]{2,1,0:T(8,128)S(1)}, f32[142,8,128]{2,1,0:T(8,128)S(1)}, u32[]{:S(2)}, u32[]{:S(2)}) %collective-permute-start.5) | collective-permute-done | bytes 581664 | tf_op jit(solution)/shard_map/ppermute | solution.py:447
  42.7 6.3 %shard_map.49 = (f32[24,2,64,128]{3,2,1,0:T(8,128)S(1)}, f32[24,2,48,128]{3,2,1,0:T(8,128)S(1)}, f32[24,2,48,128]{3,2,1,0:T(8,128)S(1)}, f32[2,4,16,128]{3,2,1,0...) custom-call(f32[3,8,32,128]{3,2,1,0:T(8,128)S(1)} %copy-done, ...), custom_call_target="tpu_custom_call" | custom-call | tf_op jit(solution)/shard_map/pallas_call | solution.py:434
  49.0 8.1 %collective-permute-start.6 = (f32[2,16,128]{2,1,0:T(8,128)S(1)}, f32[2,16,128]{2,1,0:T(8,128)S(1)}, u32[]{:S(2)}, u32[]{:S(2)}) collective-permute-start(f32[2,16,128]{2,1,0:T(8,128)S(1)} %get-tuple-element.34), channel_id=1, source_target_pairs={{0,1},{1,2},{2,3},{4,5},{5,6},{6,7},{8,9},{9,10},{10,11},{12,13},{... | collective-permute-start | bytes 49160 | tf_op jit(solution)/shard_map/ppermute | solution.py:447
  58.6 8.1 %collective-permute-done.7.znext = f32[2,16,128]{2,1,0:T(8,128)S(1)} collective-permute-done((f32[2,16,128]{2,1,0:T(8,128)S(1)}, f32[2,16,128]{2,1,0:T(8,128)S(1)}, u32[]{:S(2)}, u32[]{:S(2)}) %collective-permute-start.7) | collective-permute-done | bytes 16416 | tf_op jit(solution)/shard_map/ppermute | solution.py:447
  66.8 9.9 %collective-permute-start.8 = (f32[1,2,4,16,128]{4,3,2,1,0:T(8,128)S(1)}, f32[1,2,4,16,128]{4,3,2,1,0:T(8,128)S(1)}, u32[]{:S(2)}, u32[]{:S(2)}) collective-permute-start(f32[1,2,4,16,128]{4,3,2,1,0:T(8,128)S(1)} %shard_map.50), channel_id=1, source_target_pairs={{0,256},{64,320},{128,384},{192,448},{256,0},{320,64},{384,128},{4... | collective-permute-start | bytes 196616 | tf_op jit(solution)/shard_map/ppermute | solution.py:451
  76.7 3.4 %collective-permute-done.8 = f32[1,2,4,16,128]{4,3,2,1,0:T(8,128)S(1)} collective-permute-done((f32[1,2,4,16,128]{4,3,2,1,0:T(8,128)S(1)}, f32[1,2,4,16,128]{4,3,2,1,0:T(8,128)S(1)}, u32[]{:S(2)}, u32[]{:S(2)}) %collective-permute-start.8) | collective-permute-done | bytes 65568 | tf_op jit(solution)/shard_map/ppermute | solution.py:451
  80.2 3.2 %collective-permute-start.9 = (f32[2,2,4,16,128]{4,3,2,1,0:T(8,128)S(1)}, f32[2,2,4,16,128]{4,3,2,1,0:T(8,128)S(1)}, u32[]{:S(2)}, u32[]{:S(2)}) collective-permute-start(f32[2,2,4,16,128]{4,3,2,1,0:T(8,128)S(1)} %pad_maximum_fusion.1), channel_id=1, source_target_pairs={{0,128},{64,192},{128,0},{192,64},{256,384},{320,448},{384,256},{4... | collective-permute-start | bytes 393224 | tf_op jit(solution)/shard_map/ppermute | solution.py:451
  83.3 4.8 %collective-permute-done.9 = f32[2,2,4,16,128]{4,3,2,1,0:T(8,128)S(1)} collective-permute-done((f32[2,2,4,16,128]{4,3,2,1,0:T(8,128)S(1)}, f32[2,2,4,16,128]{4,3,2,1,0:T(8,128)S(1)}, u32[]{:S(2)}, u32[]{:S(2)}) %collective-permute-start.9) | collective-permute-done | bytes 131104 | tf_op jit(solution)/shard_map/ppermute | solution.py:451
  88.3 1.9 %collective-permute-start.10 = (f32[36,8,128]{2,1,0:T(8,128)S(1)}, f32[36,8,128]{2,1,0:T(8,128)S(1)}, u32[]{:S(2)}, u32[]{:S(2)}) collective-permute-start(f32[36,8,128]{2,1,0:T(8,128)S(1)} %get-tuple-element.36), channel_id=1, source_target_pairs={{0,4},{4,8},{8,12},{12,16},{16,20},{20,24},{24,28},{28,32},{32,36}... | collective-permute-start | bytes 442376 | tf_op jit(solution)/shard_map/ppermute | solution.py:447
  90.2 3.9 %collective-permute-start.11 = (f32[36,8,128]{2,1,0:T(8,128)S(1)}, f32[36,8,128]{2,1,0:T(8,128)S(1)}, u32[]{:S(2)}, u32[]{:S(2)}) collective-permute-start(f32[36,8,128]{2,1,0:T(8,128)S(1)} %get-tuple-element.37), channel_id=1, source_target_pairs={{4,0},{8,4},{12,8},{16,12},{20,16},{24,20},{28,24},{32,28},{36,32}... | collective-permute-start | bytes 442376 | tf_op jit(solution)/shard_map/ppermute | solution.py:447
  95.8 4.0 %collective-permute-done.11.ynext = f32[36,8,128]{2,1,0:T(8,128)S(1)} collective-permute-done((f32[36,8,128]{2,1,0:T(8,128)S(1)}, f32[36,8,128]{2,1,0:T(8,128)S(1)}, u32[]{:S(2)}, u32[]{:S(2)}) %collective-permute-start.11) | collective-permute-done | bytes 147488 | tf_op jit(solution)/shard_map/ppermute | solution.py:447
  99.9 1.9 %collective-permute-start.12 = (f32[4,2,4,40,128]{4,3,2,1,0:T(8,128)S(1)}, f32[4,2,4,40,128]{4,3,2,1,0:T(8,128)}, u32[]{:S(2)}, u32[]{:S(2)}) collective-permute-start(f32[4,2,4,40,128]{4,3,2,1,0:T(8,128)S(1)} %shard_map.52.near), channel_id=1, source_target_pairs={{0,64},{64,0},{128,192},{192,128},{256,320},{320,256},{384,448},{4... | collective-permute-start | bytes 1966088 | tf_op jit(solution)/shard_map/ppermute | solution.py:451
  101.8 2.2 %collective-permute-done.12.far = f32[4,2,4,40,128]{4,3,2,1,0:T(8,128)} collective-permute-done((f32[4,2,4,40,128]{4,3,2,1,0:T(8,128)S(1)}, f32[4,2,4,40,128]{4,3,2,1,0:T(8,128)}, u32[]{:S(2)}, u32[]{:S(2)}) %collective-permute-start.12) | collective-permute-done | bytes 655392 | tf_op jit(solution)/shard_map/ppermute | solution.py:451
  104.0 5.8 %shard_map.53 = (f32[47,1,56,128]{3,2,1,0:T(8,128)S(1)}, f32[47,1,40,128]{3,2,1,0:T(8,128)S(1)}, f32[47,1,40,128]{3,2,1,0:T(8,128)S(1)}, f32[16,8,128]{2,1,0:T(8...) custom-call(s32[1]{0:T(128)} %bitcast.place, f32[4,2,4,40,128]{4,3,2,1,0:T(8,128)S(1)} %shard_map.52.near, ...), custom_call_target="tpu_custom_call" | custom-call | tf_op jit(solution)/shard_map/pallas_call | solution.py:434
  109.8 1.9 %collective-permute-start.13 = (f32[20,8,128]{2,1,0:T(8,128)S(1)}, f32[20,8,128]{2,1,0:T(8,128)S(1)}, u32[]{:S(2)}, u32[]{:S(2)}) collective-permute-start(f32[20,8,128]{2,1,0:T(8,128)S(1)} %get-tuple-element.39), channel_id=1, source_target_pairs={{0,4},{4,8},{8,12},{12,16},{16,20},{20,24},{24,28},{28,32},{32,36}... | collective-permute-start | bytes 245768 | tf_op jit(solution)/shard_map/ppermute | solution.py:447
  111.7 3.9 %collective-permute-start.14 = (f32[20,8,128]{2,1,0:T(8,128)S(1)}, f32[20,8,128]{2,1,0:T(8,128)S(1)}, u32[]{:S(2)}, u32[]{:S(2)}) collective-permute-start(f32[20,8,128]{2,1,0:T(8,128)S(1)} %get-tuple-element.40), channel_id=1, source_target_pairs={{4,0},{8,4},{12,8},{16,12},{20,16},{24,20},{28,24},{32,28},{36,32}... | collective-permute-start | bytes 245768 | tf_op jit(solution)/shard_map/ppermute | solution.py:447
  116.2 4.0 %collective-permute-done.14.after = f32[20,8,128]{2,1,0:T(8,128)S(1)} collective-permute-done((f32[20,8,128]{2,1,0:T(8,128)S(1)}, f32[20,8,128]{2,1,0:T(8,128)S(1)}, u32[]{:S(2)}, u32[]{:S(2)}) %collective-permute-start.14) | collective-permute-done | bytes 81952 | tf_op jit(solution)/shard_map/ppermute | solution.py:447
  120.2 6.7 %shard_map.54 = f32[8,32,128]{2,1,0:T(8,128)} custom-call(s32[1]{0:T(128)} %bitcast.place, f32[16,8,128]{2,1,0:T(8,128)S(1)} %get-tuple-element.38.two, f32[20,8,128]{2,1,0:T(8,128)S(1)} %collective-permute-done.13.before, f32[20,8,128]{2,1,0:T(8,128)S(1)} %collective-permute-done.14.after, f32[47,1,56,128]{3,2,1,0:T(8,128)S(1)} %get-tuple-element.41.x1, ...), custom_call_target="tpu_custom_call" | custom-call | tf_op jit(solution)/shard_map/pallas_call | solution.py:434
  (23 shorter events, 10.5 us)
Async XLA Ops:
  2.7 11.0 %collective-permute-start = (f32[2,32,128]{2,1,0:T(8,128)}, f32[2,32,128]{2,1,0:T(8,128)S(1)}, u32[]{:S(2)}, u32[]{:S(2)}) collective-permute-start(f32[2,32,128]{2,1,0:T(8,128)} %get-tuple-element.27), channel_id=1, source_target_pairs={{0,1},{1,2},{2,3},{4,5},{5,6},{6,7},{8,9},{9,10},{10,11},{12,13},{... | collective-permute-start | bytes 98312 | tf_op jit(solution)/shard_map/ppermute | solution.py:447
  11.8 11.9 %collective-permute-start.1 = (f32[2,32,128]{2,1,0:T(8,128)}, f32[2,32,128]{2,1,0:T(8,128)S(1)}, u32[]{:S(2)}, u32[]{:S(2)}) collective-permute-start(f32[2,32,128]{2,1,0:T(8,128)} %get-tuple-element.28), channel_id=1, source_target_pairs={{1,0},{2,1},{3,2},{5,4},{6,5},{7,6},{9,8},{10,9},{11,10},{13,12},{... | collective-permute-start | bytes 98312 | tf_op jit(solution)/shard_map/ppermute | solution.py:447
  23.7 1.0 copy-start
  24.7 6.7 %collective-permute-start.2 = (f32[28,8,128]{2,1,0:T(8,128)S(1)}, f32[28,8,128]{2,1,0:T(8,128)S(1)}, u32[]{:S(2)}, u32[]{:S(2)}) collective-permute-start(f32[28,8,128]{2,1,0:T(8,128)S(1)} %get-tuple-element.29), channel_id=1, source_target_pairs={{0,4},{4,8},{8,12},{12,16},{16,20},{20,24},{24,28},{28,32},{32,36}... | collective-permute-start | bytes 344072 | tf_op jit(solution)/shard_map/ppermute | solution.py:447
  28.1 8.8 %collective-permute-start.3 = (f32[28,8,128]{2,1,0:T(8,128)S(1)}, f32[28,8,128]{2,1,0:T(8,128)S(1)}, u32[]{:S(2)}, u32[]{:S(2)}) collective-permute-start(f32[28,8,128]{2,1,0:T(8,128)S(1)} %get-tuple-element.30), channel_id=1, source_target_pairs={{4,0},{8,4},{12,8},{16,12},{20,16},{24,20},{28,24},{32,28},{36,32}... | collective-permute-start | bytes 344072 | tf_op jit(solution)/shard_map/ppermute | solution.py:447
  37.0 2.9 %collective-permute-start.4 = (f32[142,8,128]{2,1,0:T(8,128)S(1)}, f32[142,8,128]{2,1,0:T(8,128)S(1)}, u32[]{:S(2)}, u32[]{:S(2)}) collective-permute-start(f32[142,8,128]{2,1,0:T(8,128)S(1)} %get-tuple-element.31), channel_id=1, source_target_pairs={{0,64},{64,128},{128,192},{192,256},{256,320},{320,384},{384,448},... | collective-permute-start | bytes 1744904 | tf_op jit(solution)/shard_map/ppermute | solution.py:447
  38.3 4.4 %collective-permute-start.5 = (f32[142,8,128]{2,1,0:T(8,128)S(1)}, f32[142,8,128]{2,1,0:T(8,128)S(1)}, u32[]{:S(2)}, u32[]{:S(2)}) collective-permute-start(f32[142,8,128]{2,1,0:T(8,128)S(1)} %get-tuple-element.32), channel_id=1, source_target_pairs={{64,0},{128,64},{192,128},{256,192},{320,256},{384,320},{448,384},... | collective-permute-start | bytes 1744904 | tf_op jit(solution)/shard_map/ppermute | solution.py:447
  49.0 50.9 %copy-start.1 = (f32[24,2,48,128]{3,2,1,0:T(8,128)}, f32[24,2,48,128]{3,2,1,0:T(8,128)S(1)}, u32[]{:S(2)}) copy-start(f32[24,2,48,128]{3,2,1,0:T(8,128)S(1)} %get-tuple-element.46.inv0) | copy-start | bytes 3538948
  49.0 9.6 %collective-permute-start.6 = (f32[2,16,128]{2,1,0:T(8,128)S(1)}, f32[2,16,128]{2,1,0:T(8,128)S(1)}, u32[]{:S(2)}, u32[]{:S(2)}) collective-permute-start(f32[2,16,128]{2,1,0:T(8,128)S(1)} %get-tuple-element.34), channel_id=1, source_target_pairs={{0,1},{1,2},{2,3},{4,5},{5,6},{6,7},{8,9},{9,10},{10,11},{12,13},{... | collective-permute-start | bytes 49160 | tf_op jit(solution)/shard_map/ppermute | solution.py:447
  57.1 9.5 %collective-permute-start.7 = (f32[2,16,128]{2,1,0:T(8,128)S(1)}, f32[2,16,128]{2,1,0:T(8,128)S(1)}, u32[]{:S(2)}, u32[]{:S(2)}) collective-permute-start(f32[2,16,128]{2,1,0:T(8,128)S(1)} %get-tuple-element.35), channel_id=1, source_target_pairs={{1,0},{2,1},{3,2},{5,4},{6,5},{7,6},{9,8},{10,9},{11,10},{13,12},{... | collective-permute-start | bytes 49160 | tf_op jit(solution)/shard_map/ppermute | solution.py:447
  66.8 13.4 %collective-permute-start.8 = (f32[1,2,4,16,128]{4,3,2,1,0:T(8,128)S(1)}, f32[1,2,4,16,128]{4,3,2,1,0:T(8,128)S(1)}, u32[]{:S(2)}, u32[]{:S(2)}) collective-permute-start(f32[1,2,4,16,128]{4,3,2,1,0:T(8,128)S(1)} %shard_map.50), channel_id=1, source_target_pairs={{0,256},{64,320},{128,384},{192,448},{256,0},{320,64},{384,128},{4... | collective-permute-start | bytes 196616 | tf_op jit(solution)/shard_map/ppermute | solution.py:451
  80.2 8.0 %collective-permute-start.9 = (f32[2,2,4,16,128]{4,3,2,1,0:T(8,128)S(1)}, f32[2,2,4,16,128]{4,3,2,1,0:T(8,128)S(1)}, u32[]{:S(2)}, u32[]{:S(2)}) collective-permute-start(f32[2,2,4,16,128]{4,3,2,1,0:T(8,128)S(1)} %pad_maximum_fusion.1), channel_id=1, source_target_pairs={{0,128},{64,192},{128,0},{192,64},{256,384},{320,448},{384,256},{4... | collective-permute-start | bytes 393224 | tf_op jit(solution)/shard_map/ppermute | solution.py:451
  88.3 7.5 %collective-permute-start.10 = (f32[36,8,128]{2,1,0:T(8,128)S(1)}, f32[36,8,128]{2,1,0:T(8,128)S(1)}, u32[]{:S(2)}, u32[]{:S(2)}) collective-permute-start(f32[36,8,128]{2,1,0:T(8,128)S(1)} %get-tuple-element.36), channel_id=1, source_target_pairs={{0,4},{4,8},{8,12},{12,16},{16,20},{20,24},{24,28},{28,32},{32,36}... | collective-permute-start | bytes 442376 | tf_op jit(solution)/shard_map/ppermute | solution.py:447
  90.2 9.6 %collective-permute-start.11 = (f32[36,8,128]{2,1,0:T(8,128)S(1)}, f32[36,8,128]{2,1,0:T(8,128)S(1)}, u32[]{:S(2)}, u32[]{:S(2)}) collective-permute-start(f32[36,8,128]{2,1,0:T(8,128)S(1)} %get-tuple-element.37), channel_id=1, source_target_pairs={{4,0},{8,4},{12,8},{16,12},{20,16},{24,20},{28,24},{32,28},{36,32}... | collective-permute-start | bytes 442376 | tf_op jit(solution)/shard_map/ppermute | solution.py:447
  99.9 4.1 %collective-permute-start.12 = (f32[4,2,4,40,128]{4,3,2,1,0:T(8,128)S(1)}, f32[4,2,4,40,128]{4,3,2,1,0:T(8,128)}, u32[]{:S(2)}, u32[]{:S(2)}) collective-permute-start(f32[4,2,4,40,128]{4,3,2,1,0:T(8,128)S(1)} %shard_map.52.near), channel_id=1, source_target_pairs={{0,64},{64,0},{128,192},{192,128},{256,320},{320,256},{384,448},{4... | collective-permute-start | bytes 1966088 | tf_op jit(solution)/shard_map/ppermute | solution.py:451
  101.8 18.4 %copy-start.2 = (f32[24,2,48,128]{3,2,1,0:T(8,128)S(1)}, f32[24,2,48,128]{3,2,1,0:T(8,128)}, u32[]{:S(2)}) copy-start(f32[24,2,48,128]{3,2,1,0:T(8,128)} %copy-done.1) | copy-start | bytes 3538948
  109.8 6.4 %collective-permute-start.13 = (f32[20,8,128]{2,1,0:T(8,128)S(1)}, f32[20,8,128]{2,1,0:T(8,128)S(1)}, u32[]{:S(2)}, u32[]{:S(2)}) collective-permute-start(f32[20,8,128]{2,1,0:T(8,128)S(1)} %get-tuple-element.39), channel_id=1, source_target_pairs={{0,4},{4,8},{8,12},{12,16},{16,20},{20,24},{24,28},{28,32},{32,36}... | collective-permute-start | bytes 245768 | tf_op jit(solution)/shard_map/ppermute | solution.py:447
  111.7 8.5 %collective-permute-start.14 = (f32[20,8,128]{2,1,0:T(8,128)S(1)}, f32[20,8,128]{2,1,0:T(8,128)S(1)}, u32[]{:S(2)}, u32[]{:S(2)}) collective-permute-start(f32[20,8,128]{2,1,0:T(8,128)S(1)} %get-tuple-element.40), channel_id=1, source_target_pairs={{4,0},{8,4},{12,8},{16,12},{20,16},{24,20},{28,24},{32,28},{36,32}... | collective-permute-start | bytes 245768 | tf_op jit(solution)/shard_map/ppermute | solution.py:447

commit v2 on v1

--- a/solution.py
+++ b/solution.py
@@ -106,6 +106,12 @@
 
 def inverse(mass):
     return jnp.where(mass > 0.0, 1.0 / (6.0 + mass), 0.0)
+
+
+def by_parity(place, a, b, body):
+    odd = place[0] % 2
+    pl.when(odd == 1)(lambda: body(a, b))
+    pl.when(odd == 0)(lambda: body(b, a))
 
 
 def first_kernel(table, pred, right, zone, main, to_next, to_before, codes, sems):
@@ -134,15 +140,20 @@
             out[half] = packed
 
 
-def second_kernel(main, zbefore, znext, to_next, to_before):
-    for start, out in ((24, to_next), (0, to_before)):
-        rows = pl.ds(start, 8)
-        for f in range(3):
-            for x in range(8):
-                out[f * 8 + x] = main[f, x, rows]
-        for half in range(2):
-            out[24 + half] = zbefore[half, rows]
-            out[26 + half] = znext[half, rows]
+def second_kernel(py, main, zbefore, znext, ya, yb, kept):
+    kept[...] = main[...]
+
+    def body(to_next, to_before):
+        for start, out in ((24, to_next), (0, to_before)):
+            rows = pl.ds(start, 8)
+            for f in range(3):
+                for x in range(8):
+                    out[f * 8 + x] = main[f, x, rows]
+            for half in range(2):
+                out[24 + half] = zbefore[half, rows]
+                out[26 + half] = znext[half, rows]
+
+    by_parity(py, ya, yb, body)
 
 
 def main_tile(f, k, t):
@@ -156,26 +167,36 @@
 TILES = 142
 
 
-def third_kernel(main, zbefore, znext, ybefore, ynext, to_next, to_before):
+def third_kernel(px, py, main, zbefore, znext, ya, yb, xa, xb, ybefore, ynext):
     row = rows_like((8, 128))
-    for out in (to_next, to_before):
-        for k in range(8):
-            x = 7 - k if out is to_next else k
-            for f in range(3 if k < 7 else 1):
+
+    def settle(after, before):
+        ynext[...] = after[...]
+        ybefore[...] = before[...]
+
+    by_parity(py, ya, yb, settle)
+
+    def body(to_next, to_before):
+        for out in (to_next, to_before):
+            for k in range(8):
+                x = 7 - k if out is to_next else k
+                for f in range(3 if k < 7 else 1):
+                    for t in range(4):
+                        out[main_tile(f, k, t)] = main[f, x, pl.ds(8 * t, 8)]
+                    n, at = f * 8 + x, y_tile(f, k)
+                    if k < 3:
+                        out[at] = ynext[n]
+                        out[at + 1] = ybefore[n]
+                    elif k < 7:
+                        out[at] = jnp.where(row < 4, ynext[n], ybefore[n])
+            for half in range(2):
                 for t in range(4):
-                    out[main_tile(f, k, t)] = main[f, x, pl.ds(8 * t, 8)]
-                n, at = f * 8 + x, y_tile(f, k)
-                if k < 3:
-                    out[at] = ynext[n]
-                    out[at + 1] = ybefore[n]
-                elif k < 7:
-                    out[at] = jnp.where(row < 4, ynext[n], ybefore[n])
-        for half in range(2):
-            for t in range(4):
-                out[118 + half * 4 + t] = zbefore[half, pl.ds(8 * t, 8)]
-                out[126 + half * 4 + t] = znext[half, pl.ds(8 * t, 8)]
-        out[134:138] = ynext[24:28]
-        out[138:142] = ybefore[24:28]
+                    out[118 + half * 4 + t] = zbefore[half, pl.ds(8 * t, 8)]
+                    out[126 + half * 4 + t] = znext[half, pl.ds(8 * t, 8)]
+            out[134:138] = ynext[24:28]
+            out[138:142] = ybefore[24:28]
+
+    by_parity(px, xa, xb, body)
 
 
 def coarsen_matrix(source):
@@ -184,7 +205,7 @@
     return jnp.where(source(rows) == cols, 0.5, 0.0).astype(F32)
 
 
-def descend_kernel(main, zbefore, znext, ybefore, ynext, before, after, fa, src, inv, one_out, to_next, to_before,
+def descend_kernel(px, main, zbefore, znext, ybefore, ynext, xa, xb, fa, src, inv, one_out, to_next, to_before,
                    fb, upd, mass, pair):
     lane = lanes_like((8, 128))
     row = rows_like((8, 128))
@@ -211,30 +232,34 @@
             centre = zero
         return centre, message[corner + half], message[corner + 2 + half]
 
-    for plane in range(24):
-        x = plane % 8
-        for h in range(2):
-            for field in (fa, fb):
-                field[plane, h, pl.ds(0, 8)] = zero
-                field[plane, h, pl.ds(56, 8)] = zero
-        for f in range(3 if 0 < plane < 23 else 1):
-            at = (f % 2) * 64 + 8 * x
-            for t in range(6):
-                if plane < 8:
-                    centre, zb, zn = far_tile(before, f, 7 - x, t)
-                elif plane < 16:
-                    centre, zb, zn = own_tile(f, x, t)
-                else:
-                    centre, zb, zn = far_tile(after, f, x, t)
-                side = jnp.where(lane < 8, turn(zn, -at, 1), 0.0)
-                side = jnp.where(lane >= 120, turn(zb, 120 - at, 1), side)
-                if f == 2:
-                    if 8 <= plane < 16 and 1 <= t < 5:
-                        mass[x, pl.ds(8 * t - 8, 8)] = centre
-                    centre, side = inverse(centre), inverse(side)
-                dest, down = ((fa, 8), (src, 0), (inv, 0))[f]
-                dest[plane, 0, pl.ds(8 * t + down, 8)] = centre
-                dest[plane, 1, pl.ds(8 * t + down, 8)] = side
+    def fill(planes, tile_of):
+        for plane in planes:
+            x = plane % 8
+            for h in range(2):
+                for field in (fa, fb):
+                    field[plane, h, pl.ds(0, 8)] = zero
+                    field[plane, h, pl.ds(56, 8)] = zero
+            for f in range(3 if 0 < plane < 23 else 1):
+                at = (f % 2) * 64 + 8 * x
+                for t in range(6):
+                    centre, zb, zn = tile_of(f, x, t)
+                    side = jnp.where(lane < 8, turn(zn, -at, 1), 0.0)
+                    side = jnp.where(lane >= 120, turn(zb, 120 - at, 1), side)
+                    if f == 2:
+                        if 8 <= plane < 16 and 1 <= t < 5:
+                            mass[x, pl.ds(8 * t - 8, 8)] = centre
+                        centre, side = inverse(centre), inverse(side)
+                    dest, down = ((fa, 8), (src, 0), (inv, 0))[f]
+                    dest[plane, 0, pl.ds(8 * t + down, 8)] = centre
+                    dest[plane, 1, pl.ds(8 * t + down, 8)] = side
+
+    fill(range(8, 16), own_tile)
+
+    def fill_far(after, before):
+        fill(range(8), lambda f, x, t: far_tile(before, f, 7 - x, t))
+        fill(range(16, 24), lambda f, x, t: far_tile(after, f, x, t))
+
+    by_parity(px, xa, xb, fill_far)
     xin, xout = fa, fb
     for k, (a, c) in enumerate(factors(SMOOTH_DEG, *SMOOTH)):
         sweep(xin, xout, upd, src, inv, k + 1, 23 - k, a, c, 2, False)
@@ -272,27 +297,34 @@
             out[0, f, i] = jnp.where(lane // 32 == 3, turn(zbefore[f], 96 - 32 * i, 1), v)
 
 
-def rows_kernel(near, to_next, to_before):
-    for start, extra, out in ((8, 7, to_next), (0, 8, to_before)):
+def rows_kernel(py, near, ya, yb):
+    def body(to_next, to_before):
+        for start, extra, out in ((8, 7, to_next), (0, 8, to_before)):
+            for n in range(32):
+                block = near.at[n // 4 % 4, n // 16, n % 4]
+                out[n] = block[pl.ds(start, 8)]
+                out[32 + n // 8, pl.ds(n % 8, 1)] = block[pl.ds(extra, 1)]
+
+    by_parity(py, ya, yb, body)
+
+
+def join_kernel(py, near, ya, yb, out):
+    row = rows_like((8, 128))
+
+    def body(ynext, ybefore):
         for n in range(32):
-            block = near.at[n // 4 % 4, n // 16, n % 4]
-            out[n] = block[pl.ds(start, 8)]
-            out[32 + n // 8, pl.ds(n % 8, 1)] = block[pl.ds(extra, 1)]
-
-
-def join_kernel(near, ybefore, ynext, out):
-    row = rows_like((8, 128))
-    for n in range(32):
-        place = n // 4 % 4, n // 16, n % 4
-        tile, at = 32 + n // 8, pl.ds(n % 8, 1)
-        out[(*place, pl.ds(0, 16))] = near[place]
-        out[(*place, pl.ds(16, 8))] = ynext[n]
-        mix = jnp.where(row == 0, ynext[tile, at], 0.0)
-        out[(*place, pl.ds(24, 8))] = jnp.where(row == 7, ybefore[tile, at], mix)
-        out[(*place, pl.ds(32, 8))] = ybefore[n]
-
-
-def middle_kernel(place, near, far, fb, src, inv, two_out, to_next, to_before,
+            place = n // 4 % 4, n // 16, n % 4
+            tile, at = 32 + n // 8, pl.ds(n % 8, 1)
+            out[(*place, pl.ds(0, 16))] = near[place]
+            out[(*place, pl.ds(16, 8))] = ynext[n]
+            mix = jnp.where(row == 0, ynext[tile, at], 0.0)
+            out[(*place, pl.ds(24, 8))] = jnp.where(row == 7, ybefore[tile, at], mix)
+            out[(*place, pl.ds(32, 8))] = ybefore[n]
+
+    by_parity(py, ya, yb, body)
+
+
+def middle_kernel(place, py, near, far, fb, src, inv, two_out, ya, yb,
                   fa, upd, mass, pair, pairs):
     zero = jnp.zeros((40, 128), F32)
     for end in (0, 1, 2, 3, 4, 5, 6, 39, 40, 41, 42, 43, 44, 45, 46):
@@ -342,14 +374,17 @@
         low = pairs[pl.ds(16 * f, 8)].reshape(192, 128)
         high = pairs[pl.ds(16 * f + 8, 8)].reshape(192, 128)
         made = (dot(low, down[0]) + dot(high, down[1])).reshape(8, 24, 128)
-        for i in range(8):
-            n = 8 * f + i
-            two_out[n] = made[i, 0:8]
-            at = pl.ds(2 * (n % 4), 2)
-            to_next[n] = made[i, 0:8]
-            to_before[n] = made[i, 0:8]
-            to_next[16 + n // 4, at] = made[i, 18:20]
-            to_before[16 + n // 4, at] = made[i, 8:10]
+        def body(to_next, to_before):
+            for i in range(8):
+                n = 8 * f + i
+                at = pl.ds(2 * (n % 4), 2)
+                two_out[n] = made[i, 0:8]
+                to_next[n] = made[i, 0:8]
+                to_before[n] = made[i, 0:8]
+                to_next[16 + n // 4, at] = made[i, 18:20]
+                to_before[16 + n // 4, at] = made[i, 8:10]
+
+        by_parity(py, ya, yb, body)
 
 
 def one_hot(shape, axis, source):
@@ -357,25 +392,29 @@
     return jnp.where(at == source, 1.0, 0.0).astype(F32)
 
 
-def ascend_kernel(place, two, before, after, x1, src1, inv1, x0, src0, inv0, out,
+def ascend_kernel(place, py, two, ya, yb, x1, src1, inv1, x0, src0, inv0, out,
                   ca, cb, cupd, csrc, cinv, flat, oa, ob, oupd, za, zb, zupd):
     row = rows_like((8, 128))
     lane = lanes_like((32, 128))
     (_, scale), *later = factors(COARSE_DEG, *COARSE)
-    for i in range(8):
-        values = []
-        for f in range(2):
-            n = 8 * f + i
-            mix = jnp.where(row < 2, turn(after[16 + n // 4], -2 * (n % 4), 0), 0.0)
-            mix = jnp.where(row >= 6, turn(before[16 + n // 4], 6 - 2 * (n % 4), 0), mix)
-            values.append(jnp.concatenate([two[n], after[n], mix, before[n]], axis=0))
-        values[1] = inverse(values[1])
-        csrc[1 + i, 0] = values[0]
-        cinv[1 + i, 0] = values[1]
-        u = scale * (values[0] * values[1])
-        cupd[1 + i, 0] = u
-        for t in range(4):
-            put(ca, 1 + i, 0, 8 * t, u[8 * t:8 * t + 8], 32, True)
+
+    def fill(after, before):
+        for i in range(8):
+            values = []
+            for f in range(2):
+                n = 8 * f + i
+                mix = jnp.where(row < 2, turn(after[16 + n // 4], -2 * (n % 4), 0), 0.0)
+                mix = jnp.where(row >= 6, turn(before[16 + n // 4], 6 - 2 * (n % 4), 0), mix)
+                values.append(jnp.concatenate([two[n], after[n], mix, before[n]], axis=0))
+            values[1] = inverse(values[1])
+            csrc[1 + i, 0] = values[0]
+            cinv[1 + i, 0] = values[1]
+            u = scale * (values[0] * values[1])
+            cupd[1 + i, 0] = u
+            for t in range(4):
+                put(ca, 1 + i, 0, 8 * t, u[8 * t:8 * t + 8], 32, True)
+
+    by_parity(py, ya, yb, fill)
     xin, xout = ca, cb
     core = pl.ds(8, 32)
     for a, c in later:
@@ -451,45 +490,58 @@
     return lax.ppermute(value, axis, [(i, i ^ bit) for i in range(lax.axis_size(axis))])
 
 
+def swap_both(a, b, axis):
+    count = lax.axis_size(axis)
+    got = []
+    for value, first in ((a, 1), (b, 0)):
+        ups = [(i, i + 1) for i in range(first, count - 1, 2)]
+        got.append(lax.ppermute(value, axis, ups + [(j, i) for i, j in ups]))
+    return got
+
+
 def per_device(right_side, predicted, zone, zone_table):
-    place = lax.axis_index("gx").astype(jnp.int32).reshape(1)
+    px = lax.axis_index("gx").astype(jnp.int32).reshape(1)
+    py = lax.axis_index("gy").astype(jnp.int32).reshape(1)
+    one_scalar, two_scalars = [pltpu.SMEM], [pltpu.SMEM] * 2
     block = (8, 32, 128)
     main, nxt, bef = call(first_kernel, [(3, *block), (2, 32, 128), (2, 32, 128)],
                           [pltpu.VMEM(block, jnp.int32), pltpu.SemaphoreType.DMA((3,))],
                           zone_table, predicted, right_side, zone,
                           spaces=[pltpu.SMEM, pltpu.HBM, pltpu.HBM, pltpu.HBM], limit=56)
     zbefore, znext = shift(nxt, "gz", 1), shift(bef, "gz", -1)
-    nxt, bef = call(second_kernel, [(28, 8, 128)] * 2, [], main, zbefore, znext)
-    ybefore, ynext = shift(nxt, "gy", 1), shift(bef, "gy", -1)
-    nxt, bef = call(third_kernel, [(TILES, 8, 128)] * 2, [], main, zbefore, znext, ybefore, ynext)
-    before, after = shift(nxt, "gx", 1), shift(bef, "gx", -1)
+    ya, yb, main = call(second_kernel, [(28, 8, 128)] * 2 + [(3, *block)], [],
+                        py, main, zbefore, znext, spaces=one_scalar)
+    ya, yb = swap_both(ya, yb, "gy")
+    xa, xb, ybefore, ynext = call(third_kernel, [(TILES, 8, 128)] * 2 + [(28, 8, 128)] * 2, [],
+                                  px, py, main, zbefore, znext, ya, yb, spaces=two_scalars)
+    xa, xb = swap_both(xa, xb, "gx")
     tall, flat = (24, 2, 64, 128), (24, 2, 48, 128)
     x0, src0, inv0, one, nxt, bef = call(
         descend_kernel,
         [tall, flat, flat, (2, 4, 16, 128), (2, 16, 128), (2, 16, 128)],
         [tall, flat, block, block],
-        main, zbefore, znext, ybefore, ynext, before, after)
+        px, main, zbefore, znext, ybefore, ynext, xa, xb, spaces=one_scalar)
     zbefore, znext = shift(nxt, "gz", 1), shift(bef, "gz", -1)
     near, = call(widen_kernel, [(1, 2, 4, 16, 128)], [], one, zbefore, znext)
     near = jnp.concatenate([near, swap(near, "gx", 4)])
     near = jnp.concatenate([near, swap(near, "gx", 2)])
-    nxt, bef = call(rows_kernel, [(36, 8, 128)] * 2, [], near)
-    ybefore, ynext = shift(nxt, "gy", 1), shift(bef, "gy", -1)
-    near, = call(join_kernel, [(4, 2, 4, 40, 128)], [], near, ybefore, ynext)
+    ya, yb = call(rows_kernel, [(36, 8, 128)] * 2, [], py, near, spaces=one_scalar)
+    ya, yb = swap_both(ya, yb, "gy")
+    near, = call(join_kernel, [(4, 2, 4, 40, 128)], [], py, near, ya, yb, spaces=one_scalar)
     far = swap(near, "gx", 1)
     tall, flat = (47, 1, 56, 128), (47, 1, 40, 128)
-    x1, src1, inv1, two, nxt, bef = call(
+    x1, src1, inv1, two, ya, yb = call(
         middle_kernel,
         [tall, flat, flat, (16, 8, 128), (20, 8, 128), (20, 8, 128)],
         [tall, flat, (47, 40, 128), (32, 40, 128), (32, 24, 128)],
-        place, near, far, spaces=[pltpu.SMEM])
-    before, after = shift(nxt, "gy", 1), shift(bef, "gy", -1)
+        px, py, near, far, spaces=two_scalars)
+    ya, yb = swap_both(ya, yb, "gy")
     out, = call(
         ascend_kernel,
         [(8, 32, 128)],
         [(10, 1, 48, 128)] * 2 + [(10, 1, 32, 128)] * 3 + [(22, 32, 128)]
         + [(16, 1, 56, 128)] * 2 + [(16, 1, 40, 128)] + [(16, 2, 64, 128)] * 2 + [(16, 2, 48, 128)],
-        place, two, before, after, x1, src1, inv1, x0, src0, inv0, spaces=[pltpu.SMEM])
+        px, py, two, ya, yb, x1, src1, inv1, x0, src0, inv0, spaces=two_scalars)
     return out
 
 

time: 127 us -> 122 us (0.961)
  the two profiles are of different devices: /device:TPU:14 before, /device:TPU:56 now
where the time goes in v2:
time: 122 us
  starting transfers between devices  51.4 us (42%)
  waiting for transfers between devices  47.5 us (39%)
  Pallas kernels  21.8 us (18%)
    ppermute x8, starting transfers between devices, swap_both(): got.append(lax.ppermute(value, axis, ups + [(j, i) for i, j in ups]))  24.3 us
    pallas_call x9, Pallas kernels, call(): pl.pallas_call(kernel, out_shape=[jax.ShapeDtypeStruct(s, F32) for s in o...  21.8 us
    ppermute x4, starting transfers between devices, shift(): return lax.ppermute(value, axis, pairs)  19.8 us
    ppermute x8, waiting for transfers between devices, swap_both(): got.append(lax.ppermute(value, axis, ups + [(j, i) for i, j in ups]))  19.6 us
    ppermute x4, waiting for transfers between devices, shift(): return lax.ppermute(value, axis, pairs)  17.2 us
    ppermute x3, waiting for transfers between devices, swap(): lax.ppermute(value, axis, [(i, i ^ bit) for i in range(lax.axis_size(axis...  10.7 us
    ppermute x3, starting transfers between devices, swap(): lax.ppermute(value, axis, [(i, i ^ bit) for i in range(lax.axis_size(axis...  7.22 us
  transfers between devices with their start and end apart: 15, of which 14 were waited for; matrix products, arithmetic and copies ran while one was open for 0% of the time, Pallas kernels for 0%

profile of v2, /device:TPU:56, one launch (start us, length us, event | category | flops | bytes accessed | tf_op | source)
XLA Modules:
  0.0 121.9 jit_solution(840518225860958030)
XLA Ops:
  0.0 2.7 %shard_map.46 = (f32[3,8,32,128]{3,2,1,0:T(8,128)}, f32[2,32,128]{2,1,0:T(8,128)}, f32[2,32,128]{2,1,0:T(8,128)}) custom-call(f32[16]{0:T(128)} %table.1, f32[8,32,128]{2,1,0:T(8,128)} %pred_.1, f32[8,32,128]{2,1,0:T(8,128)} %right.1, s32[8,32,128]{2,1,0:T(8,128)} %zone.1), custom_call_target="tpu_custom_call" | custom-call | tf_op jit(solution)/shard_map/pallas_call | solution.py:473
  2.7 9.1 %collective-permute-start = (f32[2,32,128]{2,1,0:T(8,128)}, f32[2,32,128]{2,1,0:T(8,128)S(1)}, u32[]{:S(2)}, u32[]{:S(2)}) collective-permute-start(f32[2,32,128]{2,1,0:T(8,128)} %get-tuple-element.30), channel_id=1, source_target_pairs={{0,1},{1,2},{2,3},{4,5},{5,6},{6,7},{8,9},{9,10},{10,11},{12,13},{... | collective-permute-start | bytes 98312 | tf_op jit(solution)/shard_map/ppermute | solution.py:486
  13.7 8.4 %collective-permute-done.1.znext = f32[2,32,128]{2,1,0:T(8,128)S(1)} collective-permute-done((f32[2,32,128]{2,1,0:T(8,128)}, f32[2,32,128]{2,1,0:T(8,128)S(1)}, u32[]{:S(2)}, u32[]{:S(2)}) %collective-permute-start.1) | collective-permute-done | bytes 32800 | tf_op jit(solution)/shard_map/ppermute | solution.py:486
  23.1 4.8 %collective-permute-start.2 = (f32[28,8,128]{2,1,0:T(8,128)S(1)}, f32[28,8,128]{2,1,0:T(8,128)S(1)}, u32[]{:S(2)}, u32[]{:S(2)}) collective-permute-start(f32[28,8,128]{2,1,0:T(8,128)S(1)} %get-tuple-element.33), channel_id=1, source_target_pairs={{4,8},{12,16},{20,24},{28,32},{36,40},{44,48},{52,56},{8,4},{16,12... | collective-permute-start | bytes 344072 | tf_op jit(solution)/shard_map/ppermute | solution.py:498
  28.0 1.9 %collective-permute-start.3 = (f32[28,8,128]{2,1,0:T(8,128)S(1)}, f32[28,8,128]{2,1,0:T(8,128)S(1)}, u32[]{:S(2)}, u32[]{:S(2)}) collective-permute-start(f32[28,8,128]{2,1,0:T(8,128)S(1)} %get-tuple-element.34), channel_id=1, source_target_pairs={{0,4},{8,12},{16,20},{24,28},{32,36},{40,44},{48,52},{56,60},{4,0}... | collective-permute-start | bytes 344072 | tf_op jit(solution)/shard_map/ppermute | solution.py:498
  30.0 2.0 %collective-permute-done.2.ya = f32[28,8,128]{2,1,0:T(8,128)S(1)} collective-permute-done((f32[28,8,128]{2,1,0:T(8,128)S(1)}, f32[28,8,128]{2,1,0:T(8,128)S(1)}, u32[]{:S(2)}, u32[]{:S(2)}) %collective-permute-start.2) | collective-permute-done | bytes 114720 | tf_op jit(solution)/shard_map/ppermute | solution.py:498
  31.9 2.7 %collective-permute-done.3.yb = f32[28,8,128]{2,1,0:T(8,128)S(1)} collective-permute-done((f32[28,8,128]{2,1,0:T(8,128)S(1)}, f32[28,8,128]{2,1,0:T(8,128)S(1)}, u32[]{:S(2)}, u32[]{:S(2)}) %collective-permute-start.3) | collective-permute-done | bytes 114720 | tf_op jit(solution)/shard_map/ppermute | solution.py:498
  34.8 1.9 %collective-permute-start.4 = (f32[142,8,128]{2,1,0:T(8,128)S(1)}, f32[142,8,128]{2,1,0:T(8,128)S(1)}, u32[]{:S(2)}, u32[]{:S(2)}) collective-permute-start(f32[142,8,128]{2,1,0:T(8,128)S(1)} %get-tuple-element.37), channel_id=1, source_target_pairs={{64,128},{192,256},{320,384},{128,64},{256,192},{384,320},{65,129}... | collective-permute-start | bytes 1744904 | tf_op jit(solution)/shard_map/ppermute | solution.py:498
  36.7 3.8 %collective-permute-start.5 = (f32[142,8,128]{2,1,0:T(8,128)S(1)}, f32[142,8,128]{2,1,0:T(8,128)S(1)}, u32[]{:S(2)}, u32[]{:S(2)}) collective-permute-start(f32[142,8,128]{2,1,0:T(8,128)S(1)} %get-tuple-element.38), channel_id=1, source_target_pairs={{0,64},{128,192},{256,320},{384,448},{64,0},{192,128},{320,256},{4... | collective-permute-start | bytes 1744904 | tf_op jit(solution)/shard_map/ppermute | solution.py:498
  40.6 5.3 %collective-permute-done.4.xa = f32[142,8,128]{2,1,0:T(8,128)S(1)} collective-permute-done((f32[142,8,128]{2,1,0:T(8,128)S(1)}, f32[142,8,128]{2,1,0:T(8,128)S(1)}, u32[]{:S(2)}, u32[]{:S(2)}) %collective-permute-start.4) | collective-permute-done | bytes 581664 | tf_op jit(solution)/shard_map/ppermute | solution.py:498
  45.9 6.7 %shard_map.49 = (f32[24,2,64,128]{3,2,1,0:T(8,128)S(1)}, f32[24,2,48,128]{3,2,1,0:T(8,128)S(1)}, f32[24,2,48,128]{3,2,1,0:T(8,128)S(1)}, f32[2,4,16,128]{3,2,1,0...) custom-call(s32[1]{0:T(128)} %bitcast.px.place, f32[3,8,32,128]{3,2,1,0:T(8,128)S(1)} %get-tuple-element.32.main, ...), custom_call_target="tpu_custom_call" | custom-call | tf_op jit(solution)/shard_map/pallas_call | solution.py:473
  52.6 8.1 %collective-permute-start.6 = (f32[2,16,128]{2,1,0:T(8,128)S(1)}, f32[2,16,128]{2,1,0:T(8,128)S(1)}, u32[]{:S(2)}, u32[]{:S(2)}) collective-permute-start(f32[2,16,128]{2,1,0:T(8,128)S(1)} %get-tuple-element.40), channel_id=1, source_target_pairs={{0,1},{1,2},{2,3},{4,5},{5,6},{6,7},{8,9},{9,10},{10,11},{12,13},{... | collective-permute-start | bytes 49160 | tf_op jit(solution)/shard_map/ppermute | solution.py:486
  62.1 8.1 %collective-permute-done.7.znext = f32[2,16,128]{2,1,0:T(8,128)S(1)} collective-permute-done((f32[2,16,128]{2,1,0:T(8,128)S(1)}, f32[2,16,128]{2,1,0:T(8,128)S(1)}, u32[]{:S(2)}, u32[]{:S(2)}) %collective-permute-start.7) | collective-permute-done | bytes 16416 | tf_op jit(solution)/shard_map/ppermute | solution.py:486
  70.3 3.4 %collective-permute-start.8 = (f32[1,2,4,16,128]{4,3,2,1,0:T(8,128)S(1)}, f32[1,2,4,16,128]{4,3,2,1,0:T(8,128)S(1)}, u32[]{:S(2)}, u32[]{:S(2)}) collective-permute-start(f32[1,2,4,16,128]{4,3,2,1,0:T(8,128)S(1)} %shard_map.50), channel_id=1, source_target_pairs={{0,256},{64,320},{128,384},{192,448},{256,0},{320,64},{384,128},{4... | collective-permute-start | bytes 196616 | tf_op jit(solution)/shard_map/ppermute | solution.py:490
  73.7 3.7 %collective-permute-done.8 = f32[1,2,4,16,128]{4,3,2,1,0:T(8,128)S(1)} collective-permute-done((f32[1,2,4,16,128]{4,3,2,1,0:T(8,128)S(1)}, f32[1,2,4,16,128]{4,3,2,1,0:T(8,128)S(1)}, u32[]{:S(2)}, u32[]{:S(2)}) %collective-permute-start.8) | collective-permute-done | bytes 65568 | tf_op jit(solution)/shard_map/ppermute | solution.py:490
  79.4 4.9 %collective-permute-done.9 = f32[2,2,4,16,128]{4,3,2,1,0:T(8,128)S(1)} collective-permute-done((f32[2,2,4,16,128]{4,3,2,1,0:T(8,128)S(1)}, f32[2,2,4,16,128]{4,3,2,1,0:T(8,128)S(1)}, u32[]{:S(2)}, u32[]{:S(2)}) %collective-permute-start.9) | collective-permute-done | bytes 131104 | tf_op jit(solution)/shard_map/ppermute | solution.py:490
  84.4 3.1 %collective-permute-start.10 = (f32[36,8,128]{2,1,0:T(8,128)S(1)}, f32[36,8,128]{2,1,0:T(8,128)S(1)}, u32[]{:S(2)}, u32[]{:S(2)}) collective-permute-start(f32[36,8,128]{2,1,0:T(8,128)S(1)} %get-tuple-element.42), channel_id=1, source_target_pairs={{4,8},{12,16},{20,24},{28,32},{36,40},{44,48},{52,56},{8,4},{16,12... | collective-permute-start | bytes 442376 | tf_op jit(solution)/shard_map/ppermute | solution.py:498
  89.4 4.1 %collective-permute-done.10.ya = f32[36,8,128]{2,1,0:T(8,128)S(1)} collective-permute-done((f32[36,8,128]{2,1,0:T(8,128)S(1)}, f32[36,8,128]{2,1,0:T(8,128)S(1)}, u32[]{:S(2)}, u32[]{:S(2)}) %collective-permute-start.10) | collective-permute-done | bytes 147488 | tf_op jit(solution)/shard_map/ppermute | solution.py:498
  96.5 2.1 %collective-permute-done.12.far = f32[4,2,4,40,128]{4,3,2,1,0:T(8,128)S(1)} collective-permute-done((f32[4,2,4,40,128]{4,3,2,1,0:T(8,128)S(1)}, f32[4,2,4,40,128]{4,3,2,1,0:T(8,128)S(1)}, u32[]{:S(2)}, u32[]{:S(2)}) %collective-permute-start.12) | collective-permute-done | bytes 655392 | tf_op jit(solution)/shard_map/ppermute | solution.py:490
  98.6 5.1 %shard_map.53 = (f32[47,1,56,128]{3,2,1,0:T(8,128)S(1)}, f32[47,1,40,128]{3,2,1,0:T(8,128)S(1)}, f32[47,1,40,128]{3,2,1,0:T(8,128)S(1)}, f32[16,8,128]{2,1,0:T(8...) custom-call(s32[1]{0:T(128)} %bitcast.px.place, s32[1]{0:T(128)} %bitcast.1.py, ...), custom_call_target="tpu_custom_call" | custom-call | tf_op jit(solution)/shard_map/pallas_call | solution.py:473
  103.7 4.8 %collective-permute-start.13 = (f32[20,8,128]{2,1,0:T(8,128)S(1)}, f32[20,8,128]{2,1,0:T(8,128)S(1)}, u32[]{:S(2)}, u32[]{:S(2)}) collective-permute-start(f32[20,8,128]{2,1,0:T(8,128)S(1)} %get-tuple-element.45), channel_id=1, source_target_pairs={{4,8},{12,16},{20,24},{28,32},{36,40},{44,48},{52,56},{8,4},{16,12... | collective-permute-start | bytes 245768 | tf_op jit(solution)/shard_map/ppermute | solution.py:498
  108.6 1.9 %collective-permute-start.14 = (f32[20,8,128]{2,1,0:T(8,128)S(1)}, f32[20,8,128]{2,1,0:T(8,128)S(1)}, u32[]{:S(2)}, u32[]{:S(2)}) collective-permute-start(f32[20,8,128]{2,1,0:T(8,128)S(1)} %get-tuple-element.46), channel_id=1, source_target_pairs={{0,4},{8,12},{16,20},{24,28},{32,36},{40,44},{48,52},{56,60},{4,0}... | collective-permute-start | bytes 245768 | tf_op jit(solution)/shard_map/ppermute | solution.py:498
  112.2 2.7 %collective-permute-done.14.yb = f32[20,8,128]{2,1,0:T(8,128)S(1)} collective-permute-done((f32[20,8,128]{2,1,0:T(8,128)S(1)}, f32[20,8,128]{2,1,0:T(8,128)S(1)}, u32[]{:S(2)}, u32[]{:S(2)}) %collective-permute-start.14) | collective-permute-done | bytes 81952 | tf_op jit(solution)/shard_map/ppermute | solution.py:498
  114.9 7.0 %shard_map.54 = f32[8,32,128]{2,1,0:T(8,128)} custom-call(s32[1]{0:T(128)} %bitcast.px.place, s32[1]{0:T(128)} %bitcast.1.py, f32[16,8,128]{2,1,0:T(8,128)S(1)} %get-tuple-element.44.two, f32[20,8,128]{2,1,0:T(8,128)S(1)} %collective-permute-done.13.ya, f32[20,8,128]{2,1,0:T(8,128)S(1)} %collective-permute-done.14.yb, ...), custom_call_target="tpu_custom_call" | custom-call | tf_op jit(solution)/shard_map/pallas_call | solution.py:473
  (19 shorter events, 13.1 us)
Async XLA Ops:
  2.7 11.0 %collective-permute-start = (f32[2,32,128]{2,1,0:T(8,128)}, f32[2,32,128]{2,1,0:T(8,128)S(1)}, u32[]{:S(2)}, u32[]{:S(2)}) collective-permute-start(f32[2,32,128]{2,1,0:T(8,128)} %get-tuple-element.30), channel_id=1, source_target_pairs={{0,1},{1,2},{2,3},{4,5},{5,6},{6,7},{8,9},{9,10},{10,11},{12,13},{... | collective-permute-start | bytes 98312 | tf_op jit(solution)/shard_map/ppermute | solution.py:486
  11.8 10.3 %collective-permute-start.1 = (f32[2,32,128]{2,1,0:T(8,128)}, f32[2,32,128]{2,1,0:T(8,128)S(1)}, u32[]{:S(2)}, u32[]{:S(2)}) collective-permute-start(f32[2,32,128]{2,1,0:T(8,128)} %get-tuple-element.31), channel_id=1, source_target_pairs={{1,0},{2,1},{3,2},{5,4},{6,5},{7,6},{9,8},{10,9},{11,10},{13,12},{... | collective-permute-start | bytes 98312 | tf_op jit(solution)/shard_map/ppermute | solution.py:486
  22.1 1.0 copy-start
  23.1 8.8 %collective-permute-start.2 = (f32[28,8,128]{2,1,0:T(8,128)S(1)}, f32[28,8,128]{2,1,0:T(8,128)S(1)}, u32[]{:S(2)}, u32[]{:S(2)}) collective-permute-start(f32[28,8,128]{2,1,0:T(8,128)S(1)} %get-tuple-element.33), channel_id=1, source_target_pairs={{4,8},{12,16},{20,24},{28,32},{36,40},{44,48},{52,56},{8,4},{16,12... | collective-permute-start | bytes 344072 | tf_op jit(solution)/shard_map/ppermute | solution.py:498
  28.0 6.7 %collective-permute-start.3 = (f32[28,8,128]{2,1,0:T(8,128)S(1)}, f32[28,8,128]{2,1,0:T(8,128)S(1)}, u32[]{:S(2)}, u32[]{:S(2)}) collective-permute-start(f32[28,8,128]{2,1,0:T(8,128)S(1)} %get-tuple-element.34), channel_id=1, source_target_pairs={{0,4},{8,12},{16,20},{24,28},{32,36},{40,44},{48,52},{56,60},{4,0}... | collective-permute-start | bytes 344072 | tf_op jit(solution)/shard_map/ppermute | solution.py:498
  34.8 11.1 %collective-permute-start.4 = (f32[142,8,128]{2,1,0:T(8,128)S(1)}, f32[142,8,128]{2,1,0:T(8,128)S(1)}, u32[]{:S(2)}, u32[]{:S(2)}) collective-permute-start(f32[142,8,128]{2,1,0:T(8,128)S(1)} %get-tuple-element.37), channel_id=1, source_target_pairs={{64,128},{192,256},{320,384},{128,64},{256,192},{384,320},{65,129}... | collective-permute-start | bytes 1744904 | tf_op jit(solution)/shard_map/ppermute | solution.py:498
  36.7 9.2 %collective-permute-start.5 = (f32[142,8,128]{2,1,0:T(8,128)S(1)}, f32[142,8,128]{2,1,0:T(8,128)S(1)}, u32[]{:S(2)}, u32[]{:S(2)}) collective-permute-start(f32[142,8,128]{2,1,0:T(8,128)S(1)} %get-tuple-element.38), channel_id=1, source_target_pairs={{0,64},{128,192},{256,320},{384,448},{64,0},{192,128},{320,256},{4... | collective-permute-start | bytes 1744904 | tf_op jit(solution)/shard_map/ppermute | solution.py:498
  52.6 9.6 %collective-permute-start.6 = (f32[2,16,128]{2,1,0:T(8,128)S(1)}, f32[2,16,128]{2,1,0:T(8,128)S(1)}, u32[]{:S(2)}, u32[]{:S(2)}) collective-permute-start(f32[2,16,128]{2,1,0:T(8,128)S(1)} %get-tuple-element.40), channel_id=1, source_target_pairs={{0,1},{1,2},{2,3},{4,5},{5,6},{6,7},{8,9},{9,10},{10,11},{12,13},{... | collective-permute-start | bytes 49160 | tf_op jit(solution)/shard_map/ppermute | solution.py:486
  60.7 9.5 %collective-permute-start.7 = (f32[2,16,128]{2,1,0:T(8,128)S(1)}, f32[2,16,128]{2,1,0:T(8,128)S(1)}, u32[]{:S(2)}, u32[]{:S(2)}) collective-permute-start(f32[2,16,128]{2,1,0:T(8,128)S(1)} %get-tuple-element.41), channel_id=1, source_target_pairs={{1,0},{2,1},{3,2},{5,4},{6,5},{7,6},{9,8},{10,9},{11,10},{13,12},{... | collective-permute-start | bytes 49160 | tf_op jit(solution)/shard_map/ppermute | solution.py:486
  70.3 7.1 %collective-permute-start.8 = (f32[1,2,4,16,128]{4,3,2,1,0:T(8,128)S(1)}, f32[1,2,4,16,128]{4,3,2,1,0:T(8,128)S(1)}, u32[]{:S(2)}, u32[]{:S(2)}) collective-permute-start(f32[1,2,4,16,128]{4,3,2,1,0:T(8,128)S(1)} %shard_map.50), channel_id=1, source_target_pairs={{0,256},{64,320},{128,384},{192,448},{256,0},{320,64},{384,128},{4... | collective-permute-start | bytes 196616 | tf_op jit(solution)/shard_map/ppermute | solution.py:490
  77.4 6.9 %collective-permute-start.9 = (f32[2,2,4,16,128]{4,3,2,1,0:T(8,128)S(1)}, f32[2,2,4,16,128]{4,3,2,1,0:T(8,128)S(1)}, u32[]{:S(2)}, u32[]{:S(2)}) collective-permute-start(f32[2,2,4,16,128]{4,3,2,1,0:T(8,128)S(1)} %pad_maximum_fusion.1), channel_id=1, source_target_pairs={{0,128},{64,192},{128,0},{192,64},{256,384},{320,448},{384,256},{4... | collective-permute-start | bytes 393224 | tf_op jit(solution)/shard_map/ppermute | solution.py:490
  84.4 9.1 %collective-permute-start.10 = (f32[36,8,128]{2,1,0:T(8,128)S(1)}, f32[36,8,128]{2,1,0:T(8,128)S(1)}, u32[]{:S(2)}, u32[]{:S(2)}) collective-permute-start(f32[36,8,128]{2,1,0:T(8,128)S(1)} %get-tuple-element.42), channel_id=1, source_target_pairs={{4,8},{12,16},{20,24},{28,32},{36,40},{44,48},{52,56},{8,4},{16,12... | collective-permute-start | bytes 442376 | tf_op jit(solution)/shard_map/ppermute | solution.py:498
  87.5 7.0 %collective-permute-start.11 = (f32[36,8,128]{2,1,0:T(8,128)S(1)}, f32[36,8,128]{2,1,0:T(8,128)S(1)}, u32[]{:S(2)}, u32[]{:S(2)}) collective-permute-start(f32[36,8,128]{2,1,0:T(8,128)S(1)} %get-tuple-element.43), channel_id=1, source_target_pairs={{0,4},{8,12},{16,20},{24,28},{32,36},{40,44},{48,52},{56,60},{4,0}... | collective-permute-start | bytes 442376 | tf_op jit(solution)/shard_map/ppermute | solution.py:498
  94.6 4.0 %collective-permute-start.12 = (f32[4,2,4,40,128]{4,3,2,1,0:T(8,128)S(1)}, f32[4,2,4,40,128]{4,3,2,1,0:T(8,128)S(1)}, u32[]{:S(2)}, u32[]{:S(2)}) collective-permute-start(f32[4,2,4,40,128]{4,3,2,1,0:T(8,128)S(1)} %shard_map.52.near), channel_id=1, source_target_pairs={{0,64},{64,0},{128,192},{192,128},{256,320},{320,256},{384,448},{4... | collective-permute-start | bytes 1966088 | tf_op jit(solution)/shard_map/ppermute | solution.py:490
  103.7 8.5 %collective-permute-start.13 = (f32[20,8,128]{2,1,0:T(8,128)S(1)}, f32[20,8,128]{2,1,0:T(8,128)S(1)}, u32[]{:S(2)}, u32[]{:S(2)}) collective-permute-start(f32[20,8,128]{2,1,0:T(8,128)S(1)} %get-tuple-element.45), channel_id=1, source_target_pairs={{4,8},{12,16},{20,24},{28,32},{36,40},{44,48},{52,56},{8,4},{16,12... | collective-permute-start | bytes 245768 | tf_op jit(solution)/shard_map/ppermute | solution.py:498
  108.6 6.3 %collective-permute-start.14 = (f32[20,8,128]{2,1,0:T(8,128)S(1)}, f32[20,8,128]{2,1,0:T(8,128)S(1)}, u32[]{:S(2)}, u32[]{:S(2)}) collective-permute-start(f32[20,8,128]{2,1,0:T(8,128)S(1)} %get-tuple-element.46), channel_id=1, source_target_pairs={{0,4},{8,12},{16,20},{24,28},{32,36},{40,44},{48,52},{56,60},{4,0}... | collective-permute-start | bytes 245768 | tf_op jit(solution)/shard_map/ppermute | solution.py:498

commit v3 on v2

--- a/solution.py
+++ b/solution.py
@@ -205,7 +205,7 @@
     return jnp.where(source(rows) == cols, 0.5, 0.0).astype(F32)
 
 
-def descend_kernel(px, main, zbefore, znext, ybefore, ynext, xa, xb, fa, src, inv, one_out, to_next, to_before,
+def descend_kernel(px, main, zbefore, znext, ybefore, ynext, xa, xb, fa, src, inv, one_out, give, keep,
                    fb, upd, mass, pair):
     lane = lanes_like((8, 128))
     row = rows_like((8, 128))
@@ -280,21 +280,25 @@
     one = dot(even.reshape(128, 128), coarsen_matrix(lambda r: r // 2)).reshape(2, 4, 16, 128)
     one_out[...] = one
     lane = lanes_like((16, 128))
-    for edge, out in ((32, to_next), (0, to_before)):
-        for f in range(2):
-            packed = jnp.zeros((16, 128), F32)
-            for i in range(4):
-                packed = jnp.where(lane // 32 == i, turn(one[f, i], 32 * i - edge, 1), packed)
-            out[f] = packed
-
-
-def widen_kernel(one, zbefore, znext, out):
+
+    def pack(to_next, to_before):
+        for edge, out in ((32, to_next), (0, to_before)):
+            for f in range(2):
+                packed = jnp.zeros((16, 128), F32)
+                for i in range(4):
+                    packed = jnp.where(lane // 32 == i, turn(one[f, i], 32 * i - edge, 1), packed)
+                out[f] = packed
+
+    by_parity(px, give, keep, pack)
+
+
+def widen_kernel(one, halo, out):
     lane = lanes_like((16, 128))
     for f in range(2):
         for i in range(4):
             v = one[f, i]
-            v = jnp.where(lane // 32 == 2, turn(znext[f], 64 - 32 * i, 1), v)
-            out[0, f, i] = jnp.where(lane // 32 == 3, turn(zbefore[f], 96 - 32 * i, 1), v)
+            v = jnp.where(lane // 32 == 2, turn(halo[0, f], 64 - 32 * i, 1), v)
+            out[0, f, i] = jnp.where(lane // 32 == 3, turn(halo[1, f], 96 - 32 * i, 1), v)
 
 
 def rows_kernel(py, near, ya, yb):
@@ -324,7 +328,7 @@
     by_parity(py, ya, yb, body)
 
 
-def middle_kernel(place, py, near, far, fb, src, inv, two_out, ya, yb,
+def middle_kernel(place, near, far, fb, src, inv, two_out, edge_out,
                   fa, upd, mass, pair, pairs):
     zero = jnp.zeros((40, 128), F32)
     for end in (0, 1, 2, 3, 4, 5, 6, 39, 40, 41, 42, 43, 44, 45, 46):
@@ -333,19 +337,30 @@
         src[end, 0] = zero
         inv[end, 0] = zero
     (_, scale), *later = factors(SMOOTH_DEG, *SMOOTH)
-    for j in range(8):
-        group = place[0] ^ ((j & 1) * 4 + (j >> 1 & 1) * 2 + (j >> 2))
-        for i in range(4):
-            plane = 7 + 4 * group + i
-            values = [(near if j < 4 else far)[j % 4, f, i] for f in range(2)]
-            mass[plane] = values[1]
-            values[1] = inverse(values[1])
-            src[plane, 0] = values[0]
-            inv[plane, 0] = values[1]
-            u = scale * (values[0] * values[1])
-            upd[plane, 0] = u
-            for t in range(5):
-                put(fa, plane, 0, 8 * t, u[8 * t:8 * t + 8], 40, True)
+    lane = lanes_like((40, 128))
+
+    def fill(first, second):
+        for j in range(4):
+            group = (place[0] // 2 * 2) ^ ((j & 1) * 4 + (j >> 1) * 2)
+            for i in range(4):
+                pairs = []
+                for f in range(2):
+                    p, q = first[j, f, i], second[j, f, i]
+                    v = jnp.where(lane < 96, turn(q, -32, 1), turn(p, 32, 1))
+                    pairs.append((jnp.where(lane < 64, p, v), jnp.where(lane < 96, q, p)))
+                for core in range(2):
+                    plane = 7 + 4 * group + 4 * core + i
+                    b1, m1 = pairs[0][core], pairs[1][core]
+                    inv1 = inverse(m1)
+                    mass[plane] = m1
+                    src[plane, 0] = b1
+                    inv[plane, 0] = inv1
+                    u = scale * (b1 * inv1)
+                    upd[plane, 0] = u
+                    for t in range(5):
+                        put(fa, plane, 0, 8 * t, u[8 * t:8 * t + 8], 40, True)
+
+    by_parity(place, far, near, fill)
     xin, xout = fa, fb
     for a, c in later:
         sweep(xin, xout, upd, src, inv, 7, 39, a, c, 4, True)
@@ -374,17 +389,12 @@
         low = pairs[pl.ds(16 * f, 8)].reshape(192, 128)
         high = pairs[pl.ds(16 * f + 8, 8)].reshape(192, 128)
         made = (dot(low, down[0]) + dot(high, down[1])).reshape(8, 24, 128)
-        def body(to_next, to_before):
-            for i in range(8):
-                n = 8 * f + i
-                at = pl.ds(2 * (n % 4), 2)
-                two_out[n] = made[i, 0:8]
-                to_next[n] = made[i, 0:8]
-                to_before[n] = made[i, 0:8]
-                to_next[16 + n // 4, at] = made[i, 18:20]
-                to_before[16 + n // 4, at] = made[i, 8:10]
-
-        by_parity(py, ya, yb, body)
+        for i in range(8):
+            n = 8 * f + i
+            two_out[n] = made[i, 0:8]
+            edge_out[n] = made[i, 0:8]
+            beyond = jnp.where(place[0] % 2 == 0, made[i, 18:20], made[i, 8:10])
+            edge_out[16 + n // 4, pl.ds(2 * (n % 4), 2)] = beyond
 
 
 def one_hot(shape, axis, source):
@@ -392,7 +402,7 @@
     return jnp.where(at == source, 1.0, 0.0).astype(F32)
 
 
-def ascend_kernel(place, py, two, ya, yb, x1, src1, inv1, x0, src0, inv0, out,
+def ascend_kernel(place, two, brought, given, x1, src1, inv1, x0, src0, inv0, out,
                   ca, cb, cupd, csrc, cinv, flat, oa, ob, oupd, za, zb, zupd):
     row = rows_like((8, 128))
     lane = lanes_like((32, 128))
@@ -414,7 +424,7 @@
             for t in range(4):
                 put(ca, 1 + i, 0, 8 * t, u[8 * t:8 * t + 8], 32, True)
 
-    by_parity(py, ya, yb, fill)
+    by_parity(place, brought, given, fill)
     xin, xout = ca, cb
     core = pl.ds(8, 32)
     for a, c in later:
@@ -499,6 +509,15 @@
     return got
 
 
+def cross(value, axis):
+    count = lax.axis_size(axis)
+    pairs = []
+    for g in range(lax.axis_size("gx")):
+        by = 1 - 2 * (g % 2)
+        pairs += [(g * count + i, g * count + i + by) for i in range(count) if 0 <= i + by < count]
+    return lax.ppermute(value, ("gx", axis), pairs)
+
+
 def per_device(right_side, predicted, zone, zone_table):
     px = lax.axis_index("gx").astype(jnp.int32).reshape(1)
     py = lax.axis_index("gy").astype(jnp.int32).reshape(1)
@@ -516,13 +535,13 @@
                                   px, py, main, zbefore, znext, ya, yb, spaces=two_scalars)
     xa, xb = swap_both(xa, xb, "gx")
     tall, flat = (24, 2, 64, 128), (24, 2, 48, 128)
-    x0, src0, inv0, one, nxt, bef = call(
+    x0, src0, inv0, one, give, keep = call(
         descend_kernel,
         [tall, flat, flat, (2, 4, 16, 128), (2, 16, 128), (2, 16, 128)],
         [tall, flat, block, block],
         px, main, zbefore, znext, ybefore, ynext, xa, xb, spaces=one_scalar)
-    zbefore, znext = shift(nxt, "gz", 1), shift(bef, "gz", -1)
-    near, = call(widen_kernel, [(1, 2, 4, 16, 128)], [], one, zbefore, znext)
+    halo = cross(jnp.stack([keep, swap(give, "gx", 1)]), "gz")
+    near, = call(widen_kernel, [(1, 2, 4, 16, 128)], [], one, halo)
     near = jnp.concatenate([near, swap(near, "gx", 4)])
     near = jnp.concatenate([near, swap(near, "gx", 2)])
     ya, yb = call(rows_kernel, [(36, 8, 128)] * 2, [], py, near, spaces=one_scalar)
@@ -530,18 +549,19 @@
     near, = call(join_kernel, [(4, 2, 4, 40, 128)], [], py, near, ya, yb, spaces=one_scalar)
     far = swap(near, "gx", 1)
     tall, flat = (47, 1, 56, 128), (47, 1, 40, 128)
-    x1, src1, inv1, two, ya, yb = call(
+    x1, src1, inv1, two, edge = call(
         middle_kernel,
-        [tall, flat, flat, (16, 8, 128), (20, 8, 128), (20, 8, 128)],
+        [tall, flat, flat, (16, 8, 128), (20, 8, 128)],
         [tall, flat, (47, 40, 128), (32, 40, 128), (32, 24, 128)],
-        px, py, near, far, spaces=two_scalars)
-    ya, yb = swap_both(ya, yb, "gy")
+        px, near, far, spaces=one_scalar)
+    brought = cross(edge, "gy")
+    given = swap(brought, "gx", 1)
     out, = call(
         ascend_kernel,
         [(8, 32, 128)],
         [(10, 1, 48, 128)] * 2 + [(10, 1, 32, 128)] * 3 + [(22, 32, 128)]
         + [(16, 1, 56, 128)] * 2 + [(16, 1, 40, 128)] + [(16, 2, 64, 128)] * 2 + [(16, 2, 48, 128)],
-        px, py, two, ya, yb, x1, src1, inv1, x0, src0, inv0, spaces=two_scalars)
+        px, two, brought, given, x1, src1, inv1, x0, src0, inv0, spaces=one_scalar)
     return out
 
 

time: 122 us -> 118 us (0.967)
  the two profiles are of different devices: /device:TPU:56 before, /device:TPU:17 now
where the time goes in v3:
time: 118 us
  starting transfers between devices  55.8 us (47%)
  waiting for transfers between devices  39.6 us (34%)
  Pallas kernels  21.2 us (18%)
    ppermute x5, starting transfers between devices, swap(): lax.ppermute(value, axis, [(i, i ^ bit) for i in range(lax.axis_size(axis...  21.4 us
    pallas_call x9, Pallas kernels, call(): pl.pallas_call(kernel, out_shape=[jax.ShapeDtypeStruct(s, F32) for s in o...  21.2 us
    ppermute x6, starting transfers between devices, swap_both(): got.append(lax.ppermute(value, axis, ups + [(j, i) for i, j in ups]))  18.7 us
    ppermute x6, waiting for transfers between devices, swap_both(): got.append(lax.ppermute(value, axis, ups + [(j, i) for i, j in ups]))  13.4 us
    ppermute x2, starting transfers between devices, shift(): return lax.ppermute(value, axis, pairs)  10.1 us
    ppermute x2, waiting for transfers between devices, cross(): return lax.ppermute(value, ('gx', axis), pairs)  9.31 us
    ppermute x2, waiting for transfers between devices, shift(): return lax.ppermute(value, axis, pairs)  9.02 us
    ppermute x5, waiting for transfers between devices, swap(): lax.ppermute(value, axis, [(i, i ^ bit) for i in range(lax.axis_size(axis...  7.89 us
  transfers between devices with their start and end apart: 15, of which 13 were waited for; matrix products, arithmetic and copies ran while one was open for 0% of the time, Pallas kernels for 0%

profile of v3, /device:TPU:17, one launch (start us, length us, event | category | flops | bytes accessed | tf_op | source)
XLA Modules:
  0.0 117.8 jit_solution(10777880594133535488)
XLA Ops:
  0.0 2.7 %shard_map.46 = (f32[3,8,32,128]{3,2,1,0:T(8,128)}, f32[2,32,128]{2,1,0:T(8,128)}, f32[2,32,128]{2,1,0:T(8,128)}) custom-call(f32[16]{0:T(128)} %table.1, f32[8,32,128]{2,1,0:T(8,128)} %pred_.1, f32[8,32,128]{2,1,0:T(8,128)} %right.1, s32[8,32,128]{2,1,0:T(8,128)} %zone.1), custom_call_target="tpu_custom_call" | custom-call | tf_op jit(solution)/shard_map/pallas_call | solution.py:483
  2.7 8.8 %collective-permute-start = (f32[2,32,128]{2,1,0:T(8,128)}, f32[2,32,128]{2,1,0:T(8,128)S(1)}, u32[]{:S(2)}, u32[]{:S(2)}) collective-permute-start(f32[2,32,128]{2,1,0:T(8,128)} %get-tuple-element.29), channel_id=1, source_target_pairs={{0,1},{1,2},{2,3},{4,5},{5,6},{6,7},{8,9},{9,10},{10,11},{12,13},{... | collective-permute-start | bytes 98312 | tf_op jit(solution)/shard_map/ppermute | solution.py:496
  12.8 9.0 %collective-permute-done.1.znext = f32[2,32,128]{2,1,0:T(8,128)S(1)} collective-permute-done((f32[2,32,128]{2,1,0:T(8,128)}, f32[2,32,128]{2,1,0:T(8,128)S(1)}, u32[]{:S(2)}, u32[]{:S(2)}) %collective-permute-start.1) | collective-permute-done | bytes 32800 | tf_op jit(solution)/shard_map/ppermute | solution.py:496
  22.9 4.3 %collective-permute-start.2 = (f32[28,8,128]{2,1,0:T(8,128)S(1)}, f32[28,8,128]{2,1,0:T(8,128)S(1)}, u32[]{:S(2)}, u32[]{:S(2)}) collective-permute-start(f32[28,8,128]{2,1,0:T(8,128)S(1)} %get-tuple-element.32), channel_id=1, source_target_pairs={{4,8},{12,16},{20,24},{28,32},{36,40},{44,48},{52,56},{8,4},{16,12... | collective-permute-start | bytes 344072 | tf_op jit(solution)/shard_map/ppermute | solution.py:508
  27.2 2.0 %collective-permute-start.3 = (f32[28,8,128]{2,1,0:T(8,128)S(1)}, f32[28,8,128]{2,1,0:T(8,128)S(1)}, u32[]{:S(2)}, u32[]{:S(2)}) collective-permute-start(f32[28,8,128]{2,1,0:T(8,128)S(1)} %get-tuple-element.33), channel_id=1, source_target_pairs={{0,4},{8,12},{16,20},{24,28},{32,36},{40,44},{48,52},{56,60},{4,0}... | collective-permute-start | bytes 344072 | tf_op jit(solution)/shard_map/ppermute | solution.py:508
  30.5 2.5 %collective-permute-done.3.yb = f32[28,8,128]{2,1,0:T(8,128)S(1)} collective-permute-done((f32[28,8,128]{2,1,0:T(8,128)S(1)}, f32[28,8,128]{2,1,0:T(8,128)S(1)}, u32[]{:S(2)}, u32[]{:S(2)}) %collective-permute-start.3) | collective-permute-done | bytes 114720 | tf_op jit(solution)/shard_map/ppermute | solution.py:508
  33.1 5.5 %collective-permute-start.4 = (f32[142,8,128]{2,1,0:T(8,128)S(1)}, f32[142,8,128]{2,1,0:T(8,128)S(1)}, u32[]{:S(2)}, u32[]{:S(2)}) collective-permute-start(f32[142,8,128]{2,1,0:T(8,128)S(1)} %get-tuple-element.36), channel_id=1, source_target_pairs={{64,128},{192,256},{320,384},{128,64},{256,192},{384,320},{65,129}... | collective-permute-start | bytes 1744904 | tf_op jit(solution)/shard_map/ppermute | solution.py:508
  38.6 1.9 %collective-permute-start.5 = (f32[142,8,128]{2,1,0:T(8,128)S(1)}, f32[142,8,128]{2,1,0:T(8,128)S(1)}, u32[]{:S(2)}, u32[]{:S(2)}) collective-permute-start(f32[142,8,128]{2,1,0:T(8,128)S(1)} %get-tuple-element.37), channel_id=1, source_target_pairs={{0,64},{128,192},{256,320},{384,448},{64,0},{192,128},{320,256},{4... | collective-permute-start | bytes 1744904 | tf_op jit(solution)/shard_map/ppermute | solution.py:508
  40.5 5.5 %collective-permute-done.4.xa = f32[142,8,128]{2,1,0:T(8,128)S(1)} collective-permute-done((f32[142,8,128]{2,1,0:T(8,128)S(1)}, f32[142,8,128]{2,1,0:T(8,128)S(1)}, u32[]{:S(2)}, u32[]{:S(2)}) %collective-permute-start.4) | collective-permute-done | bytes 581664 | tf_op jit(solution)/shard_map/ppermute | solution.py:508
  46.1 6.5 %shard_map.49 = (f32[24,2,64,128]{3,2,1,0:T(8,128)S(1)}, f32[24,2,48,128]{3,2,1,0:T(8,128)S(1)}, f32[24,2,48,128]{3,2,1,0:T(8,128)S(1)}, f32[2,4,16,128]{3,2,1,0...) custom-call(s32[1]{0:T(128)} %bitcast.px.place, f32[3,8,32,128]{3,2,1,0:T(8,128)S(1)} %get-tuple-element.31.main, ...), custom_call_target="tpu_custom_call" | custom-call | tf_op jit(solution)/shard_map/pallas_call | solution.py:483
  52.6 1.9 %collective-permute-start.6 = (f32[2,16,128]{2,1,0:T(8,128)S(1)}, f32[2,16,128]{2,1,0:T(8,128)S(1)}, u32[]{:S(2)}, u32[]{:S(2)}) collective-permute-start(f32[2,16,128]{2,1,0:T(8,128)S(1)} %get-tuple-element.40), channel_id=1, source_target_pairs={{0,64},{64,0},{128,192},{192,128},{256,320},{320,256},{384,448},{4... | collective-permute-start | bytes 49160 | tf_op jit(solution)/shard_map/ppermute | solution.py:500
  57.0 7.8 %collective-permute-done.7.halo = f32[2,2,16,128]{3,2,1,0:T(8,128)S(1)} collective-permute-done((f32[2,2,16,128]{3,2,1,0:T(8,128)S(1)}, f32[2,2,16,128]{3,2,1,0:T(8,128)S(1)}, u32[]{:S(2)}, u32[]{:S(2)}) %collective-permute-start.7) | collective-permute-done | bytes 32800 | tf_op jit(solution)/shard_map/ppermute | solution.py:518
  64.9 4.1 %collective-permute-start.8 = (f32[1,2,4,16,128]{4,3,2,1,0:T(8,128)S(1)}, f32[1,2,4,16,128]{4,3,2,1,0:T(8,128)S(1)}, u32[]{:S(2)}, u32[]{:S(2)}) collective-permute-start(f32[1,2,4,16,128]{4,3,2,1,0:T(8,128)S(1)} %shard_map.50), channel_id=1, source_target_pairs={{0,256},{64,320},{128,384},{192,448},{256,0},{320,64},{384,128},{4... | collective-permute-start | bytes 196616 | tf_op jit(solution)/shard_map/ppermute | solution.py:500
  69.1 1.8 %collective-permute-done.8 = f32[1,2,4,16,128]{4,3,2,1,0:T(8,128)S(1)} collective-permute-done((f32[1,2,4,16,128]{4,3,2,1,0:T(8,128)S(1)}, f32[1,2,4,16,128]{4,3,2,1,0:T(8,128)S(1)}, u32[]{:S(2)}, u32[]{:S(2)}) %collective-permute-start.8) | collective-permute-done | bytes 65568 | tf_op jit(solution)/shard_map/ppermute | solution.py:500
  70.9 3.7 %collective-permute-start.9 = (f32[2,2,4,16,128]{4,3,2,1,0:T(8,128)S(1)}, f32[2,2,4,16,128]{4,3,2,1,0:T(8,128)S(1)}, u32[]{:S(2)}, u32[]{:S(2)}) collective-permute-start(f32[2,2,4,16,128]{4,3,2,1,0:T(8,128)S(1)} %pad_maximum_fusion.1), channel_id=1, source_target_pairs={{0,128},{64,192},{128,0},{192,64},{256,384},{320,448},{384,256},{4... | collective-permute-start | bytes 393224 | tf_op jit(solution)/shard_map/ppermute | solution.py:500
  74.6 2.3 %collective-permute-done.9 = f32[2,2,4,16,128]{4,3,2,1,0:T(8,128)S(1)} collective-permute-done((f32[2,2,4,16,128]{4,3,2,1,0:T(8,128)S(1)}, f32[2,2,4,16,128]{4,3,2,1,0:T(8,128)S(1)}, u32[]{:S(2)}, u32[]{:S(2)}) %collective-permute-start.9) | collective-permute-done | bytes 131104 | tf_op jit(solution)/shard_map/ppermute | solution.py:500
  77.0 3.1 %collective-permute-start.10 = (f32[36,8,128]{2,1,0:T(8,128)S(1)}, f32[36,8,128]{2,1,0:T(8,128)S(1)}, u32[]{:S(2)}, u32[]{:S(2)}) collective-permute-start(f32[36,8,128]{2,1,0:T(8,128)S(1)} %get-tuple-element.41), channel_id=1, source_target_pairs={{4,8},{12,16},{20,24},{28,32},{36,40},{44,48},{52,56},{8,4},{16,12... | collective-permute-start | bytes 442376 | tf_op jit(solution)/shard_map/ppermute | solution.py:508
  80.1 1.9 %collective-permute-start.11 = (f32[36,8,128]{2,1,0:T(8,128)S(1)}, f32[36,8,128]{2,1,0:T(8,128)S(1)}, u32[]{:S(2)}, u32[]{:S(2)}) collective-permute-start(f32[36,8,128]{2,1,0:T(8,128)S(1)} %get-tuple-element.42), channel_id=1, source_target_pairs={{0,4},{8,12},{16,20},{24,28},{32,36},{40,44},{48,52},{56,60},{4,0}... | collective-permute-start | bytes 442376 | tf_op jit(solution)/shard_map/ppermute | solution.py:508
  82.1 2.9 %collective-permute-done.10.ya = f32[36,8,128]{2,1,0:T(8,128)S(1)} collective-permute-done((f32[36,8,128]{2,1,0:T(8,128)S(1)}, f32[36,8,128]{2,1,0:T(8,128)S(1)}, u32[]{:S(2)}, u32[]{:S(2)}) %collective-permute-start.10) | collective-permute-done | bytes 147488 | tf_op jit(solution)/shard_map/ppermute | solution.py:508
  86.1 6.8 %collective-permute-start.12 = (f32[4,2,4,40,128]{4,3,2,1,0:T(8,128)S(1)}, f32[4,2,4,40,128]{4,3,2,1,0:T(8,128)S(1)}, u32[]{:S(2)}, u32[]{:S(2)}) collective-permute-start(f32[4,2,4,40,128]{4,3,2,1,0:T(8,128)S(1)} %shard_map.52.near), channel_id=1, source_target_pairs={{0,64},{64,0},{128,192},{192,128},{256,320},{320,256},{384,448},{4... | collective-permute-start | bytes 1966088 | tf_op jit(solution)/shard_map/ppermute | solution.py:500
  94.5 4.9 %shard_map.53 = (f32[47,1,56,128]{3,2,1,0:T(8,128)S(1)}, f32[47,1,40,128]{3,2,1,0:T(8,128)S(1)}, f32[47,1,40,128]{3,2,1,0:T(8,128)S(1)}, f32[16,8,128]{2,1,0:T(8,128)S(1)}, f32[20,8,128]{2,1,0:T(8,128)S(1)}) custom-call(s32[1]{0:T(128)} %bitcast.px.place, f32[4,2,4,40,128]{4,3,2,1,0:T(8,128)S(1)} %shard_map.52.near, ...), custom_call_target="tpu_custom_call" | custom-call | tf_op jit(solution)/shard_map/pallas_call | solution.py:483
  99.4 4.3 %collective-permute-start.13 = (f32[20,8,128]{2,1,0:T(8,128)S(1)}, f32[20,8,128]{2,1,0:T(8,128)S(1)}, u32[]{:S(2)}, u32[]{:S(2)}) collective-permute-start(f32[20,8,128]{2,1,0:T(8,128)S(1)} %get-tuple-element.44), channel_id=1, source_target_pairs={{0,4},{4,8},{8,12},{12,16},{16,20},{20,24},{24,28},{28,32},{32,36}... | collective-permute-start | bytes 245768 | tf_op jit(solution)/shard_map/ppermute | solution.py:518
  105.2 5.0 %collective-permute-start.14 = (f32[20,8,128]{2,1,0:T(8,128)S(1)}, f32[20,8,128]{2,1,0:T(8,128)S(1)}, u32[]{:S(2)}, u32[]{:S(2)}) collective-permute-start(f32[20,8,128]{2,1,0:T(8,128)S(1)} %collective-permute-done.13.brought), channel_id=1, source_target_pairs={{0,64},{64,0},{128,192},{192,128},{256,320},{320,256},{384,448},{4... | collective-permute-start | bytes 245768 | tf_op jit(solution)/shard_map/ppermute | solution.py:500
  111.0 6.8 %shard_map.54 = f32[8,32,128]{2,1,0:T(8,128)} custom-call(s32[1]{0:T(128)} %bitcast.px.place, f32[16,8,128]{2,1,0:T(8,128)S(1)} %get-tuple-element.43.two, f32[20,8,128]{2,1,0:T(8,128)S(1)} %collective-permute-done.13.brought, f32[20,8,128]{2,1,0:T(8,128)S(1)} %collective-permute-done.14.given, f32[47,1,56,128]{3,2,1,0:T(8,128)S(1)} %get-tuple-element.45.x1, ...), custom_call_target="tpu_custom_call" | custom-call | tf_op jit(solution)/shard_map/pallas_call | solution.py:483
  (20 shorter events, 11.6 us)
Async XLA Ops:
  2.7 10.1 %collective-permute-start = (f32[2,32,128]{2,1,0:T(8,128)}, f32[2,32,128]{2,1,0:T(8,128)S(1)}, u32[]{:S(2)}, u32[]{:S(2)}) collective-permute-start(f32[2,32,128]{2,1,0:T(8,128)} %get-tuple-element.29), channel_id=1, source_target_pairs={{0,1},{1,2},{2,3},{4,5},{5,6},{6,7},{8,9},{9,10},{10,11},{12,13},{... | collective-permute-start | bytes 98312 | tf_op jit(solution)/shard_map/ppermute | solution.py:496
  11.5 10.3 %collective-permute-start.1 = (f32[2,32,128]{2,1,0:T(8,128)}, f32[2,32,128]{2,1,0:T(8,128)S(1)}, u32[]{:S(2)}, u32[]{:S(2)}) collective-permute-start(f32[2,32,128]{2,1,0:T(8,128)} %get-tuple-element.30), channel_id=1, source_target_pairs={{1,0},{2,1},{3,2},{5,4},{6,5},{7,6},{9,8},{10,9},{11,10},{13,12},{... | collective-permute-start | bytes 98312 | tf_op jit(solution)/shard_map/ppermute | solution.py:496
  21.8 1.0 copy-start
  22.9 7.6 %collective-permute-start.2 = (f32[28,8,128]{2,1,0:T(8,128)S(1)}, f32[28,8,128]{2,1,0:T(8,128)S(1)}, u32[]{:S(2)}, u32[]{:S(2)}) collective-permute-start(f32[28,8,128]{2,1,0:T(8,128)S(1)} %get-tuple-element.32), channel_id=1, source_target_pairs={{4,8},{12,16},{20,24},{28,32},{36,40},{44,48},{52,56},{8,4},{16,12... | collective-permute-start | bytes 344072 | tf_op jit(solution)/shard_map/ppermute | solution.py:508
  27.2 5.8 %collective-permute-start.3 = (f32[28,8,128]{2,1,0:T(8,128)S(1)}, f32[28,8,128]{2,1,0:T(8,128)S(1)}, u32[]{:S(2)}, u32[]{:S(2)}) collective-permute-start(f32[28,8,128]{2,1,0:T(8,128)S(1)} %get-tuple-element.33), channel_id=1, source_target_pairs={{0,4},{8,12},{16,20},{24,28},{32,36},{40,44},{48,52},{56,60},{4,0}... | collective-permute-start | bytes 344072 | tf_op jit(solution)/shard_map/ppermute | solution.py:508
  33.1 13.0 %collective-permute-start.4 = (f32[142,8,128]{2,1,0:T(8,128)S(1)}, f32[142,8,128]{2,1,0:T(8,128)S(1)}, u32[]{:S(2)}, u32[]{:S(2)}) collective-permute-start(f32[142,8,128]{2,1,0:T(8,128)S(1)} %get-tuple-element.36), channel_id=1, source_target_pairs={{64,128},{192,256},{320,384},{128,64},{256,192},{384,320},{65,129}... | collective-permute-start | bytes 1744904 | tf_op jit(solution)/shard_map/ppermute | solution.py:508
  38.6 7.5 %collective-permute-start.5 = (f32[142,8,128]{2,1,0:T(8,128)S(1)}, f32[142,8,128]{2,1,0:T(8,128)S(1)}, u32[]{:S(2)}, u32[]{:S(2)}) collective-permute-start(f32[142,8,128]{2,1,0:T(8,128)S(1)} %get-tuple-element.37), channel_id=1, source_target_pairs={{0,64},{128,192},{256,320},{384,448},{64,0},{192,128},{320,256},{4... | collective-permute-start | bytes 1744904 | tf_op jit(solution)/shard_map/ppermute | solution.py:508
  52.6 3.1 %collective-permute-start.6 = (f32[2,16,128]{2,1,0:T(8,128)S(1)}, f32[2,16,128]{2,1,0:T(8,128)S(1)}, u32[]{:S(2)}, u32[]{:S(2)}) collective-permute-start(f32[2,16,128]{2,1,0:T(8,128)S(1)} %get-tuple-element.40), channel_id=1, source_target_pairs={{0,64},{64,0},{128,192},{192,128},{256,320},{320,256},{384,448},{4... | collective-permute-start | bytes 49160 | tf_op jit(solution)/shard_map/ppermute | solution.py:500
  55.7 9.1 %collective-permute-start.7 = (f32[2,2,16,128]{3,2,1,0:T(8,128)S(1)}, f32[2,2,16,128]{3,2,1,0:T(8,128)S(1)}, u32[]{:S(2)}, u32[]{:S(2)}) collective-permute-start(f32[2,2,16,128]{3,2,1,0:T(8,128)S(1)} %pad_maximum_fusion.2), channel_id=1, source_target_pairs={{0,1},{1,2},{2,3},{65,64},{66,65},{67,66},{128,129},{129,130},{130... | collective-permute-start | bytes 98312 | tf_op jit(solution)/shard_map/ppermute | solution.py:518
  64.9 5.9 %collective-permute-start.8 = (f32[1,2,4,16,128]{4,3,2,1,0:T(8,128)S(1)}, f32[1,2,4,16,128]{4,3,2,1,0:T(8,128)S(1)}, u32[]{:S(2)}, u32[]{:S(2)}) collective-permute-start(f32[1,2,4,16,128]{4,3,2,1,0:T(8,128)S(1)} %shard_map.50), channel_id=1, source_target_pairs={{0,256},{64,320},{128,384},{192,448},{256,0},{320,64},{384,128},{4... | collective-permute-start | bytes 196616 | tf_op jit(solution)/shard_map/ppermute | solution.py:500
  70.9 6.1 %collective-permute-start.9 = (f32[2,2,4,16,128]{4,3,2,1,0:T(8,128)S(1)}, f32[2,2,4,16,128]{4,3,2,1,0:T(8,128)S(1)}, u32[]{:S(2)}, u32[]{:S(2)}) collective-permute-start(f32[2,2,4,16,128]{4,3,2,1,0:T(8,128)S(1)} %pad_maximum_fusion.1), channel_id=1, source_target_pairs={{0,128},{64,192},{128,0},{192,64},{256,384},{320,448},{384,256},{4... | collective-permute-start | bytes 393224 | tf_op jit(solution)/shard_map/ppermute | solution.py:500
  77.0 8.0 %collective-permute-start.10 = (f32[36,8,128]{2,1,0:T(8,128)S(1)}, f32[36,8,128]{2,1,0:T(8,128)S(1)}, u32[]{:S(2)}, u32[]{:S(2)}) collective-permute-start(f32[36,8,128]{2,1,0:T(8,128)S(1)} %get-tuple-element.41), channel_id=1, source_target_pairs={{4,8},{12,16},{20,24},{28,32},{36,40},{44,48},{52,56},{8,4},{16,12... | collective-permute-start | bytes 442376 | tf_op jit(solution)/shard_map/ppermute | solution.py:508
  80.1 5.9 %collective-permute-start.11 = (f32[36,8,128]{2,1,0:T(8,128)S(1)}, f32[36,8,128]{2,1,0:T(8,128)S(1)}, u32[]{:S(2)}, u32[]{:S(2)}) collective-permute-start(f32[36,8,128]{2,1,0:T(8,128)S(1)} %get-tuple-element.42), channel_id=1, source_target_pairs={{0,4},{8,12},{16,20},{24,28},{32,36},{40,44},{48,52},{56,60},{4,0}... | collective-permute-start | bytes 442376 | tf_op jit(solution)/shard_map/ppermute | solution.py:508
  86.1 8.5 %collective-permute-start.12 = (f32[4,2,4,40,128]{4,3,2,1,0:T(8,128)S(1)}, f32[4,2,4,40,128]{4,3,2,1,0:T(8,128)S(1)}, u32[]{:S(2)}, u32[]{:S(2)}) collective-permute-start(f32[4,2,4,40,128]{4,3,2,1,0:T(8,128)S(1)} %shard_map.52.near), channel_id=1, source_target_pairs={{0,64},{64,0},{128,192},{192,128},{256,320},{320,256},{384,448},{4... | collective-permute-start | bytes 1966088 | tf_op jit(solution)/shard_map/ppermute | solution.py:500
  99.4 5.7 %collective-permute-start.13 = (f32[20,8,128]{2,1,0:T(8,128)S(1)}, f32[20,8,128]{2,1,0:T(8,128)S(1)}, u32[]{:S(2)}, u32[]{:S(2)}) collective-permute-start(f32[20,8,128]{2,1,0:T(8,128)S(1)} %get-tuple-element.44), channel_id=1, source_target_pairs={{0,4},{4,8},{8,12},{12,16},{16,20},{20,24},{24,28},{28,32},{32,36}... | collective-permute-start | bytes 245768 | tf_op jit(solution)/shard_map/ppermute | solution.py:518
  105.2 5.9 %collective-permute-start.14 = (f32[20,8,128]{2,1,0:T(8,128)S(1)}, f32[20,8,128]{2,1,0:T(8,128)S(1)}, u32[]{:S(2)}, u32[]{:S(2)}) collective-permute-start(f32[20,8,128]{2,1,0:T(8,128)S(1)} %collective-permute-done.13.brought), channel_id=1, source_target_pairs={{0,64},{64,0},{128,192},{192,128},{256,320},{320,256},{384,448},{4... | collective-permute-start | bytes 245768 | tf_op jit(solution)/shard_map/ppermute | solution.py:500

commit v4 on v3

--- a/solution.py
+++ b/solution.py
@@ -56,7 +56,7 @@
         x[i, h, pl.ds(7, 1)] = value[7:8]
 
 
-def stencil(x, first, group, halves, rows, use):
+def stencil(x, first, group, halves, rows, use, flush=None):
     lane = lanes_like((8, 128))
     for row in rows:
         def load(i):
@@ -73,6 +73,8 @@
             ]
             use(j, row, own, total)
             below, own = own, above
+        if flush is not None and (group > 4 or row // 8 % 2 == 1 or row == rows[-1]):
+            flush()
 
 
 def sweep(xin, xout, upd, src, inv, start, stop, a, c, group, cyclic, offset=0):
@@ -84,10 +86,16 @@
             for h in range(halves):
                 g = (src[i + offset, h, tile] + total[h]) * inv[i + offset, h, tile] - own[h]
                 u = c * g if a == 0.0 else a * upd[i, h, tile] + c * g
-                upd[i, h, tile] = u
-                put(xout, i, h, row, own[h] + u, height, cyclic)
-
-        stencil(xin, first, group, halves, range(0, height, 8), use)
+                made.append((i, h, row, u, own[h] + u))
+
+        def flush():
+            for i, h, row, u, value in made:
+                upd[i, h, pl.ds(row, 8)] = u
+                put(xout, i, h, row, value, height, cyclic)
+            made.clear()
+
+        made = []
+        stencil(xin, first, group, halves, range(0, height, 8), use, flush)
 
     steps = (stop - start) // group
     if steps == 1:
@@ -397,6 +405,11 @@
             edge_out[16 + n // 4, pl.ds(2 * (n % 4), 2)] = beyond
 
 
+def double(x, i, h, row, value):
+    for odd in range(2):
+        x.at[i, h][pl.ds(row + odd, value.shape[0], stride=2), :] = value
+
+
 def one_hot(shape, axis, source):
     at = lax.broadcasted_iota(jnp.int32, shape, axis)
     return jnp.where(at == source, 1.0, 0.0).astype(F32)
@@ -440,35 +453,37 @@
         flat[3 + q] = v if q < 8 else pltpu.roll(v, 64, 1)
     l = lax.broadcasted_iota(jnp.int32, (1, 128), 1)
     wide = one_hot((128, 128), 0, jnp.where(l < 96, 16 + l // 2, l // 2 - 48))
-    r = lax.broadcasted_iota(jnp.int32, (40, 1), 0)
-    tall = one_hot((40, 32), 1, jnp.where(r < 28, r // 2, 12 + r // 2))
     part = dot(flat[pl.ds(2 * place[0], 8)].reshape(256, 128), wide)
-    fine = dot(tall, jnp.concatenate([part[32 * w:32 * w + 32] for w in range(8)], axis=1))
     first = 4 * place[0] + 1
-    for w in range(16):
-        v = w // 2
+    for v in range(8):
+        double(oa, 2 * v, 0, 32, part[32 * v + 24:32 * v + 32])
+        double(oa, 2 * v, 0, 8, part[32 * v:32 * v + 14])
         for t in range(5):
-            value = x1[first + w, 0, pl.ds(8 + 8 * t, 8)] + fine[8 * t:8 * t + 8, 128 * v:128 * v + 128]
-            put(oa, w, 0, 8 * t, value, 40, True)
+            fine = oa[2 * v, 0, pl.ds(8 + 8 * t, 8)]
+            for w in (2 * v, 2 * v + 1):
+                put(oa, w, 0, 8 * t, x1[first + w, 0, pl.ds(8 + 8 * t, 8)] + fine, 40, True)
     xin, xout = oa, ob
     for k, (a, c) in enumerate(factors(SMOOTH_DEG, *SMOOTH)):
         sweep(xin, xout, oupd, src1, inv1, k + 1, 15 - k, a, c, 14 - 2 * k, True, offset=first)
         xin, xout = xout, xin
     side = jnp.where((l < 8) | (l >= 120), 64 + l // 2, -1)
     wide = [one_hot((128, 128), 0, l // 2), one_hot((128, 128), 0, side)]
-    r = lax.broadcasted_iota(jnp.int32, (48, 1), 0)
-    tall = one_hot((48, 40), 1, jnp.where(r < 8, 36 + r // 2, r // 2 - 4))
     below = xin[4:12, 0, 8:48].reshape(320, 128)
     zero = jnp.zeros((8, 128), F32)
     for h in range(2):
         part = dot(below, wide[h])
-        fine = dot(tall, jnp.concatenate([part[40 * w:40 * w + 40] for w in range(8)], axis=1))
-        for w in range(16):
-            v = w // 2
-            za[w, h, pl.ds(8, 48)] = x0[4 + w, h, pl.ds(8, 48)] + fine[:, 128 * v:128 * v + 128]
-            for field in (za, zb):
-                field[w, h, pl.ds(0, 8)] = zero
-                field[w, h, pl.ds(56, 8)] = zero
+        for v in range(8):
+            double(za, 2 * v, h, 0, part[40 * v + 32:40 * v + 40])
+            double(za, 2 * v, h, 16, part[40 * v:40 * v + 20])
+            for t in range(6):
+                tile = pl.ds(8 + 8 * t, 8)
+                fine = za[2 * v, h, tile]
+                for w in (2 * v, 2 * v + 1):
+                    za[w, h, tile] = x0[4 + w, h, tile] + fine
+            for w in (2 * v, 2 * v + 1):
+                for field in (za, zb):
+                    field[w, h, pl.ds(0, 8)] = zero
+                    field[w, h, pl.ds(56, 8)] = zero
     xin, xout = za, zb
     for k, (a, c) in enumerate(factors(SMOOTH_DEG, *SMOOTH)):
         sweep(xin, xout, zupd, src0, inv0, k + 1, 15 - k, a, c, 2, False, offset=4)

time: 118 us -> 117 us (level)
  the two profiles are of different devices: /device:TPU:17 before, /device:TPU:9 now
where the time goes in v4:
time: 117 us
  starting transfers between devices  55.8 us (48%)
  waiting for transfers between devices  39.6 us (34%)
  Pallas kernels  20.2 us (17%)
    ppermute x5, starting transfers between devices, swap(): lax.ppermute(value, axis, [(i, i ^ bit) for i in range(lax.axis_size(axis...  21.4 us
    pallas_call x9, Pallas kernels, call(): pl.pallas_call(kernel, out_shape=[jax.ShapeDtypeStruct(s, F32) for s in o...  20.2 us
    ppermute x6, starting transfers between devices, swap_both(): got.append(lax.ppermute(value, axis, ups + [(j, i) for i, j in ups]))  18.7 us
    ppermute x6, waiting for transfers between devices, swap_both(): got.append(lax.ppermute(value, axis, ups + [(j, i) for i, j in ups]))  13.4 us
    ppermute x2, starting transfers between devices, shift(): return lax.ppermute(value, axis, pairs)  10.1 us
    ppermute x2, waiting for transfers between devices, cross(): return lax.ppermute(value, ('gx', axis), pairs)  9.31 us
    ppermute x2, waiting for transfers between devices, shift(): return lax.ppermute(value, axis, pairs)  9.02 us
    ppermute x5, waiting for transfers between devices, swap(): lax.ppermute(value, axis, [(i, i ^ bit) for i in range(lax.axis_size(axis...  7.89 us
  transfers between devices with their start and end apart: 15, of which 13 were waited for; matrix products, arithmetic and copies ran while one was open for 0% of the time, Pallas kernels for 0%

profile of v4, /device:TPU:9, one launch (start us, length us, event | category | flops | bytes accessed | tf_op | source)
XLA Modules:
  0.0 116.9 jit_solution(4327019158936685800)
XLA Ops:
  0.0 2.7 %shard_map.46 = (f32[3,8,32,128]{3,2,1,0:T(8,128)}, f32[2,32,128]{2,1,0:T(8,128)}, f32[2,32,128]{2,1,0:T(8,128)}) custom-call(f32[16]{0:T(128)} %table.1, f32[8,32,128]{2,1,0:T(8,128)} %pred_.1, f32[8,32,128]{2,1,0:T(8,128)} %right.1, s32[8,32,128]{2,1,0:T(8,128)} %zone.1), custom_call_target="tpu_custom_call" | custom-call | tf_op jit(solution)/shard_map/pallas_call | solution.py:498
  2.7 8.8 %collective-permute-start = (f32[2,32,128]{2,1,0:T(8,128)}, f32[2,32,128]{2,1,0:T(8,128)S(1)}, u32[]{:S(2)}, u32[]{:S(2)}) collective-permute-start(f32[2,32,128]{2,1,0:T(8,128)} %get-tuple-element.29), channel_id=1, source_target_pairs={{0,1},{1,2},{2,3},{4,5},{5,6},{6,7},{8,9},{9,10},{10,11},{12,13},{... | collective-permute-start | bytes 98312 | tf_op jit(solution)/shard_map/ppermute | solution.py:511
  12.8 9.0 %collective-permute-done.1.znext = f32[2,32,128]{2,1,0:T(8,128)S(1)} collective-permute-done((f32[2,32,128]{2,1,0:T(8,128)}, f32[2,32,128]{2,1,0:T(8,128)S(1)}, u32[]{:S(2)}, u32[]{:S(2)}) %collective-permute-start.1) | collective-permute-done | bytes 32800 | tf_op jit(solution)/shard_map/ppermute | solution.py:511
  22.9 4.3 %collective-permute-start.2 = (f32[28,8,128]{2,1,0:T(8,128)S(1)}, f32[28,8,128]{2,1,0:T(8,128)S(1)}, u32[]{:S(2)}, u32[]{:S(2)}) collective-permute-start(f32[28,8,128]{2,1,0:T(8,128)S(1)} %get-tuple-element.32), channel_id=1, source_target_pairs={{4,8},{12,16},{20,24},{28,32},{36,40},{44,48},{52,56},{8,4},{16,12... | collective-permute-start | bytes 344072 | tf_op jit(solution)/shard_map/ppermute | solution.py:523
  27.2 2.0 %collective-permute-start.3 = (f32[28,8,128]{2,1,0:T(8,128)S(1)}, f32[28,8,128]{2,1,0:T(8,128)S(1)}, u32[]{:S(2)}, u32[]{:S(2)}) collective-permute-start(f32[28,8,128]{2,1,0:T(8,128)S(1)} %get-tuple-element.33), channel_id=1, source_target_pairs={{0,4},{8,12},{16,20},{24,28},{32,36},{40,44},{48,52},{56,60},{4,0}... | collective-permute-start | bytes 344072 | tf_op jit(solution)/shard_map/ppermute | solution.py:523
  30.5 2.5 %collective-permute-done.3.yb = f32[28,8,128]{2,1,0:T(8,128)S(1)} collective-permute-done((f32[28,8,128]{2,1,0:T(8,128)S(1)}, f32[28,8,128]{2,1,0:T(8,128)S(1)}, u32[]{:S(2)}, u32[]{:S(2)}) %collective-permute-start.3) | collective-permute-done | bytes 114720 | tf_op jit(solution)/shard_map/ppermute | solution.py:523
  33.1 5.5 %collective-permute-start.4 = (f32[142,8,128]{2,1,0:T(8,128)S(1)}, f32[142,8,128]{2,1,0:T(8,128)S(1)}, u32[]{:S(2)}, u32[]{:S(2)}) collective-permute-start(f32[142,8,128]{2,1,0:T(8,128)S(1)} %get-tuple-element.36), channel_id=1, source_target_pairs={{64,128},{192,256},{320,384},{128,64},{256,192},{384,320},{65,129}... | collective-permute-start | bytes 1744904 | tf_op jit(solution)/shard_map/ppermute | solution.py:523
  38.6 1.9 %collective-permute-start.5 = (f32[142,8,128]{2,1,0:T(8,128)S(1)}, f32[142,8,128]{2,1,0:T(8,128)S(1)}, u32[]{:S(2)}, u32[]{:S(2)}) collective-permute-start(f32[142,8,128]{2,1,0:T(8,128)S(1)} %get-tuple-element.37), channel_id=1, source_target_pairs={{0,64},{128,192},{256,320},{384,448},{64,0},{192,128},{320,256},{4... | collective-permute-start | bytes 1744904 | tf_op jit(solution)/shard_map/ppermute | solution.py:523
  40.5 5.5 %collective-permute-done.4.xa = f32[142,8,128]{2,1,0:T(8,128)S(1)} collective-permute-done((f32[142,8,128]{2,1,0:T(8,128)S(1)}, f32[142,8,128]{2,1,0:T(8,128)S(1)}, u32[]{:S(2)}, u32[]{:S(2)}) %collective-permute-start.4) | collective-permute-done | bytes 581664 | tf_op jit(solution)/shard_map/ppermute | solution.py:523
  46.1 6.5 %shard_map.49 = (f32[24,2,64,128]{3,2,1,0:T(8,128)S(1)}, f32[24,2,48,128]{3,2,1,0:T(8,128)S(1)}, f32[24,2,48,128]{3,2,1,0:T(8,128)S(1)}, f32[2,4,16,128]{3,2,1,0...) custom-call(s32[1]{0:T(128)} %bitcast.px.place, f32[3,8,32,128]{3,2,1,0:T(8,128)S(1)} %get-tuple-element.31.main, ...), custom_call_target="tpu_custom_call" | custom-call | tf_op jit(solution)/shard_map/pallas_call | solution.py:498
  52.6 1.9 %collective-permute-start.6 = (f32[2,16,128]{2,1,0:T(8,128)S(1)}, f32[2,16,128]{2,1,0:T(8,128)S(1)}, u32[]{:S(2)}, u32[]{:S(2)}) collective-permute-start(f32[2,16,128]{2,1,0:T(8,128)S(1)} %get-tuple-element.40), channel_id=1, source_target_pairs={{0,64},{64,0},{128,192},{192,128},{256,320},{320,256},{384,448},{4... | collective-permute-start | bytes 49160 | tf_op jit(solution)/shard_map/ppermute | solution.py:515
  57.0 7.8 %collective-permute-done.7.halo = f32[2,2,16,128]{3,2,1,0:T(8,128)S(1)} collective-permute-done((f32[2,2,16,128]{3,2,1,0:T(8,128)S(1)}, f32[2,2,16,128]{3,2,1,0:T(8,128)S(1)}, u32[]{:S(2)}, u32[]{:S(2)}) %collective-permute-start.7) | collective-permute-done | bytes 32800 | tf_op jit(solution)/shard_map/ppermute | solution.py:533
  64.9 4.1 %collective-permute-start.8 = (f32[1,2,4,16,128]{4,3,2,1,0:T(8,128)S(1)}, f32[1,2,4,16,128]{4,3,2,1,0:T(8,128)S(1)}, u32[]{:S(2)}, u32[]{:S(2)}) collective-permute-start(f32[1,2,4,16,128]{4,3,2,1,0:T(8,128)S(1)} %shard_map.50), channel_id=1, source_target_pairs={{0,256},{64,320},{128,384},{192,448},{256,0},{320,64},{384,128},{4... | collective-permute-start | bytes 196616 | tf_op jit(solution)/shard_map/ppermute | solution.py:515
  69.0 1.8 %collective-permute-done.8 = f32[1,2,4,16,128]{4,3,2,1,0:T(8,128)S(1)} collective-permute-done((f32[1,2,4,16,128]{4,3,2,1,0:T(8,128)S(1)}, f32[1,2,4,16,128]{4,3,2,1,0:T(8,128)S(1)}, u32[]{:S(2)}, u32[]{:S(2)}) %collective-permute-start.8) | collective-permute-done | bytes 65568 | tf_op jit(solution)/shard_map/ppermute | solution.py:515
  70.8 3.7 %collective-permute-start.9 = (f32[2,2,4,16,128]{4,3,2,1,0:T(8,128)S(1)}, f32[2,2,4,16,128]{4,3,2,1,0:T(8,128)S(1)}, u32[]{:S(2)}, u32[]{:S(2)}) collective-permute-start(f32[2,2,4,16,128]{4,3,2,1,0:T(8,128)S(1)} %pad_maximum_fusion.1), channel_id=1, source_target_pairs={{0,128},{64,192},{128,0},{192,64},{256,384},{320,448},{384,256},{4... | collective-permute-start | bytes 393224 | tf_op jit(solution)/shard_map/ppermute | solution.py:515
  74.6 2.3 %collective-permute-done.9 = f32[2,2,4,16,128]{4,3,2,1,0:T(8,128)S(1)} collective-permute-done((f32[2,2,4,16,128]{4,3,2,1,0:T(8,128)S(1)}, f32[2,2,4,16,128]{4,3,2,1,0:T(8,128)S(1)}, u32[]{:S(2)}, u32[]{:S(2)}) %collective-permute-start.9) | collective-permute-done | bytes 131104 | tf_op jit(solution)/shard_map/ppermute | solution.py:515
  77.0 3.1 %collective-permute-start.10 = (f32[36,8,128]{2,1,0:T(8,128)S(1)}, f32[36,8,128]{2,1,0:T(8,128)S(1)}, u32[]{:S(2)}, u32[]{:S(2)}) collective-permute-start(f32[36,8,128]{2,1,0:T(8,128)S(1)} %get-tuple-element.41), channel_id=1, source_target_pairs={{4,8},{12,16},{20,24},{28,32},{36,40},{44,48},{52,56},{8,4},{16,12... | collective-permute-start | bytes 442376 | tf_op jit(solution)/shard_map/ppermute | solution.py:523
  80.1 1.9 %collective-permute-start.11 = (f32[36,8,128]{2,1,0:T(8,128)S(1)}, f32[36,8,128]{2,1,0:T(8,128)S(1)}, u32[]{:S(2)}, u32[]{:S(2)}) collective-permute-start(f32[36,8,128]{2,1,0:T(8,128)S(1)} %get-tuple-element.42), channel_id=1, source_target_pairs={{0,4},{8,12},{16,20},{24,28},{32,36},{40,44},{48,52},{56,60},{4,0}... | collective-permute-start | bytes 442376 | tf_op jit(solution)/shard_map/ppermute | solution.py:523
  82.0 2.9 %collective-permute-done.10.ya = f32[36,8,128]{2,1,0:T(8,128)S(1)} collective-permute-done((f32[36,8,128]{2,1,0:T(8,128)S(1)}, f32[36,8,128]{2,1,0:T(8,128)S(1)}, u32[]{:S(2)}, u32[]{:S(2)}) %collective-permute-start.10) | collective-permute-done | bytes 147488 | tf_op jit(solution)/shard_map/ppermute | solution.py:523
  86.1 6.8 %collective-permute-start.12 = (f32[4,2,4,40,128]{4,3,2,1,0:T(8,128)S(1)}, f32[4,2,4,40,128]{4,3,2,1,0:T(8,128)S(1)}, u32[]{:S(2)}, u32[]{:S(2)}) collective-permute-start(f32[4,2,4,40,128]{4,3,2,1,0:T(8,128)S(1)} %shard_map.52.near), channel_id=1, source_target_pairs={{0,64},{64,0},{128,192},{192,128},{256,320},{320,256},{384,448},{4... | collective-permute-start | bytes 1966088 | tf_op jit(solution)/shard_map/ppermute | solution.py:515
  94.5 4.9 %shard_map.53 = (f32[47,1,56,128]{3,2,1,0:T(8,128)S(1)}, f32[47,1,40,128]{3,2,1,0:T(8,128)S(1)}, f32[47,1,40,128]{3,2,1,0:T(8,128)S(1)}, f32[16,8,128]{2,1,0:T(8,128)S(1)}, f32[20,8,128]{2,1,0:T(8,128)S(1)}) custom-call(s32[1]{0:T(128)} %bitcast.px.place, f32[4,2,4,40,128]{4,3,2,1,0:T(8,128)S(1)} %shard_map.52.near, ...), custom_call_target="tpu_custom_call" | custom-call | tf_op jit(solution)/shard_map/pallas_call | solution.py:498
  99.4 4.3 %collective-permute-start.13 = (f32[20,8,128]{2,1,0:T(8,128)S(1)}, f32[20,8,128]{2,1,0:T(8,128)S(1)}, u32[]{:S(2)}, u32[]{:S(2)}) collective-permute-start(f32[20,8,128]{2,1,0:T(8,128)S(1)} %get-tuple-element.44), channel_id=1, source_target_pairs={{0,4},{4,8},{8,12},{12,16},{16,20},{20,24},{24,28},{28,32},{32,36}... | collective-permute-start | bytes 245768 | tf_op jit(solution)/shard_map/ppermute | solution.py:533
  105.2 5.0 %collective-permute-start.14 = (f32[20,8,128]{2,1,0:T(8,128)S(1)}, f32[20,8,128]{2,1,0:T(8,128)S(1)}, u32[]{:S(2)}, u32[]{:S(2)}) collective-permute-start(f32[20,8,128]{2,1,0:T(8,128)S(1)} %collective-permute-done.13.brought), channel_id=1, source_target_pairs={{0,64},{64,0},{128,192},{192,128},{256,320},{320,256},{384,448},{4... | collective-permute-start | bytes 245768 | tf_op jit(solution)/shard_map/ppermute | solution.py:515
  111.0 5.8 %shard_map.54 = f32[8,32,128]{2,1,0:T(8,128)} custom-call(s32[1]{0:T(128)} %bitcast.px.place, f32[16,8,128]{2,1,0:T(8,128)S(1)} %get-tuple-element.43.two, f32[20,8,128]{2,1,0:T(8,128)S(1)} %collective-permute-done.13.brought, f32[20,8,128]{2,1,0:T(8,128)S(1)} %collective-permute-done.14.given, f32[47,1,56,128]{3,2,1,0:T(8,128)S(1)} %get-tuple-element.45.x1, ...), custom_call_target="tpu_custom_call" | custom-call | tf_op jit(solution)/shard_map/pallas_call | solution.py:498
  (20 shorter events, 11.6 us)
Async XLA Ops:
  2.7 10.1 %collective-permute-start = (f32[2,32,128]{2,1,0:T(8,128)}, f32[2,32,128]{2,1,0:T(8,128)S(1)}, u32[]{:S(2)}, u32[]{:S(2)}) collective-permute-start(f32[2,32,128]{2,1,0:T(8,128)} %get-tuple-element.29), channel_id=1, source_target_pairs={{0,1},{1,2},{2,3},{4,5},{5,6},{6,7},{8,9},{9,10},{10,11},{12,13},{... | collective-permute-start | bytes 98312 | tf_op jit(solution)/shard_map/ppermute | solution.py:511
  11.5 10.3 %collective-permute-start.1 = (f32[2,32,128]{2,1,0:T(8,128)}, f32[2,32,128]{2,1,0:T(8,128)S(1)}, u32[]{:S(2)}, u32[]{:S(2)}) collective-permute-start(f32[2,32,128]{2,1,0:T(8,128)} %get-tuple-element.30), channel_id=1, source_target_pairs={{1,0},{2,1},{3,2},{5,4},{6,5},{7,6},{9,8},{10,9},{11,10},{13,12},{... | collective-permute-start | bytes 98312 | tf_op jit(solution)/shard_map/ppermute | solution.py:511
  21.8 1.0 copy-start
  22.9 7.6 %collective-permute-start.2 = (f32[28,8,128]{2,1,0:T(8,128)S(1)}, f32[28,8,128]{2,1,0:T(8,128)S(1)}, u32[]{:S(2)}, u32[]{:S(2)}) collective-permute-start(f32[28,8,128]{2,1,0:T(8,128)S(1)} %get-tuple-element.32), channel_id=1, source_target_pairs={{4,8},{12,16},{20,24},{28,32},{36,40},{44,48},{52,56},{8,4},{16,12... | collective-permute-start | bytes 344072 | tf_op jit(solution)/shard_map/ppermute | solution.py:523
  27.2 5.8 %collective-permute-start.3 = (f32[28,8,128]{2,1,0:T(8,128)S(1)}, f32[28,8,128]{2,1,0:T(8,128)S(1)}, u32[]{:S(2)}, u32[]{:S(2)}) collective-permute-start(f32[28,8,128]{2,1,0:T(8,128)S(1)} %get-tuple-element.33), channel_id=1, source_target_pairs={{0,4},{8,12},{16,20},{24,28},{32,36},{40,44},{48,52},{56,60},{4,0}... | collective-permute-start | bytes 344072 | tf_op jit(solution)/shard_map/ppermute | solution.py:523
  33.1 13.0 %collective-permute-start.4 = (f32[142,8,128]{2,1,0:T(8,128)S(1)}, f32[142,8,128]{2,1,0:T(8,128)S(1)}, u32[]{:S(2)}, u32[]{:S(2)}) collective-permute-start(f32[142,8,128]{2,1,0:T(8,128)S(1)} %get-tuple-element.36), channel_id=1, source_target_pairs={{64,128},{192,256},{320,384},{128,64},{256,192},{384,320},{65,129}... | collective-permute-start | bytes 1744904 | tf_op jit(solution)/shard_map/ppermute | solution.py:523
  38.6 7.5 %collective-permute-start.5 = (f32[142,8,128]{2,1,0:T(8,128)S(1)}, f32[142,8,128]{2,1,0:T(8,128)S(1)}, u32[]{:S(2)}, u32[]{:S(2)}) collective-permute-start(f32[142,8,128]{2,1,0:T(8,128)S(1)} %get-tuple-element.37), channel_id=1, source_target_pairs={{0,64},{128,192},{256,320},{384,448},{64,0},{192,128},{320,256},{4... | collective-permute-start | bytes 1744904 | tf_op jit(solution)/shard_map/ppermute | solution.py:523
  52.6 3.1 %collective-permute-start.6 = (f32[2,16,128]{2,1,0:T(8,128)S(1)}, f32[2,16,128]{2,1,0:T(8,128)S(1)}, u32[]{:S(2)}, u32[]{:S(2)}) collective-permute-start(f32[2,16,128]{2,1,0:T(8,128)S(1)} %get-tuple-element.40), channel_id=1, source_target_pairs={{0,64},{64,0},{128,192},{192,128},{256,320},{320,256},{384,448},{4... | collective-permute-start | bytes 49160 | tf_op jit(solution)/shard_map/ppermute | solution.py:515
  55.7 9.1 %collective-permute-start.7 = (f32[2,2,16,128]{3,2,1,0:T(8,128)S(1)}, f32[2,2,16,128]{3,2,1,0:T(8,128)S(1)}, u32[]{:S(2)}, u32[]{:S(2)}) collective-permute-start(f32[2,2,16,128]{3,2,1,0:T(8,128)S(1)} %pad_maximum_fusion.2), channel_id=1, source_target_pairs={{0,1},{1,2},{2,3},{65,64},{66,65},{67,66},{128,129},{129,130},{130... | collective-permute-start | bytes 98312 | tf_op jit(solution)/shard_map/ppermute | solution.py:533
  64.9 5.9 %collective-permute-start.8 = (f32[1,2,4,16,128]{4,3,2,1,0:T(8,128)S(1)}, f32[1,2,4,16,128]{4,3,2,1,0:T(8,128)S(1)}, u32[]{:S(2)}, u32[]{:S(2)}) collective-permute-start(f32[1,2,4,16,128]{4,3,2,1,0:T(8,128)S(1)} %shard_map.50), channel_id=1, source_target_pairs={{0,256},{64,320},{128,384},{192,448},{256,0},{320,64},{384,128},{4... | collective-permute-start | bytes 196616 | tf_op jit(solution)/shard_map/ppermute | solution.py:515
  70.8 6.1 %collective-permute-start.9 = (f32[2,2,4,16,128]{4,3,2,1,0:T(8,128)S(1)}, f32[2,2,4,16,128]{4,3,2,1,0:T(8,128)S(1)}, u32[]{:S(2)}, u32[]{:S(2)}) collective-permute-start(f32[2,2,4,16,128]{4,3,2,1,0:T(8,128)S(1)} %pad_maximum_fusion.1), channel_id=1, source_target_pairs={{0,128},{64,192},{128,0},{192,64},{256,384},{320,448},{384,256},{4... | collective-permute-start | bytes 393224 | tf_op jit(solution)/shard_map/ppermute | solution.py:515
  77.0 8.0 %collective-permute-start.10 = (f32[36,8,128]{2,1,0:T(8,128)S(1)}, f32[36,8,128]{2,1,0:T(8,128)S(1)}, u32[]{:S(2)}, u32[]{:S(2)}) collective-permute-start(f32[36,8,128]{2,1,0:T(8,128)S(1)} %get-tuple-element.41), channel_id=1, source_target_pairs={{4,8},{12,16},{20,24},{28,32},{36,40},{44,48},{52,56},{8,4},{16,12... | collective-permute-start | bytes 442376 | tf_op jit(solution)/shard_map/ppermute | solution.py:523
  80.1 5.9 %collective-permute-start.11 = (f32[36,8,128]{2,1,0:T(8,128)S(1)}, f32[36,8,128]{2,1,0:T(8,128)S(1)}, u32[]{:S(2)}, u32[]{:S(2)}) collective-permute-start(f32[36,8,128]{2,1,0:T(8,128)S(1)} %get-tuple-element.42), channel_id=1, source_target_pairs={{0,4},{8,12},{16,20},{24,28},{32,36},{40,44},{48,52},{56,60},{4,0}... | collective-permute-start | bytes 442376 | tf_op jit(solution)/shard_map/ppermute | solution.py:523
  86.1 8.5 %collective-permute-start.12 = (f32[4,2,4,40,128]{4,3,2,1,0:T(8,128)S(1)}, f32[4,2,4,40,128]{4,3,2,1,0:T(8,128)S(1)}, u32[]{:S(2)}, u32[]{:S(2)}) collective-permute-start(f32[4,2,4,40,128]{4,3,2,1,0:T(8,128)S(1)} %shard_map.52.near), channel_id=1, source_target_pairs={{0,64},{64,0},{128,192},{192,128},{256,320},{320,256},{384,448},{4... | collective-permute-start | bytes 1966088 | tf_op jit(solution)/shard_map/ppermute | solution.py:515
  99.4 5.7 %collective-permute-start.13 = (f32[20,8,128]{2,1,0:T(8,128)S(1)}, f32[20,8,128]{2,1,0:T(8,128)S(1)}, u32[]{:S(2)}, u32[]{:S(2)}) collective-permute-start(f32[20,8,128]{2,1,0:T(8,128)S(1)} %get-tuple-element.44), channel_id=1, source_target_pairs={{0,4},{4,8},{8,12},{12,16},{16,20},{20,24},{24,28},{28,32},{32,36}... | collective-permute-start | bytes 245768 | tf_op jit(solution)/shard_map/ppermute | solution.py:533
  105.2 5.9 %collective-permute-start.14 = (f32[20,8,128]{2,1,0:T(8,128)S(1)}, f32[20,8,128]{2,1,0:T(8,128)S(1)}, u32[]{:S(2)}, u32[]{:S(2)}) collective-permute-start(f32[20,8,128]{2,1,0:T(8,128)S(1)} %collective-permute-done.13.brought), channel_id=1, source_target_pairs={{0,64},{64,0},{128,192},{192,128},{256,320},{320,256},{384,448},{4... | collective-permute-start | bytes 245768 | tf_op jit(solution)/shard_map/ppermute | solution.py:515

commit v5 on v4

--- a/solution.py
+++ b/solution.py
@@ -270,7 +270,7 @@
     by_parity(px, xa, xb, fill_far)
     xin, xout = fa, fb
     for k, (a, c) in enumerate(factors(SMOOTH_DEG, *SMOOTH)):
-        sweep(xin, xout, upd, src, inv, k + 1, 23 - k, a, c, 2, False)
+        sweep(xin, xout, upd, src, inv, k + 1, 23 - k, a, c, 11 - k, False)
         xin, xout = xout, xin
     def residual(j, row, own_tile, total):
         if 8 <= row < 40:
@@ -371,7 +371,7 @@
     by_parity(place, far, near, fill)
     xin, xout = fa, fb
     for a, c in later:
-        sweep(xin, xout, upd, src, inv, 7, 39, a, c, 4, True)
+        sweep(xin, xout, upd, src, inv, 7, 39, a, c, 8, True)
         xin, xout = xout, xin
 
     def step(n, carry):
@@ -486,7 +486,7 @@
                     field[w, h, pl.ds(56, 8)] = zero
     xin, xout = za, zb
     for k, (a, c) in enumerate(factors(SMOOTH_DEG, *SMOOTH)):
-        sweep(xin, xout, zupd, src0, inv0, k + 1, 15 - k, a, c, 2, False, offset=4)
+        sweep(xin, xout, zupd, src0, inv0, k + 1, 15 - k, a, c, 7 - k, False, offset=4)
         xin, xout = xout, xin
     out[...] = xin[4:12, 0, 16:48]
 

time: 117 us -> 113 us (0.966)
  Pallas kernels: 20.2 us -> 16.3 us
    pallas_call x9, Pallas kernels: 20.2 us -> 16.3 us  [call(): pl.pallas_call(kernel, out_shape=[jax.ShapeDtypeStruct(s, F32) for s in o...]
where the time goes in v5:
time: 113 us
  starting transfers between devices  55.8 us (49%)
  waiting for transfers between devices  39.6 us (35%)
  Pallas kernels  16.3 us (14%)
    ppermute x5, starting transfers between devices, swap(): lax.ppermute(value, axis, [(i, i ^ bit) for i in range(lax.axis_size(axis...  21.4 us
    ppermute x6, starting transfers between devices, swap_both(): got.append(lax.ppermute(value, axis, ups + [(j, i) for i, j in ups]))  18.7 us
    pallas_call x9, Pallas kernels, call(): pl.pallas_call(kernel, out_shape=[jax.ShapeDtypeStruct(s, F32) for s in o...  16.3 us
    ppermute x6, waiting for transfers between devices, swap_both(): got.append(lax.ppermute(value, axis, ups + [(j, i) for i, j in ups]))  13.4 us
    ppermute x2, starting transfers between devices, shift(): return lax.ppermute(value, axis, pairs)  10.1 us
    ppermute x2, waiting for transfers between devices, cross(): return lax.ppermute(value, ('gx', axis), pairs)  9.31 us
    ppermute x2, waiting for transfers between devices, shift(): return lax.ppermute(value, axis, pairs)  9.02 us
    ppermute x5, waiting for transfers between devices, swap(): lax.ppermute(value, axis, [(i, i ^ bit) for i in range(lax.axis_size(axis...  7.89 us
  transfers between devices with their start and end apart: 15, of which 13 were waited for; matrix products, arithmetic and copies ran while one was open for 0% of the time, Pallas kernels for 0%

profile of v5, /device:TPU:9, one launch (start us, length us, event | category | flops | bytes accessed | tf_op | source)
XLA Modules:
  0.0 112.9 jit_solution(9915222503737288668)
XLA Ops:
  0.0 2.7 %shard_map.46 = (f32[3,8,32,128]{3,2,1,0:T(8,128)}, f32[2,32,128]{2,1,0:T(8,128)}, f32[2,32,128]{2,1,0:T(8,128)}) custom-call(f32[16]{0:T(128)} %table.1, f32[8,32,128]{2,1,0:T(8,128)} %pred_.1, f32[8,32,128]{2,1,0:T(8,128)} %right.1, s32[8,32,128]{2,1,0:T(8,128)} %zone.1), custom_call_target="tpu_custom_call" | custom-call | tf_op jit(solution)/shard_map/pallas_call | solution.py:498
  2.7 8.8 %collective-permute-start = (f32[2,32,128]{2,1,0:T(8,128)}, f32[2,32,128]{2,1,0:T(8,128)S(1)}, u32[]{:S(2)}, u32[]{:S(2)}) collective-permute-start(f32[2,32,128]{2,1,0:T(8,128)} %get-tuple-element.29), channel_id=1, source_target_pairs={{0,1},{1,2},{2,3},{4,5},{5,6},{6,7},{8,9},{9,10},{10,11},{12,13},{... | collective-permute-start | bytes 98312 | tf_op jit(solution)/shard_map/ppermute | solution.py:511
  12.8 9.0 %collective-permute-done.1.znext = f32[2,32,128]{2,1,0:T(8,128)S(1)} collective-permute-done((f32[2,32,128]{2,1,0:T(8,128)}, f32[2,32,128]{2,1,0:T(8,128)S(1)}, u32[]{:S(2)}, u32[]{:S(2)}) %collective-permute-start.1) | collective-permute-done | bytes 32800 | tf_op jit(solution)/shard_map/ppermute | solution.py:511
  22.9 4.3 %collective-permute-start.2 = (f32[28,8,128]{2,1,0:T(8,128)S(1)}, f32[28,8,128]{2,1,0:T(8,128)S(1)}, u32[]{:S(2)}, u32[]{:S(2)}) collective-permute-start(f32[28,8,128]{2,1,0:T(8,128)S(1)} %get-tuple-element.32), channel_id=1, source_target_pairs={{4,8},{12,16},{20,24},{28,32},{36,40},{44,48},{52,56},{8,4},{16,12... | collective-permute-start | bytes 344072 | tf_op jit(solution)/shard_map/ppermute | solution.py:523
  27.2 2.0 %collective-permute-start.3 = (f32[28,8,128]{2,1,0:T(8,128)S(1)}, f32[28,8,128]{2,1,0:T(8,128)S(1)}, u32[]{:S(2)}, u32[]{:S(2)}) collective-permute-start(f32[28,8,128]{2,1,0:T(8,128)S(1)} %get-tuple-element.33), channel_id=1, source_target_pairs={{0,4},{8,12},{16,20},{24,28},{32,36},{40,44},{48,52},{56,60},{4,0}... | collective-permute-start | bytes 344072 | tf_op jit(solution)/shard_map/ppermute | solution.py:523
  30.5 2.5 %collective-permute-done.3.yb = f32[28,8,128]{2,1,0:T(8,128)S(1)} collective-permute-done((f32[28,8,128]{2,1,0:T(8,128)S(1)}, f32[28,8,128]{2,1,0:T(8,128)S(1)}, u32[]{:S(2)}, u32[]{:S(2)}) %collective-permute-start.3) | collective-permute-done | bytes 114720 | tf_op jit(solution)/shard_map/ppermute | solution.py:523
  33.1 5.5 %collective-permute-start.4 = (f32[142,8,128]{2,1,0:T(8,128)S(1)}, f32[142,8,128]{2,1,0:T(8,128)S(1)}, u32[]{:S(2)}, u32[]{:S(2)}) collective-permute-start(f32[142,8,128]{2,1,0:T(8,128)S(1)} %get-tuple-element.36), channel_id=1, source_target_pairs={{64,128},{192,256},{320,384},{128,64},{256,192},{384,320},{65,129}... | collective-permute-start | bytes 1744904 | tf_op jit(solution)/shard_map/ppermute | solution.py:523
  38.6 1.9 %collective-permute-start.5 = (f32[142,8,128]{2,1,0:T(8,128)S(1)}, f32[142,8,128]{2,1,0:T(8,128)S(1)}, u32[]{:S(2)}, u32[]{:S(2)}) collective-permute-start(f32[142,8,128]{2,1,0:T(8,128)S(1)} %get-tuple-element.37), channel_id=1, source_target_pairs={{0,64},{128,192},{256,320},{384,448},{64,0},{192,128},{320,256},{4... | collective-permute-start | bytes 1744904 | tf_op jit(solution)/shard_map/ppermute | solution.py:523
  40.5 5.5 %collective-permute-done.4.xa = f32[142,8,128]{2,1,0:T(8,128)S(1)} collective-permute-done((f32[142,8,128]{2,1,0:T(8,128)S(1)}, f32[142,8,128]{2,1,0:T(8,128)S(1)}, u32[]{:S(2)}, u32[]{:S(2)}) %collective-permute-start.4) | collective-permute-done | bytes 581664 | tf_op jit(solution)/shard_map/ppermute | solution.py:523
  46.1 4.4 %shard_map.49 = (f32[24,2,64,128]{3,2,1,0:T(8,128)S(1)}, f32[24,2,48,128]{3,2,1,0:T(8,128)S(1)}, f32[24,2,48,128]{3,2,1,0:T(8,128)S(1)}, f32[2,4,16,128]{3,2,1,0...) custom-call(s32[1]{0:T(128)} %bitcast.px.place, f32[3,8,32,128]{3,2,1,0:T(8,128)S(1)} %get-tuple-element.31.main, ...), custom_call_target="tpu_custom_call" | custom-call | tf_op jit(solution)/shard_map/pallas_call | solution.py:498
  50.5 1.9 %collective-permute-start.6 = (f32[2,16,128]{2,1,0:T(8,128)S(1)}, f32[2,16,128]{2,1,0:T(8,128)S(1)}, u32[]{:S(2)}, u32[]{:S(2)}) collective-permute-start(f32[2,16,128]{2,1,0:T(8,128)S(1)} %get-tuple-element.40), channel_id=1, source_target_pairs={{0,64},{64,0},{128,192},{192,128},{256,320},{320,256},{384,448},{4... | collective-permute-start | bytes 49160 | tf_op jit(solution)/shard_map/ppermute | solution.py:515
  54.9 7.8 %collective-permute-done.7.halo = f32[2,2,16,128]{3,2,1,0:T(8,128)S(1)} collective-permute-done((f32[2,2,16,128]{3,2,1,0:T(8,128)S(1)}, f32[2,2,16,128]{3,2,1,0:T(8,128)S(1)}, u32[]{:S(2)}, u32[]{:S(2)}) %collective-permute-start.7) | collective-permute-done | bytes 32800 | tf_op jit(solution)/shard_map/ppermute | solution.py:533
  62.8 4.1 %collective-permute-start.8 = (f32[1,2,4,16,128]{4,3,2,1,0:T(8,128)S(1)}, f32[1,2,4,16,128]{4,3,2,1,0:T(8,128)S(1)}, u32[]{:S(2)}, u32[]{:S(2)}) collective-permute-start(f32[1,2,4,16,128]{4,3,2,1,0:T(8,128)S(1)} %shard_map.50), channel_id=1, source_target_pairs={{0,256},{64,320},{128,384},{192,448},{256,0},{320,64},{384,128},{4... | collective-permute-start | bytes 196616 | tf_op jit(solution)/shard_map/ppermute | solution.py:515
  66.9 1.8 %collective-permute-done.8 = f32[1,2,4,16,128]{4,3,2,1,0:T(8,128)S(1)} collective-permute-done((f32[1,2,4,16,128]{4,3,2,1,0:T(8,128)S(1)}, f32[1,2,4,16,128]{4,3,2,1,0:T(8,128)S(1)}, u32[]{:S(2)}, u32[]{:S(2)}) %collective-permute-start.8) | collective-permute-done | bytes 65568 | tf_op jit(solution)/shard_map/ppermute | solution.py:515
  68.7 3.7 %collective-permute-start.9 = (f32[2,2,4,16,128]{4,3,2,1,0:T(8,128)S(1)}, f32[2,2,4,16,128]{4,3,2,1,0:T(8,128)S(1)}, u32[]{:S(2)}, u32[]{:S(2)}) collective-permute-start(f32[2,2,4,16,128]{4,3,2,1,0:T(8,128)S(1)} %pad_maximum_fusion.1), channel_id=1, source_target_pairs={{0,128},{64,192},{128,0},{192,64},{256,384},{320,448},{384,256},{4... | collective-permute-start | bytes 393224 | tf_op jit(solution)/shard_map/ppermute | solution.py:515
  72.4 2.3 %collective-permute-done.9 = f32[2,2,4,16,128]{4,3,2,1,0:T(8,128)S(1)} collective-permute-done((f32[2,2,4,16,128]{4,3,2,1,0:T(8,128)S(1)}, f32[2,2,4,16,128]{4,3,2,1,0:T(8,128)S(1)}, u32[]{:S(2)}, u32[]{:S(2)}) %collective-permute-start.9) | collective-permute-done | bytes 131104 | tf_op jit(solution)/shard_map/ppermute | solution.py:515
  74.9 3.1 %collective-permute-start.10 = (f32[36,8,128]{2,1,0:T(8,128)S(1)}, f32[36,8,128]{2,1,0:T(8,128)S(1)}, u32[]{:S(2)}, u32[]{:S(2)}) collective-permute-start(f32[36,8,128]{2,1,0:T(8,128)S(1)} %get-tuple-element.41), channel_id=1, source_target_pairs={{4,8},{12,16},{20,24},{28,32},{36,40},{44,48},{52,56},{8,4},{16,12... | collective-permute-start | bytes 442376 | tf_op jit(solution)/shard_map/ppermute | solution.py:523
  78.0 1.9 %collective-permute-start.11 = (f32[36,8,128]{2,1,0:T(8,128)S(1)}, f32[36,8,128]{2,1,0:T(8,128)S(1)}, u32[]{:S(2)}, u32[]{:S(2)}) collective-permute-start(f32[36,8,128]{2,1,0:T(8,128)S(1)} %get-tuple-element.42), channel_id=1, source_target_pairs={{0,4},{8,12},{16,20},{24,28},{32,36},{40,44},{48,52},{56,60},{4,0}... | collective-permute-start | bytes 442376 | tf_op jit(solution)/shard_map/ppermute | solution.py:523
  79.9 2.9 %collective-permute-done.10.ya = f32[36,8,128]{2,1,0:T(8,128)S(1)} collective-permute-done((f32[36,8,128]{2,1,0:T(8,128)S(1)}, f32[36,8,128]{2,1,0:T(8,128)S(1)}, u32[]{:S(2)}, u32[]{:S(2)}) %collective-permute-start.10) | collective-permute-done | bytes 147488 | tf_op jit(solution)/shard_map/ppermute | solution.py:523
  83.9 6.8 %collective-permute-start.12 = (f32[4,2,4,40,128]{4,3,2,1,0:T(8,128)S(1)}, f32[4,2,4,40,128]{4,3,2,1,0:T(8,128)S(1)}, u32[]{:S(2)}, u32[]{:S(2)}) collective-permute-start(f32[4,2,4,40,128]{4,3,2,1,0:T(8,128)S(1)} %shard_map.52.near), channel_id=1, source_target_pairs={{0,64},{64,0},{128,192},{192,128},{256,320},{320,256},{384,448},{4... | collective-permute-start | bytes 1966088 | tf_op jit(solution)/shard_map/ppermute | solution.py:515
  92.4 4.0 %shard_map.53 = (f32[47,1,56,128]{3,2,1,0:T(8,128)S(1)}, f32[47,1,40,128]{3,2,1,0:T(8,128)S(1)}, f32[47,1,40,128]{3,2,1,0:T(8,128)S(1)}, f32[16,8,128]{2,1,0:T(8,128)S(1)}, f32[20,8,128]{2,1,0:T(8,128)S(1)}) custom-call(s32[1]{0:T(128)} %bitcast.px.place, f32[4,2,4,40,128]{4,3,2,1,0:T(8,128)S(1)} %shard_map.52.near, ...), custom_call_target="tpu_custom_call" | custom-call | tf_op jit(solution)/shard_map/pallas_call | solution.py:498
  96.4 4.3 %collective-permute-start.13 = (f32[20,8,128]{2,1,0:T(8,128)S(1)}, f32[20,8,128]{2,1,0:T(8,128)S(1)}, u32[]{:S(2)}, u32[]{:S(2)}) collective-permute-start(f32[20,8,128]{2,1,0:T(8,128)S(1)} %get-tuple-element.44), channel_id=1, source_target_pairs={{0,4},{4,8},{8,12},{12,16},{16,20},{20,24},{24,28},{28,32},{32,36}... | collective-permute-start | bytes 245768 | tf_op jit(solution)/shard_map/ppermute | solution.py:533
  102.2 5.0 %collective-permute-start.14 = (f32[20,8,128]{2,1,0:T(8,128)S(1)}, f32[20,8,128]{2,1,0:T(8,128)S(1)}, u32[]{:S(2)}, u32[]{:S(2)}) collective-permute-start(f32[20,8,128]{2,1,0:T(8,128)S(1)} %collective-permute-done.13.brought), channel_id=1, source_target_pairs={{0,64},{64,0},{128,192},{192,128},{256,320},{320,256},{384,448},{4... | collective-permute-start | bytes 245768 | tf_op jit(solution)/shard_map/ppermute | solution.py:515
  108.0 4.9 %shard_map.54 = f32[8,32,128]{2,1,0:T(8,128)} custom-call(s32[1]{0:T(128)} %bitcast.px.place, f32[16,8,128]{2,1,0:T(8,128)S(1)} %get-tuple-element.43.two, f32[20,8,128]{2,1,0:T(8,128)S(1)} %collective-permute-done.13.brought, f32[20,8,128]{2,1,0:T(8,128)S(1)} %collective-permute-done.14.given, f32[47,1,56,128]{3,2,1,0:T(8,128)S(1)} %get-tuple-element.45.x1, ...), custom_call_target="tpu_custom_call" | custom-call | tf_op jit(solution)/shard_map/pallas_call | solution.py:498
  (20 shorter events, 11.6 us)
Async XLA Ops:
  2.7 10.1 %collective-permute-start = (f32[2,32,128]{2,1,0:T(8,128)}, f32[2,32,128]{2,1,0:T(8,128)S(1)}, u32[]{:S(2)}, u32[]{:S(2)}) collective-permute-start(f32[2,32,128]{2,1,0:T(8,128)} %get-tuple-element.29), channel_id=1, source_target_pairs={{0,1},{1,2},{2,3},{4,5},{5,6},{6,7},{8,9},{9,10},{10,11},{12,13},{... | collective-permute-start | bytes 98312 | tf_op jit(solution)/shard_map/ppermute | solution.py:511
  11.5 10.3 %collective-permute-start.1 = (f32[2,32,128]{2,1,0:T(8,128)}, f32[2,32,128]{2,1,0:T(8,128)S(1)}, u32[]{:S(2)}, u32[]{:S(2)}) collective-permute-start(f32[2,32,128]{2,1,0:T(8,128)} %get-tuple-element.30), channel_id=1, source_target_pairs={{1,0},{2,1},{3,2},{5,4},{6,5},{7,6},{9,8},{10,9},{11,10},{13,12},{... | collective-permute-start | bytes 98312 | tf_op jit(solution)/shard_map/ppermute | solution.py:511
  21.8 1.0 copy-start
  22.9 7.6 %collective-permute-start.2 = (f32[28,8,128]{2,1,0:T(8,128)S(1)}, f32[28,8,128]{2,1,0:T(8,128)S(1)}, u32[]{:S(2)}, u32[]{:S(2)}) collective-permute-start(f32[28,8,128]{2,1,0:T(8,128)S(1)} %get-tuple-element.32), channel_id=1, source_target_pairs={{4,8},{12,16},{20,24},{28,32},{36,40},{44,48},{52,56},{8,4},{16,12... | collective-permute-start | bytes 344072 | tf_op jit(solution)/shard_map/ppermute | solution.py:523
  27.2 5.8 %collective-permute-start.3 = (f32[28,8,128]{2,1,0:T(8,128)S(1)}, f32[28,8,128]{2,1,0:T(8,128)S(1)}, u32[]{:S(2)}, u32[]{:S(2)}) collective-permute-start(f32[28,8,128]{2,1,0:T(8,128)S(1)} %get-tuple-element.33), channel_id=1, source_target_pairs={{0,4},{8,12},{16,20},{24,28},{32,36},{40,44},{48,52},{56,60},{4,0}... | collective-permute-start | bytes 344072 | tf_op jit(solution)/shard_map/ppermute | solution.py:523
  33.1 13.0 %collective-permute-start.4 = (f32[142,8,128]{2,1,0:T(8,128)S(1)}, f32[142,8,128]{2,1,0:T(8,128)S(1)}, u32[]{:S(2)}, u32[]{:S(2)}) collective-permute-start(f32[142,8,128]{2,1,0:T(8,128)S(1)} %get-tuple-element.36), channel_id=1, source_target_pairs={{64,128},{192,256},{320,384},{128,64},{256,192},{384,320},{65,129}... | collective-permute-start | bytes 1744904 | tf_op jit(solution)/shard_map/ppermute | solution.py:523
  38.6 7.5 %collective-permute-start.5 = (f32[142,8,128]{2,1,0:T(8,128)S(1)}, f32[142,8,128]{2,1,0:T(8,128)S(1)}, u32[]{:S(2)}, u32[]{:S(2)}) collective-permute-start(f32[142,8,128]{2,1,0:T(8,128)S(1)} %get-tuple-element.37), channel_id=1, source_target_pairs={{0,64},{128,192},{256,320},{384,448},{64,0},{192,128},{320,256},{4... | collective-permute-start | bytes 1744904 | tf_op jit(solution)/shard_map/ppermute | solution.py:523
  50.5 3.1 %collective-permute-start.6 = (f32[2,16,128]{2,1,0:T(8,128)S(1)}, f32[2,16,128]{2,1,0:T(8,128)S(1)}, u32[]{:S(2)}, u32[]{:S(2)}) collective-permute-start(f32[2,16,128]{2,1,0:T(8,128)S(1)} %get-tuple-element.40), channel_id=1, source_target_pairs={{0,64},{64,0},{128,192},{192,128},{256,320},{320,256},{384,448},{4... | collective-permute-start | bytes 49160 | tf_op jit(solution)/shard_map/ppermute | solution.py:515
  53.6 9.1 %collective-permute-start.7 = (f32[2,2,16,128]{3,2,1,0:T(8,128)S(1)}, f32[2,2,16,128]{3,2,1,0:T(8,128)S(1)}, u32[]{:S(2)}, u32[]{:S(2)}) collective-permute-start(f32[2,2,16,128]{3,2,1,0:T(8,128)S(1)} %pad_maximum_fusion.2), channel_id=1, source_target_pairs={{0,1},{1,2},{2,3},{65,64},{66,65},{67,66},{128,129},{129,130},{130... | collective-permute-start | bytes 98312 | tf_op jit(solution)/shard_map/ppermute | solution.py:533
  62.8 5.9 %collective-permute-start.8 = (f32[1,2,4,16,128]{4,3,2,1,0:T(8,128)S(1)}, f32[1,2,4,16,128]{4,3,2,1,0:T(8,128)S(1)}, u32[]{:S(2)}, u32[]{:S(2)}) collective-permute-start(f32[1,2,4,16,128]{4,3,2,1,0:T(8,128)S(1)} %shard_map.50), channel_id=1, source_target_pairs={{0,256},{64,320},{128,384},{192,448},{256,0},{320,64},{384,128},{4... | collective-permute-start | bytes 196616 | tf_op jit(solution)/shard_map/ppermute | solution.py:515
  68.7 6.1 %collective-permute-start.9 = (f32[2,2,4,16,128]{4,3,2,1,0:T(8,128)S(1)}, f32[2,2,4,16,128]{4,3,2,1,0:T(8,128)S(1)}, u32[]{:S(2)}, u32[]{:S(2)}) collective-permute-start(f32[2,2,4,16,128]{4,3,2,1,0:T(8,128)S(1)} %pad_maximum_fusion.1), channel_id=1, source_target_pairs={{0,128},{64,192},{128,0},{192,64},{256,384},{320,448},{384,256},{4... | collective-permute-start | bytes 393224 | tf_op jit(solution)/shard_map/ppermute | solution.py:515
  74.9 8.0 %collective-permute-start.10 = (f32[36,8,128]{2,1,0:T(8,128)S(1)}, f32[36,8,128]{2,1,0:T(8,128)S(1)}, u32[]{:S(2)}, u32[]{:S(2)}) collective-permute-start(f32[36,8,128]{2,1,0:T(8,128)S(1)} %get-tuple-element.41), channel_id=1, source_target_pairs={{4,8},{12,16},{20,24},{28,32},{36,40},{44,48},{52,56},{8,4},{16,12... | collective-permute-start | bytes 442376 | tf_op jit(solution)/shard_map/ppermute | solution.py:523
  78.0 5.9 %collective-permute-start.11 = (f32[36,8,128]{2,1,0:T(8,128)S(1)}, f32[36,8,128]{2,1,0:T(8,128)S(1)}, u32[]{:S(2)}, u32[]{:S(2)}) collective-permute-start(f32[36,8,128]{2,1,0:T(8,128)S(1)} %get-tuple-element.42), channel_id=1, source_target_pairs={{0,4},{8,12},{16,20},{24,28},{32,36},{40,44},{48,52},{56,60},{4,0}... | collective-permute-start | bytes 442376 | tf_op jit(solution)/shard_map/ppermute | solution.py:523
  83.9 8.5 %collective-permute-start.12 = (f32[4,2,4,40,128]{4,3,2,1,0:T(8,128)S(1)}, f32[4,2,4,40,128]{4,3,2,1,0:T(8,128)S(1)}, u32[]{:S(2)}, u32[]{:S(2)}) collective-permute-start(f32[4,2,4,40,128]{4,3,2,1,0:T(8,128)S(1)} %shard_map.52.near), channel_id=1, source_target_pairs={{0,64},{64,0},{128,192},{192,128},{256,320},{320,256},{384,448},{4... | collective-permute-start | bytes 1966088 | tf_op jit(solution)/shard_map/ppermute | solution.py:515
  96.4 5.7 %collective-permute-start.13 = (f32[20,8,128]{2,1,0:T(8,128)S(1)}, f32[20,8,128]{2,1,0:T(8,128)S(1)}, u32[]{:S(2)}, u32[]{:S(2)}) collective-permute-start(f32[20,8,128]{2,1,0:T(8,128)S(1)} %get-tuple-element.44), channel_id=1, source_target_pairs={{0,4},{4,8},{8,12},{12,16},{16,20},{20,24},{24,28},{28,32},{32,36}... | collective-permute-start | bytes 245768 | tf_op jit(solution)/shard_map/ppermute | solution.py:533
  102.2 5.9 %collective-permute-start.14 = (f32[20,8,128]{2,1,0:T(8,128)S(1)}, f32[20,8,128]{2,1,0:T(8,128)S(1)}, u32[]{:S(2)}, u32[]{:S(2)}) collective-permute-start(f32[20,8,128]{2,1,0:T(8,128)S(1)} %collective-permute-done.13.brought), channel_id=1, source_target_pairs={{0,64},{64,0},{128,192},{192,128},{256,320},{320,256},{384,448},{4... | collective-permute-start | bytes 245768 | tf_op jit(solution)/shard_map/ppermute | solution.py:515
